TPU v7x, 32 devices: a whole 2x2x4 slice. The times are simulated.
32 devices in a mesh: groups: 2 (over y), dp: 4 (over x, core), tensor: 4 (over z).
Axes of the slice: x: 2, y: 2, z: 4, core: 2. Of those that a mesh axis runs over, the one named last changes fastest.
Arguments:
- tokens: bfloat16 [1024, 8192], P(('groups', 'dp'), 'tensor'), parts along dimension 0, may hold values from -6 to 6
- gate_weight: bfloat16 [8192, 16384], P('dp', 'tensor'), may hold values from -0.0625 to 0.0625
- up_weight: bfloat16 [8192, 16384], P('dp', 'tensor'), may hold values from -0.0625 to 0.0625
- down_weight: bfloat16 [16384, 8192], P('tensor', 'dp'), may hold values from -0.0625 to 0.0625
- block_ids: int32 [256], P(('groups', 'tensor')), parts along dimension 0, may hold values from 0 to 127, as said below
- block_counts: int32 [8], P(('groups', 'tensor')), parts along dimension 0, may hold values from 1 to 32
Outputs:
- mixed: bfloat16 [1024, 8192], P(('groups', 'dp'), 'tensor'), parts along dimension 0
There are 2 independent parts, one for each index of `groups`. A program takes and returns all parts, laid end to end along the dimension named above; an argument that names none is the same for every part. Nothing has to cross between parts.
Inputs may be any that keep to these rules, and one draw needn't show every extreme that they name: `block_ids`: each shard's 32 entries name that shard's own blocks, each once; entries past the shard's count are padding.
All inputs are finite; a program needn't handle non-finite values.
Results may differ from a plain program's by a relative error of at most 0.005.
Values may be sent and summed in bfloat16 or wider, within the bound.
No kernel may reach another device: no remote copies, remote signals or barrier semaphores. Data moves between devices by JAX's collectives and lax.ppermute only.
A program may use at most 512 MiB of HBM per device.

v0:
```python
import jax
import jax.numpy as jnp
from jax import lax
from jax.sharding import PartitionSpec as P


def per_device(tokens, gate_weight, up_weight, down_weight, block_ids, block_counts):
    gathered = lax.all_gather(tokens, "tensor", axis=1, tiled=True)
    row_count = gathered.shape[0]
    unit_count = gate_weight.shape[1]
    gate_sum = jnp.dot(
        gathered,
        lax.all_gather(gate_weight, "dp", axis=0, tiled=True),
        preferred_element_type=jnp.float32,
    )
    up_sum = jnp.dot(
        gathered,
        lax.all_gather(up_weight, "dp", axis=0, tiled=True),
        preferred_element_type=jnp.float32,
    )
    block_total = block_ids.shape[0]
    local_ids = block_ids % block_total
    places = jnp.arange(block_total, dtype=jnp.int32)
    in_count = places < block_counts[0]
    match = (local_ids[:, None] == places[None, :]) & in_count[:, None]
    active = jnp.any(match, axis=0).astype(jnp.float32)
    product = jnp.maximum(gate_sum, 0.0) * up_sum
    product = (
        product.reshape(row_count, block_total, unit_count // block_total) * active[None, :, None]
    )
    hidden = product.reshape(row_count, unit_count).astype(jnp.bfloat16)
    partials = jnp.dot(
        hidden,
        lax.all_gather(down_weight, "dp", axis=1, tiled=True),
        preferred_element_type=jnp.float32,
    )
    return lax.psum_scatter(partials, "tensor", scatter_dimension=1, tiled=True).astype(
        jnp.bfloat16
    )


def solution(mesh):
    placed = (
        P(("groups", "dp"), "tensor"),
        P("dp", "tensor"),
        P("dp", "tensor"),
        P("tensor", "dp"),
        P(("groups", "tensor")),
        P(("groups", "tensor")),
    )
    return jax.shard_map(
        per_device,
        mesh=mesh,
        in_specs=placed,
        out_specs=P(("groups", "dp"), "tensor"),
        check_vma=False,
    )
```

profile of v0, /device:TPU:2, one launch (start us, length us, event | category | flops | bytes accessed | tf_op | source)
XLA Modules:
  0.0 1348.0 jit_solution(9751537675347615707)
XLA Ops:
  6.5 0.0 all-gather.5.cloned.1.call-start
  6.5 0.7 all-gather.5.cloned.1.call-update
  7.3 0.0 all-gather.7.cloned.1.call-start
  7.3 0.7 all-gather.7.cloned.1.call-update
  8.0 0.0 all-gather.9.cloned.1.call-start
  8.1 0.7 all-gather.9.cloned.1.call-update
  8.7 0.0 copy-start.1
  8.8 0.0 all-gather.11.cloned.1.call-start
  8.8 0.5 all-gather.11.cloned.1.call-update
  9.3 0.0 reduce-scatter.2.cloned.1.call-start
  10.0 0.0 copy-done.1
  10.1 0.1 fusion.5
  10.2 0.1 broadcast_bitcast_fusion
  10.2 45.9 %all-gather.5.cloned.1.call-done = bf16[128,8192]{1,0:T(8,128)(2,1)} async-done(((bf16[128,2048]{1,0:T(8,128)(2,1)}), bf16[128,8192]{1,0:T(8,128)(2,1)}) %all-gather.5.cloned.1.call-update) | async-done | bytes 2097168 | tf_op jit(solution)/shard_map/all_gather | solution.py:8
  56.1 0.0 copy-start
  56.1 391.9 %all-gather.7.cloned.1.call-done = bf16[8192,4096]{1,0:T(8,128)(2,1)} async-done(((bf16[2048,4096]{1,0:T(8,128)(2,1)}), bf16[8192,4096]{1,0:T(8,128)(2,1)}) %all-gather.7.cloned.1.call-update) | async-done | bytes 67108880 | tf_op jit(solution)/shard_map/all_gather | solution.py:13
  448.0 37.8 %convolution_maximum_fusion = f32[128,4096]{1,0:T(8,128)} fusion(bf16[128,8192]{1,0:T(8,128)(2,1)} %all-gather.5.cloned.1.call-done, bf16[8192,4096]{1,0:T(8,128)(2,1)} %all-gather.7.cloned.1.call-done), kind=kOutput, calls=%fused_computation.2 | convolution fusion | flops 8590458880 | bytes 71303168 | tf_op jit(solution)/shard_map/dot_general | solution.py:11
  485.8 356.6 %all-gather.9.cloned.1.call-done = bf16[8192,4096]{1,0:T(8,128)(2,1)} async-done(((bf16[2048,4096]{1,0:T(8,128)(2,1)}), bf16[8192,4096]{1,0:T(8,128)(2,1)}) %all-gather.9.cloned.1.call-update) | async-done | bytes 67108880 | tf_op jit(solution)/shard_map/all_gather | solution.py:18
  842.4 0.0 copy-done
  842.4 35.5 %fusion.1.clone.4 = bf16[128,4096]{1,0:T(8,128)(2,1)S(1)} fusion(f32[128,4096]{1,0:T(8,128)} %convolution_maximum_fusion, bf16[128,8192]{1,0:T(8,128)(2,1)S(1)} %copy-done, bf16[8192,4096]{1,0:T(8,128)(2,1)} %all-gather.9.cloned.1.call-done, f32[4096]{0:T(1024)S(1)} %broadcast_bitcast_fusion), kind=kOutput, calls=%fused_computation.3.clone.clone.clone.1 | convolution fusion | flops 8591507456 | bytes 72368128 | tf_op jit(solution)/shard_map/dot_general | solution.py:16
  877.9 358.7 %all-gather.11.cloned.1.call-done = bf16[4096,8192]{1,0:T(8,128)(2,1)} async-done(((bf16[4096,2048]{1,0:T(8,128)(2,1)}), bf16[4096,8192]{1,0:T(8,128)(2,1)}) %all-gather.11.cloned.1.call-update) | async-done | bytes 67108880 | tf_op jit(solution)/shard_map/all_gather | solution.py:34
  1236.6 24.8 %fusion.2 = f32[128,8192]{1,0:T(8,128)} fusion(bf16[4096,8192]{1,0:T(8,128)(2,1)} %all-gather.11.cloned.1.call-done, bf16[128,4096]{1,0:T(8,128)(2,1)S(1)} %fusion.1.clone.4), kind=kOutput, calls=%fused_computation.4 | convolution fusion | flops 8589934592 | bytes 72351744 | tf_op jit(solution)/shard_map/dot_general | solution.py:32
  1261.3 0.0 reduce-scatter.2.cloned.1.call-update
  1261.4 78.1 %reduce-scatter.2.cloned.1.call-done = f32[128,2048]{1,0:T(8,128)} async-done(((f32[128,8192]{1,0:T(8,128)}), f32[128,2048]{1,0:T(8,128)}) %reduce-scatter.2.cloned.1.call-update) | async-done | bytes 1048592 | tf_op jit(solution)/shard_map/reduce_scatter | solution.py:37
  1339.4 2.1 convert_element_type.15
  (3 shorter events, 0.0 us)
Async XLA Ops:
  6.5 49.6 %all-gather.5.cloned.1.call-start = ((), (), s32[]{:S(2)}) async-start(), calls=%async_computation.1 | async-start | bytes 2621440 | tf_op jit(solution)/shard_map/all_gather | solution.py:8
  7.3 440.8 %all-gather.7.cloned.1.call-start = ((), (), s32[]{:S(2)}) async-start(), calls=%async_computation.2 | async-start | bytes 83886080 | tf_op jit(solution)/shard_map/all_gather | solution.py:13
  8.0 834.4 %all-gather.9.cloned.1.call-start = ((), (), s32[]{:S(2)}) async-start(), calls=%async_computation.3 | async-start | bytes 83886080 | tf_op jit(solution)/shard_map/all_gather | solution.py:18
  8.7 1.3 copy-start.1
  8.8 1227.8 %all-gather.11.cloned.1.call-start = ((), (), s32[]{:S(2)}) async-start(), calls=%async_computation.4 | async-start | bytes 83886080 | tf_op jit(solution)/shard_map/all_gather | solution.py:34
  9.3 1330.1 %reduce-scatter.2.cloned.1.call-start = ((), (), s32[]{:S(2)}) async-start(), calls=%async_computation.5 | async-start | bytes 5242880 | tf_op jit(solution)/shard_map/reduce_scatter | solution.py:37
  56.1 786.2 %copy-start = (bf16[128,8192]{1,0:T(8,128)(2,1)S(1)}, bf16[128,8192]{1,0:T(8,128)(2,1)}, u32[]{:S(2)}) copy-start(bf16[128,8192]{1,0:T(8,128)(2,1)} %all-gather.5.cloned.1.call-done) | copy-start | bytes 6291460
Sparse Core Ops, SparseCore 0:
  8.9 47.1 all-gather.4
  57.7 390.2 all-gather.6
  449.6 392.7 all-gather.8
  843.8 392.7 all-gather.10
  1261.5 77.9 reduce-scatter.1
where the time goes:
time: 1350 us
  waiting for transfers between devices  1230 us (91%)
  matrix products  98 us (7%)
  between operations  13.8 us (1%)
    all_gather x1, waiting for transfers between devices, per_device(): lax.all_gather(gate_weight, 'dp', axis=0, tiled=True)  392 us
    all_gather x1, waiting for transfers between devices, per_device(): lax.all_gather(down_weight, 'dp', axis=1, tiled=True)  359 us
    all_gather x1, waiting for transfers between devices, per_device(): lax.all_gather(up_weight, 'dp', axis=0, tiled=True)  357 us
    reduce_scatter x1, waiting for transfers between devices, per_device(): lax.psum_scatter(partials, 'tensor', scatter_dimension=1, tiled=True)  78.1 us
    all_gather x1, waiting for transfers between devices, per_device(): gathered = lax.all_gather(tokens, 'tensor', axis=1, tiled=True)  45.9 us
    dot_general x1, matrix products, per_device(): jnp.dot(gathered, lax.all_gather(gate_weight, 'dp', axis=0, tiled=True),...  37.8 us
    dot_general x1, matrix products, per_device(): jnp.dot(gathered, lax.all_gather(up_weight, 'dp', axis=0, tiled=True), pr...  35.5 us
  transfers between devices with their start and end apart: 5, of which 5 were waited for; matrix products, arithmetic and copies ran while one was open for 5% of the time, Pallas kernels for 0%

commit v1 on v0

v1 whole, which is shorter than its diff:
```python
import functools

import jax
import jax.numpy as jnp
from jax import lax
from jax.experimental import pallas as pl
from jax.experimental.pallas import tpu as pltpu
from jax.sharding import PartitionSpec as P

CHUNKS = 2
BF16, F32 = jnp.bfloat16, jnp.float32


def xor_perm(size, mask):
    return [(i, i ^ mask) for i in range(size)]


def active_units(block_ids, block_counts, unit_count):
    block_total = block_ids.shape[0]
    places = jnp.arange(block_total, dtype=jnp.int32)
    match = (block_ids[:, None] % block_total == places[None, :]) & (
        places < block_counts[0]
    )[:, None]
    active = jnp.any(match, axis=0).astype(F32)
    return jnp.repeat(active, unit_count // block_total)


def gate_up_kernel(td_ref, x0, x1, x2, x3, gate_ref, up_ref, keep_ref, send_ref, xs):
    rows = x0.shape[0]

    @pl.when(pl.program_id(0) == 0)
    def _():
        for j, x in enumerate((x0, x1, x2, x3)):
            place = pl.multiple_of((j ^ td_ref[0]) * rows, rows)
            xs[pl.ds(place, rows), :] = x[...]

    for i, w in enumerate((gate_ref, up_ref)):
        acc = jnp.dot(xs[...], w[...], preferred_element_type=F32)
        keep_ref[0, i] = acc[:rows]
        send_ref[0, i] = acc[rows : 2 * rows].astype(BF16)
        keep_ref[1, i] = acc[2 * rows : 3 * rows]
        send_ref[1, i] = acc[3 * rows :].astype(BF16)


def gate_up(td, blocks, gate_weight, up_weight, tile=512):
    rows, depth = blocks[0].shape
    units = gate_weight.shape[1]
    whole = pl.BlockSpec((rows, depth), lambda i, td: (0, 0))
    part = pl.BlockSpec((depth, tile), lambda i, td: (0, i))
    out = pl.BlockSpec((2, 2, rows, tile), lambda i, td: (0, 0, 0, i))
    return pl.pallas_call(
        gate_up_kernel,
        grid_spec=pltpu.PrefetchScalarGridSpec(
            num_scalar_prefetch=1,
            grid=(units // tile,),
            in_specs=[whole] * 4 + [part] * 2,
            out_specs=[out, out],
            scratch_shapes=[pltpu.VMEM((4 * rows, depth), BF16)],
        ),
        out_shape=[
            jax.ShapeDtypeStruct((2, 2, rows, units), F32),
            jax.ShapeDtypeStruct((2, 2, rows, units), BF16),
        ],
        compiler_params=pltpu.CompilerParams(vmem_limit_bytes=40 << 20),
        cost_estimate=pl.CostEstimate(
            flops=16 * rows * depth * units,
            bytes_accessed=4 * depth * units + 8 * rows * depth + 24 * rows * units,
            transcendentals=0,
        ),
        name="gate_up",
    )(td, *blocks, gate_weight, up_weight)


def down_kernel(td_ref, h0, h2, h13, down_ref, o0, o1, o2, o3, hs):
    rows = h0.shape[0]

    @pl.when(pl.program_id(0) == 0)
    def _():
        for k in range(4):
            place = pl.multiple_of((k ^ td_ref[0]) * rows, rows)
            h = h0[...] if k == 0 else h2[...] if k == 2 else h13[k // 2]
            hs[pl.ds(place, rows), :] = h

    acc = jnp.dot(hs[...], down_ref[...], preferred_element_type=F32)
    for j, o in enumerate((o0, o1, o2, o3)):
        o[...] = acc[j * rows : (j + 1) * rows].astype(o.dtype)


def down(td, h0, h2, h13, down_weight, tile=256):
    rows, depth = h0.shape
    width = down_weight.shape[1]
    whole = pl.BlockSpec((rows, depth), lambda i, td: (0, 0))
    pair = pl.BlockSpec((2, rows, depth), lambda i, td: (0, 0, 0))
    part = pl.BlockSpec((depth, tile), lambda i, td: (0, i))
    out = pl.BlockSpec((rows, tile), lambda i, td: (0, i))
    return pl.pallas_call(
        down_kernel,
        grid_spec=pltpu.PrefetchScalarGridSpec(
            num_scalar_prefetch=1,
            grid=(width // tile,),
            in_specs=[whole, whole, pair, part],
            out_specs=[out] * 4,
            scratch_shapes=[pltpu.VMEM((4 * rows, depth), BF16)],
        ),
        out_shape=[jax.ShapeDtypeStruct((rows, width), t) for t in (F32, BF16, BF16, BF16)],
        compiler_params=pltpu.CompilerParams(vmem_limit_bytes=40 << 20),
        cost_estimate=pl.CostEstimate(
            flops=8 * rows * depth * width,
            bytes_accessed=2 * depth * width + 8 * rows * depth + 10 * rows * width,
            transcendentals=0,
        ),
        name="down",
    )(td, h0, h2, h13, down_weight)


def per_device(tokens, gate_weight, up_weight, down_weight, block_ids, block_counts):
    d, t = lax.axis_index("dp"), lax.axis_index("tensor")
    td = (d ^ t).reshape(1).astype(jnp.int32)
    active = active_units(block_ids, block_counts, gate_weight.shape[1])
    turn = [(a * 4 + b, b * 4 + a) for a in range(4) for b in range(4)]
    rows = tokens.shape[0] // CHUNKS
    swap = lambda x, axis, mask: lax.ppermute(x, axis, xor_perm(4, mask))
    outs = []
    for c in range(CHUNKS):
        mine = lax.ppermute(tokens[c * rows : (c + 1) * rows], ("dp", "tensor"), turn)
        blocks = [mine] + [swap(mine, "tensor", j) for j in (1, 2, 3)]
        keep, send = gate_up(td, blocks, gate_weight, up_weight)
        near = swap(send, "dp", 1)
        across = swap((keep[1] + near[1].astype(F32)).astype(BF16), "dp", 2)
        total = keep[0] + near[0].astype(F32) + across.astype(F32)
        hidden = (jnp.maximum(total[0], 0.0) * total[1] * active).astype(BF16)
        far = swap(hidden, "dp", 2)
        other = swap(jnp.stack([hidden, far]), "dp", 1)
        o = down(td, hidden, far, other, down_weight)
        mixed = o[0]
        for j in (1, 2, 3):
            mixed = mixed + swap(o[j], "tensor", j).astype(F32)
        outs.append(lax.ppermute(mixed.astype(BF16), ("dp", "tensor"), turn))
    return jnp.concatenate(outs, axis=0)


def per_device_general(tokens, gate_weight, up_weight, down_weight, block_ids, block_counts):
    gathered = lax.all_gather(tokens, "tensor", axis=1, tiled=True)
    turned = lax.all_to_all(gathered, "dp", 1, 0, tiled=True)
    active = active_units(block_ids, block_counts, gate_weight.shape[1])
    sums = [
        lax.psum_scatter(
            jnp.dot(turned, w, preferred_element_type=F32), "dp", scatter_dimension=0, tiled=True
        )
        for w in (gate_weight, up_weight)
    ]
    hidden = (jnp.maximum(sums[0], 0.0) * sums[1] * active).astype(BF16)
    hidden = lax.all_gather(hidden, "dp", axis=0, tiled=True)
    partial = jnp.dot(hidden, down_weight, preferred_element_type=F32)
    partial = lax.all_to_all(partial, "dp", 0, 1, tiled=True)
    return lax.psum_scatter(partial, "tensor", scatter_dimension=1, tiled=True).astype(BF16)


def solution(mesh):
    placed = (
        P(("groups", "dp"), "tensor"),
        P("dp", "tensor"),
        P("dp", "tensor"),
        P("tensor", "dp"),
        P(("groups", "tensor")),
        P(("groups", "tensor")),
    )
    square = mesh.shape["dp"] == 4 and mesh.shape["tensor"] == 4
    return jax.shard_map(
        per_device if square else per_device_general,
        mesh=mesh,
        in_specs=placed,
        out_specs=P(("groups", "dp"), "tensor"),
        check_vma=False,
    )
```

time: 1350 us -> 264 us (0.20)
  waiting for transfers between devices: 1230 us -> 141 us
  matrix products: 98 us -> 0 us
  starting transfers between devices: 0.15 us -> 63.6 us
  Pallas kernels: 0 us -> 53.4 us
    all_gather x4 -> x0, waiting for transfers between devices: 1150 us -> none  [the longest x1 392 us: per_device(): lax.all_gather(gate_weight, 'dp', axis=0, tiled=True)]
    ppermute x0 -> x24, waiting for transfers between devices: none -> 141 us  [the longest x20 115 us: per_device(): swap = lambda x, axis, mask: lax.ppermute(x, axis, xor_perm(4, mask))]
    dot_general x3 -> x0, matrix products: 98 us -> none  [the longest x1 37.8 us: per_device(): jnp.dot(gathered, lax.all_gather(gate_weight, 'dp', axis=0, tiled=True),...]
    reduce_scatter x1 -> x0, waiting for transfers between devices: 78.1 us -> none  [per_device(): lax.psum_scatter(partials, 'tensor', scatter_dimension=1, tiled=True)]
    ppermute x0 -> x24, starting transfers between devices: none -> 63.6 us  [the longest x20 37.7 us: per_device(): swap = lambda x, axis, mask: lax.ppermute(x, axis, xor_perm(4, mask))]
    pallas_call x0 -> x4, Pallas kernels: none -> 53.4 us  [the longest x2 32.1 us: gate_up(): pl.pallas_call(gate_up_kernel, grid_spec=pltpu.PrefetchScalarGridSpec(num...]
  transfers between devices with their start and end apart: 5 -> 24, of which waited for: 5 -> 15; matrix products, arithmetic and copies ran while one was open for 5% -> 1% of each run, Pallas kernels for 0% -> 20%
where the time goes in v1:
time: 264 us; the launch traced here: 263 us
  waiting for transfers between devices  141 us (53%)
  starting transfers between devices  63.6 us (24%)
  Pallas kernels  53.4 us (20%)
  other arithmetic  3.26 us (1%)
    ppermute x20, waiting for transfers between devices, per_device(): swap = lambda x, axis, mask: lax.ppermute(x, axis, xor_perm(4, mask))  115 us
    ppermute x20, starting transfers between devices, per_device(): swap = lambda x, axis, mask: lax.ppermute(x, axis, xor_perm(4, mask))  37.7 us
    pallas_call x2, Pallas kernels, gate_up(): pl.pallas_call(gate_up_kernel, grid_spec=pltpu.PrefetchScalarGridSpec(num...  32.1 us
    pallas_call x2, Pallas kernels, down(): pl.pallas_call(down_kernel, grid_spec=pltpu.PrefetchScalarGridSpec(num_sc...  21.3 us
    ppermute x2, starting transfers between devices, per_device(): outs.append(lax.ppermute(mixed.astype(BF16), ('dp', 'tensor'), turn))  19.5 us
    ppermute x2, waiting for transfers between devices, per_device(): mine = lax.ppermute(tokens[c * rows:(c + 1) * rows], ('dp', 'tensor'), turn)  13.6 us
    ppermute x2, waiting for transfers between devices, per_device(): outs.append(lax.ppermute(mixed.astype(BF16), ('dp', 'tensor'), turn))  12.4 us
    ppermute x2, starting transfers between devices, per_device(): mine = lax.ppermute(tokens[c * rows:(c + 1) * rows], ('dp', 'tensor'), turn)  6.38 us
  transfers between devices with their start and end apart: 24, of which 15 were waited for; matrix products, arithmetic and copies ran while one was open for 1% of the time, Pallas kernels for 20%

profile of v1, /device:TPU:2, one launch (start us, length us, event | category | flops | bytes accessed | tf_op | source)
XLA Modules:
  0.0 263.3 jit_solution(11030642626576941762)
XLA Ops:
  1.1 4.5 %collective-permute-start.12 = (bf16[64,2048]{1,0:T(8,128)(2,1)S(1)}, bf16[64,2048]{1,0:T(8,128)(2,1)S(1)}, u32[]{:S(2)}, u32[]{:S(2)}) collective-permute-start(bf16[64,2048]{1,0:T(8,128)(2,1)S(1)} %get-tuple-element.30), channel_id=1, source_target_pairs={{0,0},{1,4},{2,8},{3,12},{4,1},{5,5},{6,9},{7,13},{8,2},{9,6},{10,... | collective-permute-start | bytes 786440 | tf_op jit(solution)/shard_map/ppermute | solution.py:125
  5.5 13.6 %collective-permute-done.12.x0 = bf16[64,2048]{1,0:T(8,128)(2,1)S(1)} collective-permute-done((bf16[64,2048]{1,0:T(8,128)(2,1)S(1)}, bf16[64,2048]{1,0:T(8,128)(2,1)S(1)}, u32[]{:S(2)}, u32[]{:S(2)}) %collective-permute-start.12) | collective-permute-done | bytes 262176 | tf_op jit(solution)/shard_map/ppermute | solution.py:125
  19.3 4.2 %collective-permute-start.15 = (bf16[64,2048]{1,0:T(8,128)(2,1)S(1)}, bf16[64,2048]{1,0:T(8,128)(2,1)S(1)}, u32[]{:S(2)}, u32[]{:S(2)}) collective-permute-start(bf16[64,2048]{1,0:T(8,128)(2,1)S(1)} %collective-permute-done.12.x0), channel_id=1, source_target_pairs={{0,3},{1,2},{2,1},{3,0},{4,7},{5,6},{6,5},{7,4},{8,11},{9,10},{10,... | collective-permute-start | bytes 786440 | tf_op jit(solution)/shard_map/ppermute | solution.py:122
  23.5 1.9 collective-permute-start
  25.4 2.9 %collective-permute-done.13.x1 = bf16[64,2048]{1,0:T(8,128)(2,1)S(1)} collective-permute-done((bf16[64,2048]{1,0:T(8,128)(2,1)S(1)}, bf16[64,2048]{1,0:T(8,128)(2,1)S(1)}, u32[]{:S(2)}, u32[]{:S(2)}) %collective-permute-start.13) | collective-permute-done | bytes 262176 | tf_op jit(solution)/shard_map/ppermute | solution.py:122
  28.3 9.6 %collective-permute-done.14.x2 = bf16[64,2048]{1,0:T(8,128)(2,1)S(1)} collective-permute-done((bf16[64,2048]{1,0:T(8,128)(2,1)S(1)}, bf16[64,2048]{1,0:T(8,128)(2,1)S(1)}, u32[]{:S(2)}, u32[]{:S(2)}) %collective-permute-start.14) | collective-permute-done | bytes 262176 | tf_op jit(solution)/shard_map/ppermute | solution.py:122
  37.9 16.0 %gate_up.3 = (f32[2,2,64,4096]{3,2,1,0:T(8,128)S(1)}, bf16[2,2,64,4096]{3,2,1,0:T(8,128)(2,1)S(1)}) custom-call(s32[1]{0:T(128)} %bitcast.td_ref, bf16[64,2048]{1,0:T(8,128)(2,1)S(1)} %collective-permute-done.12.x0, bf16[64,2048]{1,0:T(8,128)(2,1)S(1)} %collective-permute-done.13.x1, bf16[64,2048]{1,0:T(8,128)(2,1)S(1)} %collective-permute-done.14.x2, ...), custom_call_target="tpu_custom_call" | custom-call | flops 8589934592 | bytes 40894464 | tf_op jit(solution)/shard_map/gate_up/pallas_call | solution.py:51
  54.0 11.5 %collective-permute-start.1 = (bf16[64,2048]{1,0:T(8,128)(2,1)S(1)}, bf16[64,2048]{1,0:T(8,128)(2,1)S(1)}, u32[]{:S(2)}, u32[]{:S(2)}) collective-permute-start(bf16[64,2048]{1,0:T(8,128)(2,1)S(1)} %collective-permute-done.x0), channel_id=1, source_target_pairs={{0,1},{1,0},{2,3},{3,2},{4,5},{5,4},{6,7},{7,6},{8,9},{9,8},{10,11... | collective-permute-start | bytes 786440 | tf_op jit(solution)/shard_map/ppermute | solution.py:122
  65.5 2.0 collective-permute-start.2
  68.9 9.1 %collective-permute-done.1.x1 = bf16[64,2048]{1,0:T(8,128)(2,1)S(1)} collective-permute-done((bf16[64,2048]{1,0:T(8,128)(2,1)S(1)}, bf16[64,2048]{1,0:T(8,128)(2,1)S(1)}, u32[]{:S(2)}, u32[]{:S(2)}) %collective-permute-start.1) | collective-permute-done | bytes 262176 | tf_op jit(solution)/shard_map/ppermute | solution.py:122
  78.0 8.8 %collective-permute-done.3.x3 = bf16[64,2048]{1,0:T(8,128)(2,1)S(1)} collective-permute-done((bf16[64,2048]{1,0:T(8,128)(2,1)S(1)}, bf16[64,2048]{1,0:T(8,128)(2,1)S(1)}, u32[]{:S(2)}, u32[]{:S(2)}) %collective-permute-start.3) | collective-permute-done | bytes 262176 | tf_op jit(solution)/shard_map/ppermute | solution.py:122
  86.9 16.0 %gate_up.2 = (f32[2,2,64,4096]{3,2,1,0:T(8,128)S(1)}, bf16[2,2,64,4096]{3,2,1,0:T(8,128)(2,1)S(1)}) custom-call(s32[1]{0:T(128)} %bitcast.td_ref, bf16[64,2048]{1,0:T(8,128)(2,1)S(1)} %collective-permute-done.x0, bf16[64,2048]{1,0:T(8,128)(2,1)S(1)} %collective-permute-done.1.x1, bf16[64,2048]{1,0:T(8,128)(2,1)S(1)} %collective-permute-done.2.x2, ...), custom_call_target="tpu_custom_call" | custom-call | flops 8589934592 | bytes 40894464 | tf_op jit(solution)/shard_map/gate_up/pallas_call | solution.py:51
  104.0 2.1 collective-permute-start.17
  107.4 2.1 collective-permute-start.5
  109.5 20.7 %collective-permute-done.17 = bf16[2,64,4096]{2,1,0:T(8,128)(2,1)S(1)} collective-permute-done((bf16[2,64,4096]{2,1,0:T(8,128)(2,1)S(1)}, bf16[2,64,4096]{2,1,0:T(8,128)(2,1)S(1)}, u32[]{:S(2)}, u32[]{:S(2)}) %collective-permute-start.17) | collective-permute-done | bytes 1048608 | tf_op jit(solution)/shard_map/ppermute | solution.py:122
  130.5 21.9 %collective-permute-done.5 = bf16[2,64,4096]{2,1,0:T(8,128)(2,1)S(1)} collective-permute-done((bf16[2,64,4096]{2,1,0:T(8,128)(2,1)S(1)}, bf16[2,64,4096]{2,1,0:T(8,128)(2,1)S(1)}, u32[]{:S(2)}, u32[]{:S(2)}) %collective-permute-start.5) | collective-permute-done | bytes 1048608 | tf_op jit(solution)/shard_map/ppermute | solution.py:122
  153.1 1.8 collective-permute-start.6
  155.6 12.4 %collective-permute-done.6.h2 = bf16[64,4096]{1,0:T(8,128)(2,1)S(1)} collective-permute-done((bf16[64,4096]{1,0:T(8,128)(2,1)S(1)}, bf16[64,4096]{1,0:T(8,128)(2,1)S(1)}, u32[]{:S(2)}, u32[]{:S(2)}) %collective-permute-start.6) | collective-permute-done | bytes 524320 | tf_op jit(solution)/shard_map/ppermute | solution.py:122
  168.2 10.0 %collective-permute-done.18.h2 = bf16[64,4096]{1,0:T(8,128)(2,1)S(1)} collective-permute-done((bf16[64,4096]{1,0:T(8,128)(2,1)S(1)}, bf16[64,4096]{1,0:T(8,128)(2,1)S(1)}, u32[]{:S(2)}, u32[]{:S(2)}) %collective-permute-start.18) | collective-permute-done | bytes 524320 | tf_op jit(solution)/shard_map/ppermute | solution.py:122
  178.4 10.7 %down.2 = (f32[64,2048]{1,0:T(8,128)S(1)}, bf16[64,2048]{1,0:T(8,128)(2,1)S(1)}, bf16[64,2048]{1,0:T(8,128)(2,1)S(1)}, bf16[64,2048]{1,0:T(8,128)(2,1)S(1)}) custom-call(s32[1]{0:T(128)} %bitcast.td_ref, bf16[64,4096]{1,0:T(8,128)(2,1)S(1)} %get-tuple-element.33.h0, bf16[64,4096]{1,0:T(8,128)(2,1)S(1)} %collective-permute-done.6.h2, ...), custom_call_target="tpu_custom_call" | custom-call | flops 4294967296 | bytes 20185088 | tf_op jit(solution)/shard_map/down/pallas_call | solution.py:96
  189.0 2.9 %collective-permute-start.10 = (bf16[64,2048]{1,0:T(8,128)(2,1)S(1)}, bf16[64,2048]{1,0:T(8,128)(2,1)S(1)}, u32[]{:S(2)}, u32[]{:S(2)}) collective-permute-start(bf16[64,2048]{1,0:T(8,128)(2,1)S(1)} %get-tuple-element.22), channel_id=1, source_target_pairs={{0,3},{1,2},{2,1},{3,0},{4,7},{5,6},{6,5},{7,4},{8,11},{9,10},{10,... | collective-permute-start | bytes 786440 | tf_op jit(solution)/shard_map/ppermute | solution.py:122
  192.0 4.5 %collective-permute-start.8 = (bf16[64,2048]{1,0:T(8,128)(2,1)S(1)}, bf16[64,2048]{1,0:T(8,128)(2,1)S(1)}, u32[]{:S(2)}, u32[]{:S(2)}) collective-permute-start(bf16[64,2048]{1,0:T(8,128)(2,1)S(1)} %get-tuple-element.20), channel_id=1, source_target_pairs={{0,1},{1,0},{2,3},{3,2},{4,5},{5,4},{6,7},{7,6},{8,9},{9,8},{10,11... | collective-permute-start | bytes 786440 | tf_op jit(solution)/shard_map/ppermute | solution.py:122
  196.5 10.6 %down.3 = (f32[64,2048]{1,0:T(8,128)S(1)}, bf16[64,2048]{1,0:T(8,128)(2,1)S(1)}, bf16[64,2048]{1,0:T(8,128)(2,1)S(1)}, bf16[64,2048]{1,0:T(8,128)(2,1)S(1)}) custom-call(s32[1]{0:T(128)} %bitcast.td_ref, bf16[64,4096]{1,0:T(8,128)(2,1)S(1)} %get-tuple-element.34.h0, bf16[64,4096]{1,0:T(8,128)(2,1)S(1)} %collective-permute-done.18.h2, ...), custom_call_target="tpu_custom_call" | custom-call | flops 4294967296 | bytes 20185088 | tf_op jit(solution)/shard_map/down/pallas_call | solution.py:96
  207.1 1.6 collective-permute-start.20
  208.7 1.5 collective-permute-start.21
  211.6 5.4 %collective-permute-done.9 = bf16[64,2048]{1,0:T(8,128)(2,1)S(1)} collective-permute-done((bf16[64,2048]{1,0:T(8,128)(2,1)S(1)}, bf16[64,2048]{1,0:T(8,128)(2,1)S(1)}, u32[]{:S(2)}, u32[]{:S(2)}) %collective-permute-start.9) | collective-permute-done | bytes 262176 | tf_op jit(solution)/shard_map/ppermute | solution.py:122
  217.1 2.9 %collective-permute-start.11 = (bf16[64,2048]{1,0:T(8,128)(2,1)S(1)}, bf16[64,2048]{1,0:T(8,128)(2,1)S(1)}, u32[]{:S(2)}, u32[]{:S(2)}) collective-permute-start(bf16[64,2048]{1,0:T(8,128)(2,1)S(1)} %add_convert_fusion.3), channel_id=1, source_target_pairs={{0,0},{1,4},{2,8},{3,12},{4,1},{5,5},{6,9},{7,13},{8,2},{9,6},{10,... | collective-permute-start | bytes 786440 | tf_op jit(solution)/shard_map/ppermute | solution.py:138
  220.0 1.8 collective-permute-done.20
  221.9 11.5 %collective-permute-done.21 = bf16[64,2048]{1,0:T(8,128)(2,1)S(1)} collective-permute-done((bf16[64,2048]{1,0:T(8,128)(2,1)S(1)}, bf16[64,2048]{1,0:T(8,128)(2,1)S(1)}, u32[]{:S(2)}, u32[]{:S(2)}) %collective-permute-start.21) | collective-permute-done | bytes 262176 | tf_op jit(solution)/shard_map/ppermute | solution.py:122
  233.5 16.5 %collective-permute-start.23 = (bf16[64,2048]{1,0:T(8,128)(2,1)S(1)}, bf16[64,2048]{1,0:T(8,128)(2,1)S(1)}, u32[]{:S(2)}, u32[]{:S(2)}) collective-permute-start(bf16[64,2048]{1,0:T(8,128)(2,1)S(1)} %add_convert_fusion.2), channel_id=1, source_target_pairs={{0,0},{1,4},{2,8},{3,12},{4,1},{5,5},{6,9},{7,13},{8,2},{9,6},{10,... | collective-permute-start | bytes 786440 | tf_op jit(solution)/shard_map/ppermute | solution.py:138
  250.0 6.8 %collective-permute-done.11 = bf16[64,2048]{1,0:T(8,128)(2,1)S(1)} collective-permute-done((bf16[64,2048]{1,0:T(8,128)(2,1)S(1)}, bf16[64,2048]{1,0:T(8,128)(2,1)S(1)}, u32[]{:S(2)}, u32[]{:S(2)}) %collective-permute-start.11) | collective-permute-done | bytes 262176 | tf_op jit(solution)/shard_map/ppermute | solution.py:138
  256.9 5.6 %collective-permute-done.23 = bf16[64,2048]{1,0:T(8,128)(2,1)S(1)} collective-permute-done((bf16[64,2048]{1,0:T(8,128)(2,1)S(1)}, bf16[64,2048]{1,0:T(8,128)(2,1)S(1)}, u32[]{:S(2)}, u32[]{:S(2)}) %collective-permute-start.23) | collective-permute-done | bytes 262176 | tf_op jit(solution)/shard_map/ppermute | solution.py:138
  (39 shorter events, 8.9 us)
Async XLA Ops:
  1.1 18.1 %collective-permute-start.12 = (bf16[64,2048]{1,0:T(8,128)(2,1)S(1)}, bf16[64,2048]{1,0:T(8,128)(2,1)S(1)}, u32[]{:S(2)}, u32[]{:S(2)}) collective-permute-start(bf16[64,2048]{1,0:T(8,128)(2,1)S(1)} %get-tuple-element.30), channel_id=1, source_target_pairs={{0,0},{1,4},{2,8},{3,12},{4,1},{5,5},{6,9},{7,13},{8,2},{9,6},{10,... | collective-permute-start | bytes 786440 | tf_op jit(solution)/shard_map/ppermute | solution.py:125
  19.1 9.2 %collective-permute-start.13 = (bf16[64,2048]{1,0:T(8,128)(2,1)S(1)}, bf16[64,2048]{1,0:T(8,128)(2,1)S(1)}, u32[]{:S(2)}, u32[]{:S(2)}) collective-permute-start(bf16[64,2048]{1,0:T(8,128)(2,1)S(1)} %collective-permute-done.12.x0), channel_id=1, source_target_pairs={{0,1},{1,0},{2,3},{3,2},{4,5},{5,4},{6,7},{7,6},{8,9},{9,8},{10,11... | collective-permute-start | bytes 786440 | tf_op jit(solution)/shard_map/ppermute | solution.py:122
  19.3 18.6 %collective-permute-start.14 = (bf16[64,2048]{1,0:T(8,128)(2,1)S(1)}, bf16[64,2048]{1,0:T(8,128)(2,1)S(1)}, u32[]{:S(2)}, u32[]{:S(2)}) collective-permute-start(bf16[64,2048]{1,0:T(8,128)(2,1)S(1)} %collective-permute-done.12.x0), channel_id=1, source_target_pairs={{0,2},{1,3},{2,0},{3,1},{4,6},{5,7},{6,4},{7,5},{8,10},{9,11},{10,... | collective-permute-start | bytes 786440 | tf_op jit(solution)/shard_map/ppermute | solution.py:122
  19.3 18.6 %collective-permute-start.15 = (bf16[64,2048]{1,0:T(8,128)(2,1)S(1)}, bf16[64,2048]{1,0:T(8,128)(2,1)S(1)}, u32[]{:S(2)}, u32[]{:S(2)}) collective-permute-start(bf16[64,2048]{1,0:T(8,128)(2,1)S(1)} %collective-permute-done.12.x0), channel_id=1, source_target_pairs={{0,3},{1,2},{2,1},{3,0},{4,7},{5,6},{6,5},{7,4},{8,11},{9,10},{10,... | collective-permute-start | bytes 786440 | tf_op jit(solution)/shard_map/ppermute | solution.py:122
  23.5 30.5 %collective-permute-start = (bf16[64,2048]{1,0:T(8,128)(2,1)S(1)}, bf16[64,2048]{1,0:T(8,128)(2,1)S(1)}, u32[]{:S(2)}, u32[]{:S(2)}) collective-permute-start(bf16[64,2048]{1,0:T(8,128)(2,1)S(1)} %get-tuple-element.29), channel_id=1, source_target_pairs={{0,0},{1,4},{2,8},{3,12},{4,1},{5,5},{6,9},{7,13},{8,2},{9,6},{10,... | collective-permute-start | bytes 786440 | tf_op jit(solution)/shard_map/ppermute | solution.py:125
  53.9 49.7 %copy-start = (s32[32]{0:T(128)S(1)}, s32[32]{0:T(128)}, u32[]{:S(2)}) copy-start(s32[32]{0:T(128)} %param.10) | copy-start | bytes 388
  53.9 49.8 %collective-permute-start.16 = (bf16[2,2,64,4096]{3,2,1,0:T(8,128)(2,1)S(1)}, bf16[2,2,64,4096]{3,2,1,0:T(8,128)(2,1)S(1)}, u32[]{:S(2)}, u32[]{:S(2)}) collective-permute-start(bf16[2,2,64,4096]{3,2,1,0:T(8,128)(2,1)S(1)} %get-tuple-element.24), channel_id=1, source_target_pairs={{0,4},{4,0},{8,12},{12,8},{1,5},{5,1},{9,13},{13,9},{2,6},{6,2},{1... | collective-permute-start | bytes 6291464 | tf_op jit(solution)/shard_map/ppermute | solution.py:122
  54.0 24.0 %collective-permute-start.1 = (bf16[64,2048]{1,0:T(8,128)(2,1)S(1)}, bf16[64,2048]{1,0:T(8,128)(2,1)S(1)}, u32[]{:S(2)}, u32[]{:S(2)}) collective-permute-start(bf16[64,2048]{1,0:T(8,128)(2,1)S(1)} %collective-permute-done.x0), channel_id=1, source_target_pairs={{0,1},{1,0},{2,3},{3,2},{4,5},{5,4},{6,7},{7,6},{8,9},{9,8},{10,11... | collective-permute-start | bytes 786440 | tf_op jit(solution)/shard_map/ppermute | solution.py:122
  65.5 12.5 %collective-permute-start.2 = (bf16[64,2048]{1,0:T(8,128)(2,1)S(1)}, bf16[64,2048]{1,0:T(8,128)(2,1)S(1)}, u32[]{:S(2)}, u32[]{:S(2)}) collective-permute-start(bf16[64,2048]{1,0:T(8,128)(2,1)S(1)} %collective-permute-done.x0), channel_id=1, source_target_pairs={{0,2},{1,3},{2,0},{3,1},{4,6},{5,7},{6,4},{7,5},{8,10},{9,11},{10,... | collective-permute-start | bytes 786440 | tf_op jit(solution)/shard_map/ppermute | solution.py:122
  67.5 19.3 %collective-permute-start.3 = (bf16[64,2048]{1,0:T(8,128)(2,1)S(1)}, bf16[64,2048]{1,0:T(8,128)(2,1)S(1)}, u32[]{:S(2)}, u32[]{:S(2)}) collective-permute-start(bf16[64,2048]{1,0:T(8,128)(2,1)S(1)} %collective-permute-done.x0), channel_id=1, source_target_pairs={{0,3},{1,2},{2,1},{3,0},{4,7},{5,6},{6,5},{7,4},{8,11},{9,10},{10,... | collective-permute-start | bytes 786440 | tf_op jit(solution)/shard_map/ppermute | solution.py:122
  102.9 4.2 %collective-permute-start.4 = (bf16[2,2,64,4096]{3,2,1,0:T(8,128)(2,1)S(1)}, bf16[2,2,64,4096]{3,2,1,0:T(8,128)(2,1)S(1)}, u32[]{:S(2)}, u32[]{:S(2)}) collective-permute-start(bf16[2,2,64,4096]{3,2,1,0:T(8,128)(2,1)S(1)} %get-tuple-element.18), channel_id=1, source_target_pairs={{0,4},{4,0},{8,12},{12,8},{1,5},{5,1},{9,13},{13,9},{2,6},{6,2},{1... | collective-permute-start | bytes 6291464 | tf_op jit(solution)/shard_map/ppermute | solution.py:122
  104.0 26.1 %collective-permute-start.17 = (bf16[2,64,4096]{2,1,0:T(8,128)(2,1)S(1)}, bf16[2,64,4096]{2,1,0:T(8,128)(2,1)S(1)}, u32[]{:S(2)}, u32[]{:S(2)}) collective-permute-start(bf16[2,64,4096]{2,1,0:T(8,128)(2,1)S(1)} %fusion.1), channel_id=1, source_target_pairs={{0,8},{4,12},{8,0},{12,4},{1,9},{5,13},{9,1},{13,5},{2,10},{6,14},... | collective-permute-start | bytes 3145736 | tf_op jit(solution)/shard_map/ppermute | solution.py:122
  107.4 45.0 %collective-permute-start.5 = (bf16[2,64,4096]{2,1,0:T(8,128)(2,1)S(1)}, bf16[2,64,4096]{2,1,0:T(8,128)(2,1)S(1)}, u32[]{:S(2)}, u32[]{:S(2)}) collective-permute-start(bf16[2,64,4096]{2,1,0:T(8,128)(2,1)S(1)} %fusion), channel_id=1, source_target_pairs={{0,8},{4,12},{8,0},{12,4},{1,9},{5,13},{9,1},{13,5},{2,10},{6,14},... | collective-permute-start | bytes 3145736 | tf_op jit(solution)/shard_map/ppermute | solution.py:122
  153.1 14.9 %collective-permute-start.6 = (bf16[64,4096]{1,0:T(8,128)(2,1)S(1)}, bf16[64,4096]{1,0:T(8,128)(2,1)S(1)}, u32[]{:S(2)}, u32[]{:S(2)}) collective-permute-start(bf16[64,4096]{1,0:T(8,128)(2,1)S(1)} %get-tuple-element.33.h0), channel_id=1, source_target_pairs={{0,8},{4,12},{8,0},{12,4},{1,9},{5,13},{9,1},{13,5},{2,10},{6,14},... | collective-permute-start | bytes 1572872 | tf_op jit(solution)/shard_map/ppermute | solution.py:122
  154.9 23.2 %collective-permute-start.18 = (bf16[64,4096]{1,0:T(8,128)(2,1)S(1)}, bf16[64,4096]{1,0:T(8,128)(2,1)S(1)}, u32[]{:S(2)}, u32[]{:S(2)}) collective-permute-start(bf16[64,4096]{1,0:T(8,128)(2,1)S(1)} %get-tuple-element.34.h0), channel_id=1, source_target_pairs={{0,8},{4,12},{8,0},{12,4},{1,9},{5,13},{9,1},{13,5},{2,10},{6,14},... | collective-permute-start | bytes 1572872 | tf_op jit(solution)/shard_map/ppermute | solution.py:122
  168.1 10.3 %collective-permute-start.7 = (bf16[2,64,4096]{2,1,0:T(8,128)(2,1)S(1)}, bf16[2,64,4096]{2,1,0:T(8,128)(2,1)S(1)}, u32[]{:S(2)}, u32[]{:S(2)}) collective-permute-start(bf16[2,64,4096]{2,1,0:T(8,128)(2,1)S(1)} %pad_maximum_fusion), channel_id=1, source_target_pairs={{0,4},{4,0},{8,12},{12,8},{1,5},{5,1},{9,13},{13,9},{2,6},{6,2},{1... | collective-permute-start | bytes 3145736 | tf_op jit(solution)/shard_map/ppermute | solution.py:122
  178.3 18.2 %collective-permute-start.19 = (bf16[2,64,4096]{2,1,0:T(8,128)(2,1)S(1)}, bf16[2,64,4096]{2,1,0:T(8,128)(2,1)S(1)}, u32[]{:S(2)}, u32[]{:S(2)}) collective-permute-start(bf16[2,64,4096]{2,1,0:T(8,128)(2,1)S(1)} %pad_maximum_fusion.1), channel_id=1, source_target_pairs={{0,4},{4,0},{8,12},{12,8},{1,5},{5,1},{9,13},{13,9},{2,6},{6,2},{1... | collective-permute-start | bytes 3145736 | tf_op jit(solution)/shard_map/ppermute | solution.py:122
  189.0 21.1 %collective-permute-start.10 = (bf16[64,2048]{1,0:T(8,128)(2,1)S(1)}, bf16[64,2048]{1,0:T(8,128)(2,1)S(1)}, u32[]{:S(2)}, u32[]{:S(2)}) collective-permute-start(bf16[64,2048]{1,0:T(8,128)(2,1)S(1)} %get-tuple-element.22), channel_id=1, source_target_pairs={{0,3},{1,2},{2,1},{3,0},{4,7},{5,6},{6,5},{7,4},{8,11},{9,10},{10,... | collective-permute-start | bytes 786440 | tf_op jit(solution)/shard_map/ppermute | solution.py:122
  192.0 19.6 %collective-permute-start.8 = (bf16[64,2048]{1,0:T(8,128)(2,1)S(1)}, bf16[64,2048]{1,0:T(8,128)(2,1)S(1)}, u32[]{:S(2)}, u32[]{:S(2)}) collective-permute-start(bf16[64,2048]{1,0:T(8,128)(2,1)S(1)} %get-tuple-element.20), channel_id=1, source_target_pairs={{0,1},{1,0},{2,3},{3,2},{4,5},{5,4},{6,7},{7,6},{8,9},{9,8},{10,11... | collective-permute-start | bytes 786440 | tf_op jit(solution)/shard_map/ppermute | solution.py:122
  196.5 20.5 %collective-permute-start.9 = (bf16[64,2048]{1,0:T(8,128)(2,1)S(1)}, bf16[64,2048]{1,0:T(8,128)(2,1)S(1)}, u32[]{:S(2)}, u32[]{:S(2)}) collective-permute-start(bf16[64,2048]{1,0:T(8,128)(2,1)S(1)} %get-tuple-element.21), channel_id=1, source_target_pairs={{0,2},{1,3},{2,0},{3,1},{4,6},{5,7},{6,4},{7,5},{8,10},{9,11},{10,... | collective-permute-start | bytes 786440 | tf_op jit(solution)/shard_map/ppermute | solution.py:122
  207.1 14.7 %collective-permute-start.20 = (bf16[64,2048]{1,0:T(8,128)(2,1)S(1)}, bf16[64,2048]{1,0:T(8,128)(2,1)S(1)}, u32[]{:S(2)}, u32[]{:S(2)}) collective-permute-start(bf16[64,2048]{1,0:T(8,128)(2,1)S(1)} %get-tuple-element.26), channel_id=1, source_target_pairs={{0,1},{1,0},{2,3},{3,2},{4,5},{5,4},{6,7},{7,6},{8,9},{9,8},{10,11... | collective-permute-start | bytes 786440 | tf_op jit(solution)/shard_map/ppermute | solution.py:122
  208.7 24.6 %collective-permute-start.21 = (bf16[64,2048]{1,0:T(8,128)(2,1)S(1)}, bf16[64,2048]{1,0:T(8,128)(2,1)S(1)}, u32[]{:S(2)}, u32[]{:S(2)}) collective-permute-start(bf16[64,2048]{1,0:T(8,128)(2,1)S(1)} %get-tuple-element.27), channel_id=1, source_target_pairs={{0,2},{1,3},{2,0},{3,1},{4,6},{5,7},{6,4},{7,5},{8,10},{9,11},{10,... | collective-permute-start | bytes 786440 | tf_op jit(solution)/shard_map/ppermute | solution.py:122
  210.2 23.2 %collective-permute-start.22 = (bf16[64,2048]{1,0:T(8,128)(2,1)S(1)}, bf16[64,2048]{1,0:T(8,128)(2,1)S(1)}, u32[]{:S(2)}, u32[]{:S(2)}) collective-permute-start(bf16[64,2048]{1,0:T(8,128)(2,1)S(1)} %get-tuple-element.28), channel_id=1, source_target_pairs={{0,3},{1,2},{2,1},{3,0},{4,7},{5,6},{6,5},{7,4},{8,11},{9,10},{10,... | collective-permute-start | bytes 786440 | tf_op jit(solution)/shard_map/ppermute | solution.py:122
  217.1 39.8 %collective-permute-start.11 = (bf16[64,2048]{1,0:T(8,128)(2,1)S(1)}, bf16[64,2048]{1,0:T(8,128)(2,1)S(1)}, u32[]{:S(2)}, u32[]{:S(2)}) collective-permute-start(bf16[64,2048]{1,0:T(8,128)(2,1)S(1)} %add_convert_fusion.3), channel_id=1, source_target_pairs={{0,0},{1,4},{2,8},{3,12},{4,1},{5,5},{6,9},{7,13},{8,2},{9,6},{10,... | collective-permute-start | bytes 786440 | tf_op jit(solution)/shard_map/ppermute | solution.py:138
  233.5 29.0 %collective-permute-start.23 = (bf16[64,2048]{1,0:T(8,128)(2,1)S(1)}, bf16[64,2048]{1,0:T(8,128)(2,1)S(1)}, u32[]{:S(2)}, u32[]{:S(2)}) collective-permute-start(bf16[64,2048]{1,0:T(8,128)(2,1)S(1)} %add_convert_fusion.2), channel_id=1, source_target_pairs={{0,0},{1,4},{2,8},{3,12},{4,1},{5,5},{6,9},{7,13},{8,2},{9,6},{10,... | collective-permute-start | bytes 786440 | tf_op jit(solution)/shard_map/ppermute | solution.py:138

commit v2 on v1

v2 whole, which is shorter than its diff:
```python
import functools

import jax
import jax.numpy as jnp
from jax import lax
from jax.experimental import pallas as pl
from jax.experimental.pallas import tpu as pltpu
from jax.sharding import PartitionSpec as P

SIZES = (64, 64)
CHUNKS = len(SIZES)
COST1 = 20000
COST2 = 1000
HOLD = True
AFTER = True
SPREAD = "p"
HALVES = (1, 1)
MIXAT = 1
TILE2 = 512
CUBE = (True, True)
ORDER = 0
MIX = 0
RESIDENT = False
BF16, F32 = jnp.bfloat16, jnp.float32


def xor_perm(size, mask):
    return [(i, i ^ mask) for i in range(size)]


def active_units(block_ids, block_counts, unit_count):
    block_total = block_ids.shape[0]
    places = jnp.arange(block_total, dtype=jnp.int32)
    match = (block_ids[:, None] % block_total == places[None, :]) & (
        places < block_counts[0]
    )[:, None]
    active = jnp.any(match, axis=0).astype(F32)
    return jnp.repeat(active, unit_count // block_total)


def gate_up_kernel(tile, td_ref, *refs):
    xrefs, (gate_ref, up_ref, keep_ref, send_ref, xs) = refs[:-5], refs[-5:]
    rows = xs.shape[0] // 4

    @pl.when(pl.program_id(0) == 0)
    def _():
        for j in range(4):
            place = pl.multiple_of((j ^ td_ref[0]) * rows, rows)
            xs[pl.ds(place, rows), :] = xrefs[j][...] if len(xrefs) == 4 else xrefs[0][j]

    cols = pl.ds(pl.multiple_of(pl.program_id(0) * tile, tile), tile)
    for i, w in enumerate((gate_ref, up_ref)):
        acc = jnp.dot(xs[...], w[:, cols] if RESIDENT else w[...], preferred_element_type=F32)
        keep_ref[0, i] = acc[:rows]
        send_ref[0, i] = acc[rows : 2 * rows].astype(BF16)
        keep_ref[1, i] = acc[2 * rows : 3 * rows]
        send_ref[1, i] = acc[3 * rows :].astype(BF16)


def gate_up(td, blocks, gate_weight, up_weight, tile=512):
    rows, depth = blocks[0].shape[-2:]
    units = gate_weight.shape[1]
    whole = [pl.BlockSpec(x.shape, lambda i, td, r=x.ndim: (0,) * r) for x in blocks]
    part = pl.BlockSpec(memory_space=pltpu.VMEM) if RESIDENT else pl.BlockSpec((depth, tile), lambda i, td: (0, i))
    out = pl.BlockSpec((2, 2, rows, tile), lambda i, td: (0, 0, 0, i))
    return pl.pallas_call(
        functools.partial(gate_up_kernel, tile),
        grid_spec=pltpu.PrefetchScalarGridSpec(
            num_scalar_prefetch=1,
            grid=(units // tile,),
            in_specs=whole + [part] * 2,
            out_specs=[out, out],
            scratch_shapes=[pltpu.VMEM((4 * rows, depth), BF16)],
        ),
        out_shape=[
            jax.ShapeDtypeStruct((2, 2, rows, units), F32),
            jax.ShapeDtypeStruct((2, 2, rows, units), BF16),
        ],
        compiler_params=pltpu.CompilerParams(vmem_limit_bytes=(8 if RESIDENT else 40) << 20),
        cost_estimate=pl.CostEstimate(
            flops=COST1 * 1000,
            bytes_accessed=COST1 * 1000,
            transcendentals=0,
        ),
        name="gate_up",
    )(td, *blocks, gate_weight, up_weight)


def down_kernel(tile, td_ref, h0, h1, h2, h3, down_ref, own_ref, full_ref, hs):
    rows = h0.shape[0]

    @pl.when(pl.program_id(0) == 0)
    def _():
        for k, h in enumerate((h0, h1, h2, h3)):
            place = pl.multiple_of((k ^ td_ref[0]) * rows, rows)
            hs[pl.ds(place, rows), :] = h[...]

    cols = pl.ds(pl.multiple_of(pl.program_id(0) * tile, tile), tile)
    acc = jnp.dot(hs[...], down_ref[:, cols] if RESIDENT else down_ref[...], preferred_element_type=F32)
    own_ref[...] = acc[:rows]
    for j in range(4):
        full_ref[j ^ td_ref[1]] = acc[j * rows : (j + 1) * rows].astype(BF16)


def down(td, h0, h1, h2, h3, down_weight, part, parts):
    rows, depth = h0.shape
    width = down_weight.shape[1] // parts
    tile = TILE2
    first = part * (width // tile)
    whole = pl.BlockSpec((rows, depth), lambda i, td: (0, 0))
    weight = pl.BlockSpec((depth, tile), lambda i, td: (0, first + i))
    out = pl.BlockSpec((rows, tile), lambda i, td: (0, i))
    return pl.pallas_call(
        functools.partial(down_kernel, tile),
        grid_spec=pltpu.PrefetchScalarGridSpec(
            num_scalar_prefetch=1,
            grid=(width // tile,),
            in_specs=[whole] * 4 + [weight],
            out_specs=[out, pl.BlockSpec((4, rows, tile), lambda i, td: (0, 0, i))],
            scratch_shapes=[pltpu.VMEM((4 * rows, depth), BF16)],
        ),
        out_shape=[jax.ShapeDtypeStruct((rows, width), F32), jax.ShapeDtypeStruct((4, rows, width), BF16)],
        compiler_params=pltpu.CompilerParams(vmem_limit_bytes=(8 if RESIDENT else 40) << 20),
        cost_estimate=pl.CostEstimate(
            flops=COST2 * 1000,
            bytes_accessed=COST2 * 1000,
            transcendentals=0,
        ),
        name="down",
    )(td, h0, h1, h2, h3, down_weight)


def per_device(tokens, gate_weight, up_weight, down_weight, block_ids, block_counts):
    d, t = lax.axis_index("dp"), lax.axis_index("tensor")
    td = (d ^ t).reshape(1).astype(jnp.int32)
    dt = jnp.stack([d ^ t, t]).astype(jnp.int32)
    dd = d.reshape(1).astype(jnp.int32)
    active = active_units(block_ids, block_counts, gate_weight.shape[1])
    turn = [(a * 4 + b, b * 4 + a) for a in range(4) for b in range(4)]
    starts = [sum(SIZES[:c]) for c in range(CHUNKS + 1)]
    swap = lambda x, axis, mask: lax.ppermute(x, axis, xor_perm(4, mask))
    after = lambda x, *earlier: lax.optimization_barrier((x, *earlier))[0]
    blocks, mine, keep, send, near, across, hidden, far, pair = ([None] * CHUNKS for _ in range(9))
    parts, got, outs = {}, {}, {}
    tick = [td]


    def turn_in(c):
        x = tokens[starts[c] : starts[c + 1]]
        if c > 0:
            x = after(x, mine[c - 1])
        mine[c] = lax.ppermute(x, ("dp", "tensor"), turn)

    def spread(c):
        x = mine[c]
        if c > 0 and AFTER:
            x = after(x, *blocks[c - 1])
        if SPREAD == "a":
            y = lax.all_to_all(jnp.broadcast_to(x, (4, *x.shape)), "tensor", 0, 0, tiled=True)
            blocks[c] = [y]
        else:
            one, two = swap(x, "tensor", 1), swap(x, "tensor", 2)
            three = swap(two, "tensor", 1) if CUBE[c] else swap(x, "tensor", 3)
            blocks[c] = [mine[c], one, two, three]

    def first(c):
        if c + 1 < CHUNKS:
            tick.append(mine[c + 1])
        keep[c], send[c] = gate_up(after(dd if SPREAD == "a" else td, *tick), blocks[c], gate_weight, up_weight)
        tick[:] = [send[c]]

    def near_sum(c):
        held = after(send[c], *blocks[c + 1][:3 if CUBE[c + 1] else 4]) if HOLD and c + 1 < CHUNKS else send[c]
        near[c] = swap(held, "dp", 1)

    def add(c):
        x, _ = lax.optimization_barrier((keep[c], tuple(tick)))
        keep[c] = x
        summed = (x[1] + near[c][1].astype(F32)).astype(BF16)
        across[c] = swap(summed, "dp", 2)
        tick[:] = [summed]

    def gated(c):
        x, _ = lax.optimization_barrier((keep[c], tuple(tick)))
        total = x[0] + near[c][0].astype(F32) + across[c].astype(F32)
        hidden[c] = (jnp.maximum(total[0], 0.0) * total[1] * active).astype(BF16)
        far[c] = swap(hidden[c], "dp", 2)
        pair[c] = [swap(hidden[c], "dp", 1), swap(far[c], "dp", 1)]
        tick[:] = [hidden[c]]

    def second(c, h):
        parts[c, h] = down(after(dt, *tick), hidden[c], pair[c][0], far[c], pair[c][1], down_weight, h, HALVES[c])
        got[c, h] = lax.all_to_all(parts[c, h][1], "tensor", 0, 0, tiled=True)
        tick[:] = [parts[c, h][1]]

    def mix(c, h):
        mixed, _ = lax.optimization_barrier((parts[c, h][0], tuple(tick)))
        for j in range(4):
            mixed = mixed + jnp.where(t == j, 0.0, got[c, h][j].astype(F32))
        mixed = mixed.astype(BF16)
        outs[c, h] = lax.ppermute(mixed, ("dp", "tensor"), turn)
        tick[:] = [mixed]

    turn_in(0)
    spread(0)
    turn_in(1)
    first(0)
    spread(1)
    near_sum(0)
    add(0)
    first(1)
    near_sum(1)
    gated(0)
    add(1)
    for h in range(HALVES[0]):
        second(0, h)
    gated(1)
    second(1, 0)
    if MIXAT == 0:
        for h in range(HALVES[0]):
            mix(0, h)
    for h in range(1, HALVES[1]):
        second(1, h)
    if MIXAT == 1:
        for h in range(HALVES[0]):
            mix(0, h)
    for h in range(HALVES[1]):
        mix(1, h)
    return jnp.concatenate(
        [jnp.concatenate([outs[c, h] for h in range(HALVES[c])], axis=1) for c in range(CHUNKS)], axis=0
    )


def per_device_general(tokens, gate_weight, up_weight, down_weight, block_ids, block_counts):
    gathered = lax.all_gather(tokens, "tensor", axis=1, tiled=True)
    turned = lax.all_to_all(gathered, "dp", 1, 0, tiled=True)
    active = active_units(block_ids, block_counts, gate_weight.shape[1])
    sums = [
        lax.psum_scatter(
            jnp.dot(turned, w, preferred_element_type=F32), "dp", scatter_dimension=0, tiled=True
        )
        for w in (gate_weight, up_weight)
    ]
    hidden = (jnp.maximum(sums[0], 0.0) * sums[1] * active).astype(BF16)
    hidden = lax.all_gather(hidden, "dp", axis=0, tiled=True)
    partial = jnp.dot(hidden, down_weight, preferred_element_type=F32)
    partial = lax.all_to_all(partial, "dp", 0, 1, tiled=True)
    return lax.psum_scatter(partial, "tensor", scatter_dimension=1, tiled=True).astype(BF16)


def solution(mesh):
    placed = (
        P(("groups", "dp"), "tensor"),
        P("dp", "tensor"),
        P("dp", "tensor"),
        P("tensor", "dp"),
        P(("groups", "tensor")),
        P(("groups", "tensor")),
    )
    square = mesh.shape["dp"] == 4 and mesh.shape["tensor"] == 4
    return jax.shard_map(
        per_device if square else per_device_general,
        mesh=mesh,
        in_specs=placed,
        out_specs=P(("groups", "dp"), "tensor"),
        check_vma=False,
    )
```

time: 264 us -> 216 us (0.82)
  waiting for transfers between devices: 141 us -> 102 us
  starting transfers between devices: 63.6 us -> 52.9 us
  other arithmetic: 3.26 us -> 5.97 us
    ppermute x20 -> x16, waiting for transfers between devices: 115 us -> 47.3 us  [per_device(): swap = lambda x, axis, mask: lax.ppermute(x, axis, xor_perm(4, mask))]
    all_to_all x0 -> x2, waiting for transfers between devices: none -> 21.2 us  [second(): got[c, h] = lax.all_to_all(parts[c, h][1], 'tensor', 0, 0, tiled=True)]
    ppermute x20 -> x16, starting transfers between devices: 37.7 us -> 23.6 us  [per_device(): swap = lambda x, axis, mask: lax.ppermute(x, axis, xor_perm(4, mask))]
    all_to_all x0 -> x2, starting transfers between devices: none -> 10.5 us  [second(): got[c, h] = lax.all_to_all(parts[c, h][1], 'tensor', 0, 0, tiled=True)]
    ppermute x4, waiting for transfers between devices: 26 us -> 33.7 us  [the longest x2 19.7 us: turn_in(): mine[c] = lax.ppermute(x, ('dp', 'tensor'), turn)]
    ppermute x4, starting transfers between devices: 25.9 us -> 18.8 us  [the longest x2 12.5 us: mix(): outs[c, h] = lax.ppermute(mixed, ('dp', 'tensor'), turn)]
  transfers between devices with their start and end apart: 24 -> 22, of which waited for: 15 -> 16; matrix products, arithmetic and copies ran while one was open for 1% -> 2% of each run, Pallas kernels for 20% -> 24%
where the time goes in v2:
time: 216 us; the launch traced here: 215 us
  waiting for transfers between devices  102 us (47%)
  starting transfers between devices  52.9 us (24%)
  Pallas kernels  52 us (24%)
  other arithmetic  5.97 us (3%)
    ppermute x16, waiting for transfers between devices, per_device(): swap = lambda x, axis, mask: lax.ppermute(x, axis, xor_perm(4, mask))  47.3 us
    pallas_call x2, Pallas kernels, gate_up(): pl.pallas_call(functools.partial(gate_up_kernel, tile), grid_spec=pltpu.P...  32.1 us
    ppermute x16, starting transfers between devices, per_device(): swap = lambda x, axis, mask: lax.ppermute(x, axis, xor_perm(4, mask))  23.6 us
    all_to_all x2, waiting for transfers between devices, second(): got[c, h] = lax.all_to_all(parts[c, h][1], 'tensor', 0, 0, tiled=True)  21.2 us
    pallas_call x2, Pallas kernels, down(): pl.pallas_call(functools.partial(down_kernel, tile), grid_spec=pltpu.Pref...  20 us
    ppermute x2, waiting for transfers between devices, turn_in(): mine[c] = lax.ppermute(x, ('dp', 'tensor'), turn)  19.7 us
    ppermute x2, waiting for transfers between devices, mix(): outs[c, h] = lax.ppermute(mixed, ('dp', 'tensor'), turn)  14.1 us
    ppermute x2, starting transfers between devices, mix(): outs[c, h] = lax.ppermute(mixed, ('dp', 'tensor'), turn)  12.5 us
  transfers between devices with their start and end apart: 22, of which 16 were waited for; matrix products, arithmetic and copies ran while one was open for 2% of the time, Pallas kernels for 24%

profile of v2, /device:TPU:2, one launch (start us, length us, event | category | flops | bytes accessed | tf_op | source)
XLA Modules:
  0.0 215.4 jit_solution(7393448833873592194)
XLA Ops:
  1.1 4.5 %collective-permute-start = (bf16[64,2048]{1,0:T(8,128)(2,1)S(1)}, bf16[64,2048]{1,0:T(8,128)(2,1)S(1)}, u32[]{:S(2)}, u32[]{:S(2)}) collective-permute-start(bf16[64,2048]{1,0:T(8,128)(2,1)S(1)} %get-tuple-element.46), channel_id=1, source_target_pairs={{0,0},{1,4},{2,8},{3,12},{4,1},{5,5},{6,9},{7,13},{8,2},{9,6},{10,... | collective-permute-start | bytes 786440 | tf_op jit(solution)/shard_map/ppermute | solution.py:152
  5.5 13.6 %collective-permute-done.refs_0_ = bf16[64,2048]{1,0:T(8,128)(2,1)S(1)} collective-permute-done((bf16[64,2048]{1,0:T(8,128)(2,1)S(1)}, bf16[64,2048]{1,0:T(8,128)(2,1)S(1)}, u32[]{:S(2)}, u32[]{:S(2)}) %collective-permute-start) | collective-permute-done | bytes 262176 | tf_op jit(solution)/shard_map/ppermute | solution.py:152
  19.1 1.9 collective-permute-start.1
  21.0 4.3 %collective-permute-start.2 = (bf16[64,2048]{1,0:T(8,128)(2,1)S(1)}, bf16[64,2048]{1,0:T(8,128)(2,1)S(1)}, u32[]{:S(2)}, u32[]{:S(2)}) collective-permute-start(bf16[64,2048]{1,0:T(8,128)(2,1)S(1)} %collective-permute-done.refs_0_), channel_id=1, source_target_pairs={{0,1},{1,0},{2,3},{3,2},{4,5},{5,4},{6,7},{7,6},{8,9},{9,8},{10,11... | collective-permute-start | bytes 786440 | tf_op jit(solution)/shard_map/ppermute | solution.py:141
  25.4 6.7 %collective-permute-done.3.refs_2_ = bf16[64,2048]{1,0:T(8,128)(2,1)S(1)} collective-permute-done((bf16[64,2048]{1,0:T(8,128)(2,1)S(1)}, bf16[64,2048]{1,0:T(8,128)(2,1)S(1)}, u32[]{:S(2)}, u32[]{:S(2)}) %collective-permute-start.3) | collective-permute-done | bytes 262176 | tf_op jit(solution)/shard_map/ppermute | solution.py:141
  32.1 3.4 %collective-permute-start.4 = (bf16[64,2048]{1,0:T(8,128)(2,1)S(1)}, bf16[64,2048]{1,0:T(8,128)(2,1)S(1)}, u32[]{:S(2)}, u32[]{:S(2)}) collective-permute-start(bf16[64,2048]{1,0:T(8,128)(2,1)S(1)} %collective-permute-done.3.refs_2_), channel_id=1, source_target_pairs={{0,1},{1,0},{2,3},{3,2},{4,5},{5,4},{6,7},{7,6},{8,9},{9,8},{10,11... | collective-permute-start | bytes 786440 | tf_op jit(solution)/shard_map/ppermute | solution.py:141
  35.5 6.1 %collective-permute-done.1.refs_0_ = bf16[64,2048]{1,0:T(8,128)(2,1)S(1)} collective-permute-done((bf16[64,2048]{1,0:T(8,128)(2,1)S(1)}, bf16[64,2048]{1,0:T(8,128)(2,1)S(1)}, u32[]{:S(2)}, u32[]{:S(2)}) %collective-permute-start.1) | collective-permute-done | bytes 262176 | tf_op jit(solution)/shard_map/ppermute | solution.py:152
  41.6 1.7 collective-permute-start.5
  43.4 5.6 %collective-permute-start.6 = (bf16[64,2048]{1,0:T(8,128)(2,1)S(1)}, bf16[64,2048]{1,0:T(8,128)(2,1)S(1)}, u32[]{:S(2)}, u32[]{:S(2)}) collective-permute-start(bf16[64,2048]{1,0:T(8,128)(2,1)S(1)} %collective-permute-done.1.refs_0_), channel_id=1, source_target_pairs={{0,2},{1,3},{2,0},{3,1},{4,6},{5,7},{6,4},{7,5},{8,10},{9,11},{10,... | collective-permute-start | bytes 786440 | tf_op jit(solution)/shard_map/ppermute | solution.py:141
  48.9 16.0 %gate_up.2 = (f32[2,2,64,4096]{3,2,1,0:T(8,128)S(1)}, bf16[2,2,64,4096]{3,2,1,0:T(8,128)(2,1)S(1)}) custom-call(s32[1]{0:T(128)} %bitcast.td_ref, bf16[64,2048]{1,0:T(8,128)(2,1)S(1)} %collective-permute-done.refs_0_, bf16[64,2048]{1,0:T(8,128)(2,1)S(1)} %collective-permute-done.2.refs_1_, bf16[64,2048]{1,0:T(8,128)(2,1)S(1)} %collective-permute-done.3.refs_2_, ...), custom_call_target="tpu_custom_call" | custom-call | flops 20000000 | bytes 20000000 | tf_op jit(solution)/shard_map/gate_up/pallas_call | solution.py:66
  65.0 1.7 collective-permute-start.7
  66.7 3.8 %collective-permute-done.7 = bf16[2,2,64,4096]{3,2,1,0:T(8,128)(2,1)S(1)} collective-permute-done((bf16[2,2,64,4096]{3,2,1,0:T(8,128)(2,1)S(1)}, bf16[2,2,64,4096]{3,2,1,0:T(8,128)(2,1)S(1)}, u32[]{:S(2)}, u32[]{:S(2)}) %collective-permute-start.7) | collective-permute-done | bytes 2097184 | tf_op jit(solution)/shard_map/ppermute | solution.py:141
  71.3 2.0 collective-permute-start.8
  74.1 5.5 %collective-permute-done.8.refs_3_ = bf16[64,2048]{1,0:T(8,128)(2,1)S(1)} collective-permute-done((bf16[64,2048]{1,0:T(8,128)(2,1)S(1)}, bf16[64,2048]{1,0:T(8,128)(2,1)S(1)}, u32[]{:S(2)}, u32[]{:S(2)}) %collective-permute-start.8) | collective-permute-done | bytes 262176 | tf_op jit(solution)/shard_map/ppermute | solution.py:141
  79.6 16.0 %gate_up.3 = (f32[2,2,64,4096]{3,2,1,0:T(8,128)S(1)}, bf16[2,2,64,4096]{3,2,1,0:T(8,128)(2,1)S(1)}) custom-call(s32[1]{0:T(128)} %bitcast.td_ref, bf16[64,2048]{1,0:T(8,128)(2,1)S(1)} %collective-permute-done.1.refs_0_, bf16[64,2048]{1,0:T(8,128)(2,1)S(1)} %collective-permute-done.5.refs_1_, bf16[64,2048]{1,0:T(8,128)(2,1)S(1)} %collective-permute-done.6.refs_2_, ...), custom_call_target="tpu_custom_call" | custom-call | flops 20000000 | bytes 20000000 | tf_op jit(solution)/shard_map/gate_up/pallas_call | solution.py:66
  97.9 2.0 collective-permute-done.10
  103.1 8.4 %collective-permute-done.12.h2 = bf16[64,4096]{1,0:T(8,128)(2,1)S(1)} collective-permute-done((bf16[64,4096]{1,0:T(8,128)(2,1)S(1)}, bf16[64,4096]{1,0:T(8,128)(2,1)S(1)}, u32[]{:S(2)}, u32[]{:S(2)}) %collective-permute-start.12) | collective-permute-done | bytes 524320 | tf_op jit(solution)/shard_map/ppermute | solution.py:141
  111.6 1.8 collective-permute-done.13.h3
  113.5 10.0 %down.2 = (f32[64,2048]{1,0:T(8,128)S(1)}, bf16[4,64,2048]{2,1,0:T(8,128)(2,1)}) custom-call(s32[2]{0:T(128)S(1)} %pad_add_fusion.td_ref, bf16[64,4096]{1,0:T(8,128)(2,1)S(1)} %fusion.8.h0, bf16[64,4096]{1,0:T(8,128)(2,1)S(1)} %collective-permute-done.11.h1, bf16[64,4096]{1,0:T(8,128)(2,1)S(1)} %collective-permute-done.12.h2, ...), custom_call_target="tpu_custom_call" | custom-call | flops 1000000 | bytes 1000000 | tf_op jit(solution)/shard_map/down/pallas_call | solution.py:113
  123.5 4.9 %all-to-all-start = ((bf16[4,64,2048]{2,1,0:T(8,128)(2,1)}), bf16[4,64,2048]{2,1,0:T(8,128)(2,1)S(1)}, u32[]{:S(2)}, u32[]{:S(2)}) async-start(bf16[4,64,2048]{2,1,0:T(8,128)(2,1)} %get-tuple-element.39), calls=%async_computation | async-start | bytes 2097152 | tf_op jit(solution)/shard_map/all_to_all | solution.py:193
  128.4 4.8 %collective-permute-done.14 = bf16[2,64,4096]{2,1,0:T(8,128)(2,1)S(1)} collective-permute-done((bf16[2,64,4096]{2,1,0:T(8,128)(2,1)}, bf16[2,64,4096]{2,1,0:T(8,128)(2,1)S(1)}, u32[]{:S(2)}, u32[]{:S(2)}) %collective-permute-start.14) | collective-permute-done | bytes 1048608 | tf_op jit(solution)/shard_map/ppermute | solution.py:141
  133.2 2.2 %bitcast_add_fusion = f32[2,64,4096]{2,1,0:T(8,128)S(1)} fusion(bf16[2,64,4096]{2,1,0:T(8,128)(2,1)S(1)} %collective-permute-done.14, f32[2,2,64,4096]{3,2,1,0:T(8,128)} %copy-done, bf16[2,2,64,4096]{3,2,1,0:T(8,128)(2,1)} %copy-done.1), kind=kLoop, calls=%fused_computation.2 | loop fusion | flops 2097152 | bytes 6291456 | tf_op jit(solution)/shard_map/add | solution.py:185
  135.5 1.6 collective-permute-start.16
  137.1 11.8 %collective-permute-done.16.h2 = bf16[64,4096]{1,0:T(8,128)(2,1)S(1)} collective-permute-done((bf16[64,4096]{1,0:T(8,128)(2,1)S(1)}, bf16[64,4096]{1,0:T(8,128)(2,1)S(1)}, u32[]{:S(2)}, u32[]{:S(2)}) %collective-permute-start.16) | collective-permute-done | bytes 524320 | tf_op jit(solution)/shard_map/ppermute | solution.py:141
  148.9 1.9 collective-permute-done.17.h3
  150.8 10.0 %down.3 = (f32[64,2048]{1,0:T(8,128)S(1)}, bf16[4,64,2048]{2,1,0:T(8,128)(2,1)}) custom-call(s32[2]{0:T(128)S(1)} %pad_add_fusion.td_ref, bf16[64,4096]{1,0:T(8,128)(2,1)S(1)} %fusion.5.h0, bf16[64,4096]{1,0:T(8,128)(2,1)S(1)} %collective-permute-done.15.h1, bf16[64,4096]{1,0:T(8,128)(2,1)S(1)} %collective-permute-done.16.h2, ...), custom_call_target="tpu_custom_call" | custom-call | flops 1000000 | bytes 1000000 | tf_op jit(solution)/shard_map/down/pallas_call | solution.py:113
  160.8 5.6 %all-to-all-start.1 = ((bf16[4,64,2048]{2,1,0:T(8,128)(2,1)}), bf16[4,64,2048]{2,1,0:T(8,128)(2,1)S(1)}, u32[]{:S(2)}, u32[]{:S(2)}) async-start(bf16[4,64,2048]{2,1,0:T(8,128)(2,1)} %get-tuple-element.42), calls=%async_computation.1 | async-start | bytes 2097152 | tf_op jit(solution)/shard_map/all_to_all | solution.py:193
  166.6 4.6 %collective-permute-start.18 = (bf16[64,2048]{1,0:T(8,128)(2,1)S(1)}, bf16[64,2048]{1,0:T(8,128)(2,1)S(1)}, u32[]{:S(2)}, u32[]{:S(2)}) collective-permute-start(bf16[64,2048]{1,0:T(8,128)(2,1)S(1)} %fusion.10), channel_id=1, source_target_pairs={{0,0},{1,4},{2,8},{3,12},{4,1},{5,5},{6,9},{7,13},{8,2},{9,6},{10,... | collective-permute-start | bytes 786440 | tf_op jit(solution)/shard_map/ppermute | solution.py:201
  171.2 21.2 %all-to-all-done.1 = bf16[4,64,2048]{2,1,0:T(8,128)(2,1)S(1)} async-done(((bf16[4,64,2048]{2,1,0:T(8,128)(2,1)}), bf16[4,64,2048]{2,1,0:T(8,128)(2,1)S(1)}, u32[]{:S(2)}, u32[]{:S(2)}) %all-to-all-start.1) | async-done | bytes 1048608 | tf_op jit(solution)/shard_map/all_to_all | solution.py:193
  192.6 7.9 %collective-permute-start.19 = (bf16[64,2048]{1,0:T(8,128)(2,1)S(1)}, bf16[64,2048]{1,0:T(8,128)(2,1)S(1)}, u32[]{:S(2)}, u32[]{:S(2)}) collective-permute-start(bf16[64,2048]{1,0:T(8,128)(2,1)S(1)} %fusion.9), channel_id=1, source_target_pairs={{0,0},{1,4},{2,8},{3,12},{4,1},{5,5},{6,9},{7,13},{8,2},{9,6},{10,... | collective-permute-start | bytes 786440 | tf_op jit(solution)/shard_map/ppermute | solution.py:201
  200.5 9.4 %collective-permute-done.18 = bf16[64,2048]{1,0:T(8,128)(2,1)S(1)} collective-permute-done((bf16[64,2048]{1,0:T(8,128)(2,1)S(1)}, bf16[64,2048]{1,0:T(8,128)(2,1)S(1)}, u32[]{:S(2)}, u32[]{:S(2)}) %collective-permute-start.18) | collective-permute-done | bytes 262176 | tf_op jit(solution)/shard_map/ppermute | solution.py:201
  210.0 4.6 %collective-permute-done.19 = bf16[64,2048]{1,0:T(8,128)(2,1)S(1)} collective-permute-done((bf16[64,2048]{1,0:T(8,128)(2,1)S(1)}, bf16[64,2048]{1,0:T(8,128)(2,1)S(1)}, u32[]{:S(2)}, u32[]{:S(2)}) %collective-permute-start.19) | collective-permute-done | bytes 262176 | tf_op jit(solution)/shard_map/ppermute | solution.py:201
  (38 shorter events, 9.0 us)
Async XLA Ops:
  1.1 18.0 %collective-permute-start = (bf16[64,2048]{1,0:T(8,128)(2,1)S(1)}, bf16[64,2048]{1,0:T(8,128)(2,1)S(1)}, u32[]{:S(2)}, u32[]{:S(2)}) collective-permute-start(bf16[64,2048]{1,0:T(8,128)(2,1)S(1)} %get-tuple-element.46), channel_id=1, source_target_pairs={{0,0},{1,4},{2,8},{3,12},{4,1},{5,5},{6,9},{7,13},{8,2},{9,6},{10,... | collective-permute-start | bytes 786440 | tf_op jit(solution)/shard_map/ppermute | solution.py:152
  19.1 13.0 %collective-permute-start.3 = (bf16[64,2048]{1,0:T(8,128)(2,1)S(1)}, bf16[64,2048]{1,0:T(8,128)(2,1)S(1)}, u32[]{:S(2)}, u32[]{:S(2)}) collective-permute-start(bf16[64,2048]{1,0:T(8,128)(2,1)S(1)} %collective-permute-done.refs_0_), channel_id=1, source_target_pairs={{0,2},{1,3},{2,0},{3,1},{4,6},{5,7},{6,4},{7,5},{8,10},{9,11},{10,... | collective-permute-start | bytes 786440 | tf_op jit(solution)/shard_map/ppermute | solution.py:141
  19.1 22.5 %collective-permute-start.1 = (bf16[64,2048]{1,0:T(8,128)(2,1)S(1)}, bf16[64,2048]{1,0:T(8,128)(2,1)S(1)}, u32[]{:S(2)}, u32[]{:S(2)}) collective-permute-start(bf16[64,2048]{1,0:T(8,128)(2,1)S(1)} %get-tuple-element.26), channel_id=1, source_target_pairs={{0,0},{1,4},{2,8},{3,12},{4,1},{5,5},{6,9},{7,13},{8,2},{9,6},{10,... | collective-permute-start | bytes 786440 | tf_op jit(solution)/shard_map/ppermute | solution.py:152
  21.0 20.5 %collective-permute-start.2 = (bf16[64,2048]{1,0:T(8,128)(2,1)S(1)}, bf16[64,2048]{1,0:T(8,128)(2,1)S(1)}, u32[]{:S(2)}, u32[]{:S(2)}) collective-permute-start(bf16[64,2048]{1,0:T(8,128)(2,1)S(1)} %collective-permute-done.refs_0_), channel_id=1, source_target_pairs={{0,1},{1,0},{2,3},{3,2},{4,5},{5,4},{6,7},{7,6},{8,9},{9,8},{10,11... | collective-permute-start | bytes 786440 | tf_op jit(solution)/shard_map/ppermute | solution.py:141
  32.1 9.5 %collective-permute-start.4 = (bf16[64,2048]{1,0:T(8,128)(2,1)S(1)}, bf16[64,2048]{1,0:T(8,128)(2,1)S(1)}, u32[]{:S(2)}, u32[]{:S(2)}) collective-permute-start(bf16[64,2048]{1,0:T(8,128)(2,1)S(1)} %collective-permute-done.3.refs_2_), channel_id=1, source_target_pairs={{0,1},{1,0},{2,3},{3,2},{4,5},{5,4},{6,7},{7,6},{8,9},{9,8},{10,11... | collective-permute-start | bytes 786440 | tf_op jit(solution)/shard_map/ppermute | solution.py:141
  41.6 23.3 %collective-permute-start.5 = (bf16[64,2048]{1,0:T(8,128)(2,1)S(1)}, bf16[64,2048]{1,0:T(8,128)(2,1)S(1)}, u32[]{:S(2)}, u32[]{:S(2)}) collective-permute-start(bf16[64,2048]{1,0:T(8,128)(2,1)S(1)} %collective-permute-done.1.refs_0_), channel_id=1, source_target_pairs={{0,1},{1,0},{2,3},{3,2},{4,5},{5,4},{6,7},{7,6},{8,9},{9,8},{10,11... | collective-permute-start | bytes 786440 | tf_op jit(solution)/shard_map/ppermute | solution.py:141
  43.4 21.6 %collective-permute-start.6 = (bf16[64,2048]{1,0:T(8,128)(2,1)S(1)}, bf16[64,2048]{1,0:T(8,128)(2,1)S(1)}, u32[]{:S(2)}, u32[]{:S(2)}) collective-permute-start(bf16[64,2048]{1,0:T(8,128)(2,1)S(1)} %collective-permute-done.1.refs_0_), channel_id=1, source_target_pairs={{0,2},{1,3},{2,0},{3,1},{4,6},{5,7},{6,4},{7,5},{8,10},{9,11},{10,... | collective-permute-start | bytes 786440 | tf_op jit(solution)/shard_map/ppermute | solution.py:141
  65.0 5.5 %collective-permute-start.7 = (bf16[2,2,64,4096]{3,2,1,0:T(8,128)(2,1)S(1)}, bf16[2,2,64,4096]{3,2,1,0:T(8,128)(2,1)S(1)}, u32[]{:S(2)}, u32[]{:S(2)}) collective-permute-start(bf16[2,2,64,4096]{3,2,1,0:T(8,128)(2,1)S(1)} %get-tuple-element.31), channel_id=1, source_target_pairs={{0,4},{4,0},{8,12},{12,8},{1,5},{5,1},{9,13},{13,9},{2,6},{6,2},{1... | collective-permute-start | bytes 6291464 | tf_op jit(solution)/shard_map/ppermute | solution.py:141
  66.7 6.6 %copy-start.2 = (s32[32]{0:T(128)S(1)}, s32[32]{0:T(128)}, u32[]{:S(2)}) copy-start(s32[32]{0:T(128)} %param.10) | copy-start | bytes 388
  70.7 25.5 %collective-permute-start.9 = (bf16[2,64,4096]{2,1,0:T(8,128)(2,1)S(1)}, bf16[2,64,4096]{2,1,0:T(8,128)(2,1)S(1)}, u32[]{:S(2)}, u32[]{:S(2)}) collective-permute-start(bf16[2,64,4096]{2,1,0:T(8,128)(2,1)S(1)} %fusion.2), channel_id=1, source_target_pairs={{0,8},{4,12},{8,0},{12,4},{1,9},{5,13},{9,1},{13,5},{2,10},{6,14},... | collective-permute-start | bytes 3145736 | tf_op jit(solution)/shard_map/ppermute | solution.py:141
  71.3 8.3 %collective-permute-start.8 = (bf16[64,2048]{1,0:T(8,128)(2,1)S(1)}, bf16[64,2048]{1,0:T(8,128)(2,1)S(1)}, u32[]{:S(2)}, u32[]{:S(2)}) collective-permute-start(bf16[64,2048]{1,0:T(8,128)(2,1)S(1)} %collective-permute-done.6.refs_2_), channel_id=1, source_target_pairs={{0,1},{1,0},{2,3},{3,2},{4,5},{5,4},{6,7},{7,6},{8,9},{9,8},{10,11... | collective-permute-start | bytes 786440 | tf_op jit(solution)/shard_map/ppermute | solution.py:141
  95.6 4.2 %copy-start = (f32[2,2,64,4096]{3,2,1,0:T(8,128)}, f32[2,2,64,4096]{3,2,1,0:T(8,128)S(1)}, u32[]{:S(2)}) copy-start(f32[2,2,64,4096]{3,2,1,0:T(8,128)S(1)} %get-tuple-element.40) | copy-start | bytes 12582916
  95.7 4.2 %collective-permute-start.10 = (bf16[2,2,64,4096]{3,2,1,0:T(8,128)(2,1)S(1)}, bf16[2,2,64,4096]{3,2,1,0:T(8,128)(2,1)S(1)}, u32[]{:S(2)}, u32[]{:S(2)}) collective-permute-start(bf16[2,2,64,4096]{3,2,1,0:T(8,128)(2,1)S(1)} %get-tuple-element.34), channel_id=1, source_target_pairs={{0,4},{4,0},{8,12},{12,8},{1,5},{5,1},{9,13},{13,9},{2,6},{6,2},{1... | collective-permute-start | bytes 6291464 | tf_op jit(solution)/shard_map/ppermute | solution.py:141
  96.7 14.8 %collective-permute-start.12 = (bf16[64,4096]{1,0:T(8,128)(2,1)S(1)}, bf16[64,4096]{1,0:T(8,128)(2,1)S(1)}, u32[]{:S(2)}, u32[]{:S(2)}) collective-permute-start(bf16[64,4096]{1,0:T(8,128)(2,1)S(1)} %fusion.8.h0), channel_id=1, source_target_pairs={{0,8},{4,12},{8,0},{12,4},{1,9},{5,13},{9,1},{13,5},{2,10},{6,14},... | collective-permute-start | bytes 1572872 | tf_op jit(solution)/shard_map/ppermute | solution.py:141
  99.9 1.7 copy-start.1
  101.6 31.5 %collective-permute-start.14 = (bf16[2,64,4096]{2,1,0:T(8,128)(2,1)}, bf16[2,64,4096]{2,1,0:T(8,128)(2,1)S(1)}, u32[]{:S(2)}, u32[]{:S(2)}) collective-permute-start(bf16[2,64,4096]{2,1,0:T(8,128)(2,1)} %fusion.1), channel_id=1, source_target_pairs={{0,8},{4,12},{8,0},{12,4},{1,9},{5,13},{9,1},{13,5},{2,10},{6,14},... | collective-permute-start | bytes 3145736 | tf_op jit(solution)/shard_map/ppermute | solution.py:141
  103.1 8.5 %collective-permute-start.11 = (bf16[64,4096]{1,0:T(8,128)(2,1)S(1)}, bf16[64,4096]{1,0:T(8,128)(2,1)S(1)}, u32[]{:S(2)}, u32[]{:S(2)}) collective-permute-start(bf16[64,4096]{1,0:T(8,128)(2,1)S(1)} %fusion.8.h0), channel_id=1, source_target_pairs={{0,4},{4,0},{8,12},{12,8},{1,5},{5,1},{9,13},{13,9},{2,6},{6,2},{1... | collective-permute-start | bytes 1572872 | tf_op jit(solution)/shard_map/ppermute | solution.py:141
  111.5 1.9 collective-permute-start.13
  123.5 37.3 %all-to-all-start = ((bf16[4,64,2048]{2,1,0:T(8,128)(2,1)}), bf16[4,64,2048]{2,1,0:T(8,128)(2,1)S(1)}, u32[]{:S(2)}, u32[]{:S(2)}) async-start(bf16[4,64,2048]{2,1,0:T(8,128)(2,1)} %get-tuple-element.39), calls=%async_computation | async-start | bytes 2097152 | tf_op jit(solution)/shard_map/all_to_all | solution.py:193
  135.5 13.4 %collective-permute-start.16 = (bf16[64,4096]{1,0:T(8,128)(2,1)S(1)}, bf16[64,4096]{1,0:T(8,128)(2,1)S(1)}, u32[]{:S(2)}, u32[]{:S(2)}) collective-permute-start(bf16[64,4096]{1,0:T(8,128)(2,1)S(1)} %fusion.5.h0), channel_id=1, source_target_pairs={{0,8},{4,12},{8,0},{12,4},{1,9},{5,13},{9,1},{13,5},{2,10},{6,14},... | collective-permute-start | bytes 1572872 | tf_op jit(solution)/shard_map/ppermute | solution.py:141
  137.1 11.8 %collective-permute-start.15 = (bf16[64,4096]{1,0:T(8,128)(2,1)S(1)}, bf16[64,4096]{1,0:T(8,128)(2,1)S(1)}, u32[]{:S(2)}, u32[]{:S(2)}) collective-permute-start(bf16[64,4096]{1,0:T(8,128)(2,1)S(1)} %fusion.5.h0), channel_id=1, source_target_pairs={{0,4},{4,0},{8,12},{12,8},{1,5},{5,1},{9,13},{13,9},{2,6},{6,2},{1... | collective-permute-start | bytes 1572872 | tf_op jit(solution)/shard_map/ppermute | solution.py:141
  148.9 1.9 collective-permute-start.17
  160.8 31.6 %all-to-all-start.1 = ((bf16[4,64,2048]{2,1,0:T(8,128)(2,1)}), bf16[4,64,2048]{2,1,0:T(8,128)(2,1)S(1)}, u32[]{:S(2)}, u32[]{:S(2)}) async-start(bf16[4,64,2048]{2,1,0:T(8,128)(2,1)} %get-tuple-element.42), calls=%async_computation.1 | async-start | bytes 2097152 | tf_op jit(solution)/shard_map/all_to_all | solution.py:193
  166.6 43.4 %collective-permute-start.18 = (bf16[64,2048]{1,0:T(8,128)(2,1)S(1)}, bf16[64,2048]{1,0:T(8,128)(2,1)S(1)}, u32[]{:S(2)}, u32[]{:S(2)}) collective-permute-start(bf16[64,2048]{1,0:T(8,128)(2,1)S(1)} %fusion.10), channel_id=1, source_target_pairs={{0,0},{1,4},{2,8},{3,12},{4,1},{5,5},{6,9},{7,13},{8,2},{9,6},{10,... | collective-permute-start | bytes 786440 | tf_op jit(solution)/shard_map/ppermute | solution.py:201
  192.6 22.0 %collective-permute-start.19 = (bf16[64,2048]{1,0:T(8,128)(2,1)S(1)}, bf16[64,2048]{1,0:T(8,128)(2,1)S(1)}, u32[]{:S(2)}, u32[]{:S(2)}) collective-permute-start(bf16[64,2048]{1,0:T(8,128)(2,1)S(1)} %fusion.9), channel_id=1, source_target_pairs={{0,0},{1,4},{2,8},{3,12},{4,1},{5,5},{6,9},{7,13},{8,2},{9,6},{10,... | collective-permute-start | bytes 786440 | tf_op jit(solution)/shard_map/ppermute | solution.py:201

commit v3 on v2

--- a/solution.py
+++ b/solution.py
@@ -14,9 +14,12 @@
 HOLD = True
 AFTER = True
 SPREAD = "p"
-HALVES = (1, 1)
-MIXAT = 1
+HALVES = (1, 2)
+MIXAT = 0
+MODE = ("a", "x")
 TILE2 = 512
+TILE1 = 1024
+HOLD2 = False
 CUBE = (True, True)
 ORDER = 0
 MIX = 0
@@ -57,7 +60,8 @@
         send_ref[1, i] = acc[3 * rows :].astype(BF16)
 
 
-def gate_up(td, blocks, gate_weight, up_weight, tile=512):
+def gate_up(td, blocks, gate_weight, up_weight):
+    tile = TILE1
     rows, depth = blocks[0].shape[-2:]
     units = gate_weight.shape[1]
     whole = [pl.BlockSpec(x.shape, lambda i, td, r=x.ndim: (0,) * r) for x in blocks]
@@ -86,7 +90,8 @@
     )(td, *blocks, gate_weight, up_weight)
 
 
-def down_kernel(tile, td_ref, h0, h1, h2, h3, down_ref, own_ref, full_ref, hs):
+def down_kernel(tile, td_ref, h0, h1, h2, h3, down_ref, own_ref, *refs):
+    outs, hs = refs[:-1], refs[-1]
     rows = h0.shape[0]
 
     @pl.when(pl.program_id(0) == 0)
@@ -98,11 +103,15 @@
     cols = pl.ds(pl.multiple_of(pl.program_id(0) * tile, tile), tile)
     acc = jnp.dot(hs[...], down_ref[:, cols] if RESIDENT else down_ref[...], preferred_element_type=F32)
     own_ref[...] = acc[:rows]
-    for j in range(4):
-        full_ref[j ^ td_ref[1]] = acc[j * rows : (j + 1) * rows].astype(BF16)
-
-
-def down(td, h0, h1, h2, h3, down_weight, part, parts):
+    if len(outs) == 1:
+        for j in range(4):
+            outs[0][j ^ td_ref[1]] = acc[j * rows : (j + 1) * rows].astype(BF16)
+    else:
+        for j in (1, 2, 3):
+            outs[j - 1][...] = acc[j * rows : (j + 1) * rows].astype(BF16)
+
+
+def down(td, h0, h1, h2, h3, down_weight, part, parts, mode):
     rows, depth = h0.shape
     width = down_weight.shape[1] // parts
     tile = TILE2
@@ -116,10 +125,11 @@
             num_scalar_prefetch=1,
             grid=(width // tile,),
             in_specs=[whole] * 4 + [weight],
-            out_specs=[out, pl.BlockSpec((4, rows, tile), lambda i, td: (0, 0, i))],
+            out_specs=[out] + ([pl.BlockSpec((4, rows, tile), lambda i, td: (0, 0, i))] if mode == "a" else [out] * 3),
             scratch_shapes=[pltpu.VMEM((4 * rows, depth), BF16)],
         ),
-        out_shape=[jax.ShapeDtypeStruct((rows, width), F32), jax.ShapeDtypeStruct((4, rows, width), BF16)],
+        out_shape=[jax.ShapeDtypeStruct((rows, width), F32)]
+        + ([jax.ShapeDtypeStruct((4, rows, width), BF16)] if mode == "a" else [jax.ShapeDtypeStruct((rows, width), BF16)] * 3),
         compiler_params=pltpu.CompilerParams(vmem_limit_bytes=(8 if RESIDENT else 40) << 20),
         cost_estimate=pl.CostEstimate(
             flops=COST2 * 1000,
@@ -176,7 +186,10 @@
     def add(c):
         x, _ = lax.optimization_barrier((keep[c], tuple(tick)))
         keep[c] = x
-        summed = (x[1] + near[c][1].astype(F32)).astype(BF16)
+        side = near[c][1]
+        if HOLD2 and c == 0:
+            side = after(side, blocks[1][3])
+        summed = (x[1] + side.astype(F32)).astype(BF16)
         across[c] = swap(summed, "dp", 2)
         tick[:] = [summed]
 
@@ -189,14 +202,18 @@
         tick[:] = [hidden[c]]
 
     def second(c, h):
-        parts[c, h] = down(after(dt, *tick), hidden[c], pair[c][0], far[c], pair[c][1], down_weight, h, HALVES[c])
-        got[c, h] = lax.all_to_all(parts[c, h][1], "tensor", 0, 0, tiled=True)
+        parts[c, h] = down(after(dt, *tick), hidden[c], pair[c][0], far[c], pair[c][1], down_weight, h, HALVES[c], MODE[c])
+        if MODE[c] == "a":
+            got[c, h] = lax.all_to_all(parts[c, h][1], "tensor", 0, 0, tiled=True)
+        else:
+            got[c, h] = [swap(parts[c, h][j], "tensor", j) for j in (1, 2, 3)]
         tick[:] = [parts[c, h][1]]
 
     def mix(c, h):
         mixed, _ = lax.optimization_barrier((parts[c, h][0], tuple(tick)))
-        for j in range(4):
-            mixed = mixed + jnp.where(t == j, 0.0, got[c, h][j].astype(F32))
+        for j in range(len(got[c, h]) if MODE[c] == "x" else 4):
+            g = got[c, h][j].astype(F32)
+            mixed = mixed + (g if MODE[c] == "x" else jnp.where(t == j, 0.0, g))
         mixed = mixed.astype(BF16)
         outs[c, h] = lax.ppermute(mixed, ("dp", "tensor"), turn)
         tick[:] = [mixed]

time: 216 us -> 206 us (0.954)
  waiting for transfers between devices: 102 us -> 85.3 us
  starting transfers between devices: 52.9 us -> 60.9 us
    all_to_all x2 -> x1, waiting for transfers between devices: 21.2 us -> 0.01 us  [second(): got[c, h] = lax.all_to_all(parts[c, h][1], 'tensor', 0, 0, tiled=True)]
    ppermute x16 -> x22, waiting for transfers between devices: 47.3 us -> 57.5 us  [per_device(): swap = lambda x, axis, mask: lax.ppermute(x, axis, xor_perm(4, mask))]
    ppermute x16 -> x22, starting transfers between devices: 23.6 us -> 32 us  [per_device(): swap = lambda x, axis, mask: lax.ppermute(x, axis, xor_perm(4, mask))]
    all_to_all x2 -> x1, starting transfers between devices: 10.5 us -> 4.24 us  [second(): got[c, h] = lax.all_to_all(parts[c, h][1], 'tensor', 0, 0, tiled=True)]
    ppermute x2 -> x3, waiting for transfers between devices: 14.1 us -> 8.2 us  [mix(): outs[c, h] = lax.ppermute(mixed, ('dp', 'tensor'), turn)]
    ppermute x2 -> x3, starting transfers between devices: 12.5 us -> 18.2 us  [mix(): outs[c, h] = lax.ppermute(mixed, ('dp', 'tensor'), turn)]
    pallas_call x2, Pallas kernels: 32.1 us -> 29.1 us  [gate_up(): pl.pallas_call(functools.partial(gate_up_kernel, tile), grid_spec=pltpu.P...]
    pallas_call x2 -> x3, Pallas kernels: 20 us -> 20.9 us  [down(): pl.pallas_call(functools.partial(down_kernel, tile), grid_spec=pltpu.Pref...]
  transfers between devices with their start and end apart: 22 -> 28, of which waited for: 16 -> 17; matrix products, arithmetic and copies ran while one was open for 2% -> 3% of each run, Pallas kernels for 24% -> 24%
where the time goes in v3:
time: 206 us
  waiting for transfers between devices  85.3 us (41%)
  starting transfers between devices  60.9 us (30%)
  Pallas kernels  50 us (24%)
  other arithmetic  7.79 us (4%)
    ppermute x22, waiting for transfers between devices, per_device(): swap = lambda x, axis, mask: lax.ppermute(x, axis, xor_perm(4, mask))  57.5 us
    ppermute x22, starting transfers between devices, per_device(): swap = lambda x, axis, mask: lax.ppermute(x, axis, xor_perm(4, mask))  32 us
    pallas_call x2, Pallas kernels, gate_up(): pl.pallas_call(functools.partial(gate_up_kernel, tile), grid_spec=pltpu.P...  29.1 us
    pallas_call x3, Pallas kernels, down(): pl.pallas_call(functools.partial(down_kernel, tile), grid_spec=pltpu.Pref...  20.9 us
    ppermute x2, waiting for transfers between devices, turn_in(): mine[c] = lax.ppermute(x, ('dp', 'tensor'), turn)  19.7 us
    ppermute x3, starting transfers between devices, mix(): outs[c, h] = lax.ppermute(mixed, ('dp', 'tensor'), turn)  18.2 us
    ppermute x3, waiting for transfers between devices, mix(): outs[c, h] = lax.ppermute(mixed, ('dp', 'tensor'), turn)  8.2 us
    ppermute x2, starting transfers between devices, turn_in(): mine[c] = lax.ppermute(x, ('dp', 'tensor'), turn)  6.38 us
  transfers between devices with their start and end apart: 28, of which 17 were waited for; matrix products, arithmetic and copies ran while one was open for 3% of the time, Pallas kernels for 24%

profile of v3, /device:TPU:2, one launch (start us, length us, event | category | flops | bytes accessed | tf_op | source)
XLA Modules:
  0.0 206.0 jit_solution(18400663797033821016)
XLA Ops:
  1.1 4.5 %collective-permute-start = (bf16[64,2048]{1,0:T(8,128)(2,1)S(1)}, bf16[64,2048]{1,0:T(8,128)(2,1)S(1)}, u32[]{:S(2)}, u32[]{:S(2)}) collective-permute-start(bf16[64,2048]{1,0:T(8,128)(2,1)S(1)} %get-tuple-element.62), channel_id=1, source_target_pairs={{0,0},{1,4},{2,8},{3,12},{4,1},{5,5},{6,9},{7,13},{8,2},{9,6},{10,... | collective-permute-start | bytes 786440 | tf_op jit(solution)/shard_map/ppermute | solution.py:162
  5.5 13.6 %collective-permute-done.refs_0_ = bf16[64,2048]{1,0:T(8,128)(2,1)S(1)} collective-permute-done((bf16[64,2048]{1,0:T(8,128)(2,1)S(1)}, bf16[64,2048]{1,0:T(8,128)(2,1)S(1)}, u32[]{:S(2)}, u32[]{:S(2)}) %collective-permute-start) | collective-permute-done | bytes 262176 | tf_op jit(solution)/shard_map/ppermute | solution.py:162
  19.1 1.9 collective-permute-start.1
  21.0 4.3 %collective-permute-start.2 = (bf16[64,2048]{1,0:T(8,128)(2,1)S(1)}, bf16[64,2048]{1,0:T(8,128)(2,1)S(1)}, u32[]{:S(2)}, u32[]{:S(2)}) collective-permute-start(bf16[64,2048]{1,0:T(8,128)(2,1)S(1)} %collective-permute-done.refs_0_), channel_id=1, source_target_pairs={{0,1},{1,0},{2,3},{3,2},{4,5},{5,4},{6,7},{7,6},{8,9},{9,8},{10,11... | collective-permute-start | bytes 786440 | tf_op jit(solution)/shard_map/ppermute | solution.py:151
  25.4 6.7 %collective-permute-done.3.refs_2_ = bf16[64,2048]{1,0:T(8,128)(2,1)S(1)} collective-permute-done((bf16[64,2048]{1,0:T(8,128)(2,1)S(1)}, bf16[64,2048]{1,0:T(8,128)(2,1)S(1)}, u32[]{:S(2)}, u32[]{:S(2)}) %collective-permute-start.3) | collective-permute-done | bytes 262176 | tf_op jit(solution)/shard_map/ppermute | solution.py:151
  32.1 3.4 %collective-permute-start.4 = (bf16[64,2048]{1,0:T(8,128)(2,1)S(1)}, bf16[64,2048]{1,0:T(8,128)(2,1)S(1)}, u32[]{:S(2)}, u32[]{:S(2)}) collective-permute-start(bf16[64,2048]{1,0:T(8,128)(2,1)S(1)} %collective-permute-done.3.refs_2_), channel_id=1, source_target_pairs={{0,1},{1,0},{2,3},{3,2},{4,5},{5,4},{6,7},{7,6},{8,9},{9,8},{10,11... | collective-permute-start | bytes 786440 | tf_op jit(solution)/shard_map/ppermute | solution.py:151
  35.5 6.1 %collective-permute-done.1.refs_0_ = bf16[64,2048]{1,0:T(8,128)(2,1)S(1)} collective-permute-done((bf16[64,2048]{1,0:T(8,128)(2,1)S(1)}, bf16[64,2048]{1,0:T(8,128)(2,1)S(1)}, u32[]{:S(2)}, u32[]{:S(2)}) %collective-permute-start.1) | collective-permute-done | bytes 262176 | tf_op jit(solution)/shard_map/ppermute | solution.py:162
  41.6 1.7 collective-permute-start.5
  43.4 5.6 %collective-permute-start.6 = (bf16[64,2048]{1,0:T(8,128)(2,1)S(1)}, bf16[64,2048]{1,0:T(8,128)(2,1)S(1)}, u32[]{:S(2)}, u32[]{:S(2)}) collective-permute-start(bf16[64,2048]{1,0:T(8,128)(2,1)S(1)} %collective-permute-done.1.refs_0_), channel_id=1, source_target_pairs={{0,2},{1,3},{2,0},{3,1},{4,6},{5,7},{6,4},{7,5},{8,10},{9,11},{10,... | collective-permute-start | bytes 786440 | tf_op jit(solution)/shard_map/ppermute | solution.py:151
  48.9 14.6 %gate_up.2 = (f32[2,2,64,4096]{3,2,1,0:T(8,128)S(1)}, bf16[2,2,64,4096]{3,2,1,0:T(8,128)(2,1)S(1)}) custom-call(s32[1]{0:T(128)} %bitcast.td_ref, bf16[64,2048]{1,0:T(8,128)(2,1)S(1)} %collective-permute-done.refs_0_, bf16[64,2048]{1,0:T(8,128)(2,1)S(1)} %collective-permute-done.2.refs_1_, bf16[64,2048]{1,0:T(8,128)(2,1)S(1)} %collective-permute-done.3.refs_2_, ...), custom_call_target="tpu_custom_call" | custom-call | flops 20000000 | bytes 20000000 | tf_op jit(solution)/shard_map/gate_up/pallas_call | solution.py:70
  65.2 3.8 %collective-permute-done.7 = bf16[2,2,64,4096]{3,2,1,0:T(8,128)(2,1)S(1)} collective-permute-done((bf16[2,2,64,4096]{3,2,1,0:T(8,128)(2,1)S(1)}, bf16[2,2,64,4096]{3,2,1,0:T(8,128)(2,1)S(1)}, u32[]{:S(2)}, u32[]{:S(2)}) %collective-permute-start.7) | collective-permute-done | bytes 2097184 | tf_op jit(solution)/shard_map/ppermute | solution.py:151
  69.8 2.0 collective-permute-start.8
  72.6 5.5 %collective-permute-done.8.refs_3_ = bf16[64,2048]{1,0:T(8,128)(2,1)S(1)} collective-permute-done((bf16[64,2048]{1,0:T(8,128)(2,1)S(1)}, bf16[64,2048]{1,0:T(8,128)(2,1)S(1)}, u32[]{:S(2)}, u32[]{:S(2)}) %collective-permute-start.8) | collective-permute-done | bytes 262176 | tf_op jit(solution)/shard_map/ppermute | solution.py:151
  78.1 14.6 %gate_up.3 = (f32[2,2,64,4096]{3,2,1,0:T(8,128)S(1)}, bf16[2,2,64,4096]{3,2,1,0:T(8,128)(2,1)S(1)}) custom-call(s32[1]{0:T(128)} %bitcast.td_ref, bf16[64,2048]{1,0:T(8,128)(2,1)S(1)} %collective-permute-done.1.refs_0_, bf16[64,2048]{1,0:T(8,128)(2,1)S(1)} %collective-permute-done.5.refs_1_, bf16[64,2048]{1,0:T(8,128)(2,1)S(1)} %collective-permute-done.6.refs_2_, ...), custom_call_target="tpu_custom_call" | custom-call | flops 20000000 | bytes 20000000 | tf_op jit(solution)/shard_map/gate_up/pallas_call | solution.py:70
  92.8 1.9 collective-permute-done.9
  99.7 10.4 %collective-permute-done.12.h2 = bf16[64,4096]{1,0:T(8,128)(2,1)S(1)} collective-permute-done((bf16[64,4096]{1,0:T(8,128)(2,1)S(1)}, bf16[64,4096]{1,0:T(8,128)(2,1)S(1)}, u32[]{:S(2)}, u32[]{:S(2)}) %collective-permute-start.12) | collective-permute-done | bytes 524320 | tf_op jit(solution)/shard_map/ppermute | solution.py:151
  110.2 1.8 collective-permute-done.13.h3
  112.0 10.0 %down.3 = (f32[64,2048]{1,0:T(8,128)S(1)}, bf16[4,64,2048]{2,1,0:T(8,128)(2,1)}) custom-call(s32[2]{0:T(128)S(1)} %pad_add_fusion.td_ref, bf16[64,4096]{1,0:T(8,128)(2,1)S(1)} %fusion.8.h0, bf16[64,4096]{1,0:T(8,128)(2,1)S(1)} %collective-permute-done.11.h1, bf16[64,4096]{1,0:T(8,128)(2,1)S(1)} %collective-permute-done.12.h2, ...), custom_call_target="tpu_custom_call" | custom-call | flops 1000000 | bytes 1000000 | tf_op jit(solution)/shard_map/down/pallas_call | solution.py:122
  122.0 4.2 %all-to-all-start = ((bf16[4,64,2048]{2,1,0:T(8,128)(2,1)}), bf16[4,64,2048]{2,1,0:T(8,128)(2,1)}, u32[]{:S(2)}, u32[]{:S(2)}) async-start(bf16[4,64,2048]{2,1,0:T(8,128)(2,1)} %get-tuple-element.47), calls=%async_computation | async-start | bytes 2097152 | tf_op jit(solution)/shard_map/all_to_all | solution.py:207
  126.2 5.0 %collective-permute-done.14 = bf16[2,64,4096]{2,1,0:T(8,128)(2,1)} collective-permute-done((bf16[2,64,4096]{2,1,0:T(8,128)(2,1)}, bf16[2,64,4096]{2,1,0:T(8,128)(2,1)}, u32[]{:S(2)}, u32[]{:S(2)}) %collective-permute-start.14) | collective-permute-done | bytes 1048608 | tf_op jit(solution)/shard_map/ppermute | solution.py:151
  131.2 2.2 %bitcast_add_fusion = f32[2,64,4096]{2,1,0:T(8,128)S(1)} fusion(bf16[2,64,4096]{2,1,0:T(8,128)(2,1)} %collective-permute-done.14, f32[2,2,64,4096]{3,2,1,0:T(8,128)} %copy-done, bf16[2,2,64,4096]{3,2,1,0:T(8,128)(2,1)S(1)} %collective-permute-done.10), kind=kLoop, calls=%fused_computation.2 | loop fusion | flops 2097152 | bytes 6291456 | tf_op jit(solution)/shard_map/add | solution.py:198
  134.2 11.9 %collective-permute-done.16.h2 = bf16[64,4096]{1,0:T(8,128)(2,1)S(1)} collective-permute-done((bf16[64,4096]{1,0:T(8,128)(2,1)S(1)}, bf16[64,4096]{1,0:T(8,128)(2,1)S(1)}, u32[]{:S(2)}, u32[]{:S(2)}) %collective-permute-start.16) | collective-permute-done | bytes 524320 | tf_op jit(solution)/shard_map/ppermute | solution.py:151
  146.1 1.9 collective-permute-done.17.h3
  148.0 5.4 %down.4 = (f32[64,1024]{1,0:T(8,128)S(1)}, bf16[64,1024]{1,0:T(8,128)(2,1)S(1)}, bf16[64,1024]{1,0:T(8,128)(2,1)S(1)}, bf16[64,1024]{1,0:T(8,128)(2,1)S(1)}) custom-call(s32[2]{0:T(128)S(1)} %pad_add_fusion.td_ref, bf16[64,4096]{1,0:T(8,128)(2,1)S(1)} %fusion.5.h0, bf16[64,4096]{1,0:T(8,128)(2,1)S(1)} %collective-permute-done.15.h1, ...), custom_call_target="tpu_custom_call" | custom-call | flops 1000000 | bytes 1000000 | tf_op jit(solution)/shard_map/down/pallas_call | solution.py:122
  154.7 3.0 %collective-permute-start.21 = (bf16[64,1024]{1,0:T(8,128)(2,1)S(1)}, bf16[64,1024]{1,0:T(8,128)(2,1)S(1)}, u32[]{:S(2)}, u32[]{:S(2)}) collective-permute-start(bf16[64,1024]{1,0:T(8,128)(2,1)S(1)} %get-tuple-element.57), channel_id=1, source_target_pairs={{0,3},{1,2},{2,1},{3,0},{4,7},{5,6},{6,5},{7,4},{8,11},{9,10},{10,... | collective-permute-start | bytes 393224 | tf_op jit(solution)/shard_map/ppermute | solution.py:151
  159.1 4.6 %collective-permute-start.18 = (bf16[64,2048]{1,0:T(8,128)(2,1)S(1)}, bf16[64,2048]{1,0:T(8,128)(2,1)S(1)}, u32[]{:S(2)}, u32[]{:S(2)}) collective-permute-start(bf16[64,2048]{1,0:T(8,128)(2,1)S(1)} %fusion.9), channel_id=1, source_target_pairs={{0,0},{1,4},{2,8},{3,12},{4,1},{5,5},{6,9},{7,13},{8,2},{9,6},{10,... | collective-permute-start | bytes 786440 | tf_op jit(solution)/shard_map/ppermute | solution.py:218
  163.6 5.5 %down.5 = (f32[64,1024]{1,0:T(8,128)S(1)}, bf16[64,1024]{1,0:T(8,128)(2,1)S(1)}, bf16[64,1024]{1,0:T(8,128)(2,1)S(1)}, bf16[64,1024]{1,0:T(8,128)(2,1)S(1)}) custom-call(s32[2]{0:T(128)S(1)} %pad_add_fusion.td_ref, bf16[64,4096]{1,0:T(8,128)(2,1)S(1)} %fusion.5.h0, bf16[64,4096]{1,0:T(8,128)(2,1)S(1)} %collective-permute-done.15.h1, ...), custom_call_target="tpu_custom_call" | custom-call | flops 1000000 | bytes 1000000 | tf_op jit(solution)/shard_map/down/pallas_call | solution.py:122
  169.9 5.3 %collective-permute-start.24 = (bf16[64,1024]{1,0:T(8,128)(2,1)S(1)}, bf16[64,1024]{1,0:T(8,128)(2,1)S(1)}, u32[]{:S(2)}, u32[]{:S(2)}) collective-permute-start(bf16[64,1024]{1,0:T(8,128)(2,1)S(1)} %get-tuple-element.60), channel_id=1, source_target_pairs={{0,2},{1,3},{2,0},{3,1},{4,6},{5,7},{6,4},{7,5},{8,10},{9,11},{10,... | collective-permute-start | bytes 393224 | tf_op jit(solution)/shard_map/ppermute | solution.py:151
  177.1 6.1 %collective-permute-done.24 = bf16[64,1024]{1,0:T(8,128)(2,1)S(1)} collective-permute-done((bf16[64,1024]{1,0:T(8,128)(2,1)S(1)}, bf16[64,1024]{1,0:T(8,128)(2,1)S(1)}, u32[]{:S(2)}, u32[]{:S(2)}) %collective-permute-start.24) | collective-permute-done | bytes 131104 | tf_op jit(solution)/shard_map/ppermute | solution.py:151
  183.3 11.8 %collective-permute-start.26 = (bf16[64,1024]{1,0:T(8,128)(2,1)S(1)}, bf16[64,1024]{1,0:T(8,128)(2,1)S(1)}, u32[]{:S(2)}, u32[]{:S(2)}) collective-permute-start(bf16[64,1024]{1,0:T(8,128)(2,1)S(1)} %add_convert_fusion.1), channel_id=1, source_target_pairs={{0,0},{1,4},{2,8},{3,12},{4,1},{5,5},{6,9},{7,13},{8,2},{9,6},{10,... | collective-permute-start | bytes 393224 | tf_op jit(solution)/shard_map/ppermute | solution.py:218
  195.0 1.9 collective-permute-start.22
  198.0 7.2 %collective-permute-done.22 = bf16[64,1024]{1,0:T(8,128)(2,1)S(1)} collective-permute-done((bf16[64,1024]{1,0:T(8,128)(2,1)S(1)}, bf16[64,1024]{1,0:T(8,128)(2,1)S(1)}, u32[]{:S(2)}, u32[]{:S(2)}) %collective-permute-start.22) | collective-permute-done | bytes 131104 | tf_op jit(solution)/shard_map/ppermute | solution.py:218
  (50 shorter events, 16.9 us)
Async XLA Ops:
  1.1 18.0 %collective-permute-start = (bf16[64,2048]{1,0:T(8,128)(2,1)S(1)}, bf16[64,2048]{1,0:T(8,128)(2,1)S(1)}, u32[]{:S(2)}, u32[]{:S(2)}) collective-permute-start(bf16[64,2048]{1,0:T(8,128)(2,1)S(1)} %get-tuple-element.62), channel_id=1, source_target_pairs={{0,0},{1,4},{2,8},{3,12},{4,1},{5,5},{6,9},{7,13},{8,2},{9,6},{10,... | collective-permute-start | bytes 786440 | tf_op jit(solution)/shard_map/ppermute | solution.py:162
  19.1 13.0 %collective-permute-start.3 = (bf16[64,2048]{1,0:T(8,128)(2,1)S(1)}, bf16[64,2048]{1,0:T(8,128)(2,1)S(1)}, u32[]{:S(2)}, u32[]{:S(2)}) collective-permute-start(bf16[64,2048]{1,0:T(8,128)(2,1)S(1)} %collective-permute-done.refs_0_), channel_id=1, source_target_pairs={{0,2},{1,3},{2,0},{3,1},{4,6},{5,7},{6,4},{7,5},{8,10},{9,11},{10,... | collective-permute-start | bytes 786440 | tf_op jit(solution)/shard_map/ppermute | solution.py:151
  19.1 22.5 %collective-permute-start.1 = (bf16[64,2048]{1,0:T(8,128)(2,1)S(1)}, bf16[64,2048]{1,0:T(8,128)(2,1)S(1)}, u32[]{:S(2)}, u32[]{:S(2)}) collective-permute-start(bf16[64,2048]{1,0:T(8,128)(2,1)S(1)} %get-tuple-element.34), channel_id=1, source_target_pairs={{0,0},{1,4},{2,8},{3,12},{4,1},{5,5},{6,9},{7,13},{8,2},{9,6},{10,... | collective-permute-start | bytes 786440 | tf_op jit(solution)/shard_map/ppermute | solution.py:162
  21.0 20.5 %collective-permute-start.2 = (bf16[64,2048]{1,0:T(8,128)(2,1)S(1)}, bf16[64,2048]{1,0:T(8,128)(2,1)S(1)}, u32[]{:S(2)}, u32[]{:S(2)}) collective-permute-start(bf16[64,2048]{1,0:T(8,128)(2,1)S(1)} %collective-permute-done.refs_0_), channel_id=1, source_target_pairs={{0,1},{1,0},{2,3},{3,2},{4,5},{5,4},{6,7},{7,6},{8,9},{9,8},{10,11... | collective-permute-start | bytes 786440 | tf_op jit(solution)/shard_map/ppermute | solution.py:151
  32.1 9.5 %collective-permute-start.4 = (bf16[64,2048]{1,0:T(8,128)(2,1)S(1)}, bf16[64,2048]{1,0:T(8,128)(2,1)S(1)}, u32[]{:S(2)}, u32[]{:S(2)}) collective-permute-start(bf16[64,2048]{1,0:T(8,128)(2,1)S(1)} %collective-permute-done.3.refs_2_), channel_id=1, source_target_pairs={{0,1},{1,0},{2,3},{3,2},{4,5},{5,4},{6,7},{7,6},{8,9},{9,8},{10,11... | collective-permute-start | bytes 786440 | tf_op jit(solution)/shard_map/ppermute | solution.py:151
  41.6 21.9 %collective-permute-start.5 = (bf16[64,2048]{1,0:T(8,128)(2,1)S(1)}, bf16[64,2048]{1,0:T(8,128)(2,1)S(1)}, u32[]{:S(2)}, u32[]{:S(2)}) collective-permute-start(bf16[64,2048]{1,0:T(8,128)(2,1)S(1)} %collective-permute-done.1.refs_0_), channel_id=1, source_target_pairs={{0,1},{1,0},{2,3},{3,2},{4,5},{5,4},{6,7},{7,6},{8,9},{9,8},{10,11... | collective-permute-start | bytes 786440 | tf_op jit(solution)/shard_map/ppermute | solution.py:151
  43.4 20.1 %collective-permute-start.6 = (bf16[64,2048]{1,0:T(8,128)(2,1)S(1)}, bf16[64,2048]{1,0:T(8,128)(2,1)S(1)}, u32[]{:S(2)}, u32[]{:S(2)}) collective-permute-start(bf16[64,2048]{1,0:T(8,128)(2,1)S(1)} %collective-permute-done.1.refs_0_), channel_id=1, source_target_pairs={{0,2},{1,3},{2,0},{3,1},{4,6},{5,7},{6,4},{7,5},{8,10},{9,11},{10,... | collective-permute-start | bytes 786440 | tf_op jit(solution)/shard_map/ppermute | solution.py:151
  63.5 5.5 %collective-permute-start.7 = (bf16[2,2,64,4096]{3,2,1,0:T(8,128)(2,1)S(1)}, bf16[2,2,64,4096]{3,2,1,0:T(8,128)(2,1)S(1)}, u32[]{:S(2)}, u32[]{:S(2)}) collective-permute-start(bf16[2,2,64,4096]{3,2,1,0:T(8,128)(2,1)S(1)} %get-tuple-element.39), channel_id=1, source_target_pairs={{0,4},{4,0},{8,12},{12,8},{1,5},{5,1},{9,13},{13,9},{2,6},{6,2},{1... | collective-permute-start | bytes 6291464 | tf_op jit(solution)/shard_map/ppermute | solution.py:151
  65.2 6.6 %copy-start.1 = (s32[32]{0:T(128)S(1)}, s32[32]{0:T(128)}, u32[]{:S(2)}) copy-start(s32[32]{0:T(128)} %param.10) | copy-start | bytes 388
  69.2 25.5 %collective-permute-start.9 = (bf16[2,64,4096]{2,1,0:T(8,128)(2,1)S(1)}, bf16[2,64,4096]{2,1,0:T(8,128)(2,1)S(1)}, u32[]{:S(2)}, u32[]{:S(2)}) collective-permute-start(bf16[2,64,4096]{2,1,0:T(8,128)(2,1)S(1)} %fusion.2), channel_id=1, source_target_pairs={{0,8},{4,12},{8,0},{12,4},{1,9},{5,13},{9,1},{13,5},{2,10},{6,14},... | collective-permute-start | bytes 3145736 | tf_op jit(solution)/shard_map/ppermute | solution.py:151
  69.8 8.3 %collective-permute-start.8 = (bf16[64,2048]{1,0:T(8,128)(2,1)S(1)}, bf16[64,2048]{1,0:T(8,128)(2,1)S(1)}, u32[]{:S(2)}, u32[]{:S(2)}) collective-permute-start(bf16[64,2048]{1,0:T(8,128)(2,1)S(1)} %collective-permute-done.6.refs_2_), channel_id=1, source_target_pairs={{0,1},{1,0},{2,3},{3,2},{4,5},{5,4},{6,7},{7,6},{8,9},{9,8},{10,11... | collective-permute-start | bytes 786440 | tf_op jit(solution)/shard_map/ppermute | solution.py:151
  92.7 4.2 %copy-start = (f32[2,2,64,4096]{3,2,1,0:T(8,128)}, f32[2,2,64,4096]{3,2,1,0:T(8,128)S(1)}, u32[]{:S(2)}) copy-start(f32[2,2,64,4096]{3,2,1,0:T(8,128)S(1)} %get-tuple-element.48) | copy-start | bytes 12582916
  92.7 4.2 %collective-permute-start.10 = (bf16[2,2,64,4096]{3,2,1,0:T(8,128)(2,1)S(1)}, bf16[2,2,64,4096]{3,2,1,0:T(8,128)(2,1)S(1)}, u32[]{:S(2)}, u32[]{:S(2)}) collective-permute-start(bf16[2,2,64,4096]{3,2,1,0:T(8,128)(2,1)S(1)} %get-tuple-element.42), channel_id=1, source_target_pairs={{0,4},{4,0},{8,12},{12,8},{1,5},{5,1},{9,13},{13,9},{2,6},{6,2},{1... | collective-permute-start | bytes 6291464 | tf_op jit(solution)/shard_map/ppermute | solution.py:151
  95.2 14.9 %collective-permute-start.12 = (bf16[64,4096]{1,0:T(8,128)(2,1)S(1)}, bf16[64,4096]{1,0:T(8,128)(2,1)S(1)}, u32[]{:S(2)}, u32[]{:S(2)}) collective-permute-start(bf16[64,4096]{1,0:T(8,128)(2,1)S(1)} %fusion.8.h0), channel_id=1, source_target_pairs={{0,8},{4,12},{8,0},{12,4},{1,9},{5,13},{9,1},{13,5},{2,10},{6,14},... | collective-permute-start | bytes 1572872 | tf_op jit(solution)/shard_map/ppermute | solution.py:151
  98.2 33.0 %collective-permute-start.14 = (bf16[2,64,4096]{2,1,0:T(8,128)(2,1)}, bf16[2,64,4096]{2,1,0:T(8,128)(2,1)}, u32[]{:S(2)}, u32[]{:S(2)}) collective-permute-start(bf16[2,64,4096]{2,1,0:T(8,128)(2,1)} %fusion.1), channel_id=1, source_target_pairs={{0,8},{4,12},{8,0},{12,4},{1,9},{5,13},{9,1},{13,5},{2,10},{6,14},... | collective-permute-start | bytes 3145736 | tf_op jit(solution)/shard_map/ppermute | solution.py:151
  99.7 10.5 %collective-permute-start.11 = (bf16[64,4096]{1,0:T(8,128)(2,1)S(1)}, bf16[64,4096]{1,0:T(8,128)(2,1)S(1)}, u32[]{:S(2)}, u32[]{:S(2)}) collective-permute-start(bf16[64,4096]{1,0:T(8,128)(2,1)S(1)} %fusion.8.h0), channel_id=1, source_target_pairs={{0,4},{4,0},{8,12},{12,8},{1,5},{5,1},{9,13},{13,9},{2,6},{6,2},{1... | collective-permute-start | bytes 1572872 | tf_op jit(solution)/shard_map/ppermute | solution.py:151
  110.1 1.9 collective-permute-start.13
  122.0 35.6 %all-to-all-start = ((bf16[4,64,2048]{2,1,0:T(8,128)(2,1)}), bf16[4,64,2048]{2,1,0:T(8,128)(2,1)}, u32[]{:S(2)}, u32[]{:S(2)}) async-start(bf16[4,64,2048]{2,1,0:T(8,128)(2,1)} %get-tuple-element.47), calls=%async_computation | async-start | bytes 2097152 | tf_op jit(solution)/shard_map/all_to_all | solution.py:207
  133.6 12.5 %collective-permute-start.16 = (bf16[64,4096]{1,0:T(8,128)(2,1)S(1)}, bf16[64,4096]{1,0:T(8,128)(2,1)S(1)}, u32[]{:S(2)}, u32[]{:S(2)}) collective-permute-start(bf16[64,4096]{1,0:T(8,128)(2,1)S(1)} %fusion.5.h0), channel_id=1, source_target_pairs={{0,8},{4,12},{8,0},{12,4},{1,9},{5,13},{9,1},{13,5},{2,10},{6,14},... | collective-permute-start | bytes 1572872 | tf_op jit(solution)/shard_map/ppermute | solution.py:151
  134.2 11.9 %collective-permute-start.15 = (bf16[64,4096]{1,0:T(8,128)(2,1)S(1)}, bf16[64,4096]{1,0:T(8,128)(2,1)S(1)}, u32[]{:S(2)}, u32[]{:S(2)}) collective-permute-start(bf16[64,4096]{1,0:T(8,128)(2,1)S(1)} %fusion.5.h0), channel_id=1, source_target_pairs={{0,4},{4,0},{8,12},{12,8},{1,5},{5,1},{9,13},{13,9},{2,6},{6,2},{1... | collective-permute-start | bytes 1572872 | tf_op jit(solution)/shard_map/ppermute | solution.py:151
  146.1 1.9 collective-permute-start.17
  153.5 21.7 %collective-permute-start.19 = (bf16[64,1024]{1,0:T(8,128)(2,1)S(1)}, bf16[64,1024]{1,0:T(8,128)(2,1)S(1)}, u32[]{:S(2)}, u32[]{:S(2)}) collective-permute-start(bf16[64,1024]{1,0:T(8,128)(2,1)S(1)} %get-tuple-element.50), channel_id=1, source_target_pairs={{0,1},{1,0},{2,3},{3,2},{4,5},{5,4},{6,7},{7,6},{8,9},{9,8},{10,11... | collective-permute-start | bytes 393224 | tf_op jit(solution)/shard_map/ppermute | solution.py:151
  154.7 14.5 %collective-permute-start.21 = (bf16[64,1024]{1,0:T(8,128)(2,1)S(1)}, bf16[64,1024]{1,0:T(8,128)(2,1)S(1)}, u32[]{:S(2)}, u32[]{:S(2)}) collective-permute-start(bf16[64,1024]{1,0:T(8,128)(2,1)S(1)} %get-tuple-element.57), channel_id=1, source_target_pairs={{0,3},{1,2},{2,1},{3,0},{4,7},{5,6},{6,5},{7,4},{8,11},{9,10},{10,... | collective-permute-start | bytes 393224 | tf_op jit(solution)/shard_map/ppermute | solution.py:151
  157.6 12.2 %collective-permute-start.20 = (bf16[64,1024]{1,0:T(8,128)(2,1)S(1)}, bf16[64,1024]{1,0:T(8,128)(2,1)}, u32[]{:S(2)}, u32[]{:S(2)}) collective-permute-start(bf16[64,1024]{1,0:T(8,128)(2,1)S(1)} %get-tuple-element.56), channel_id=1, source_target_pairs={{0,2},{1,3},{2,0},{3,1},{4,6},{5,7},{6,4},{7,5},{8,10},{9,11},{10,... | collective-permute-start | bytes 393224 | tf_op jit(solution)/shard_map/ppermute | solution.py:151
  159.1 46.1 %collective-permute-start.18 = (bf16[64,2048]{1,0:T(8,128)(2,1)S(1)}, bf16[64,2048]{1,0:T(8,128)(2,1)S(1)}, u32[]{:S(2)}, u32[]{:S(2)}) collective-permute-start(bf16[64,2048]{1,0:T(8,128)(2,1)S(1)} %fusion.9), channel_id=1, source_target_pairs={{0,0},{1,4},{2,8},{3,12},{4,1},{5,5},{6,9},{7,13},{8,2},{9,6},{10,... | collective-permute-start | bytes 786440 | tf_op jit(solution)/shard_map/ppermute | solution.py:218
  169.1 14.1 %collective-permute-start.23 = (bf16[64,1024]{1,0:T(8,128)(2,1)S(1)}, bf16[64,1024]{1,0:T(8,128)(2,1)S(1)}, u32[]{:S(2)}, u32[]{:S(2)}) collective-permute-start(bf16[64,1024]{1,0:T(8,128)(2,1)S(1)} %get-tuple-element.54), channel_id=1, source_target_pairs={{0,1},{1,0},{2,3},{3,2},{4,5},{5,4},{6,7},{7,6},{8,9},{9,8},{10,11... | collective-permute-start | bytes 393224 | tf_op jit(solution)/shard_map/ppermute | solution.py:151
  169.2 7.9 %collective-permute-start.25 = (bf16[64,1024]{1,0:T(8,128)(2,1)S(1)}, bf16[64,1024]{1,0:T(8,128)(2,1)S(1)}, u32[]{:S(2)}, u32[]{:S(2)}) collective-permute-start(bf16[64,1024]{1,0:T(8,128)(2,1)S(1)} %get-tuple-element.61), channel_id=1, source_target_pairs={{0,3},{1,2},{2,1},{3,0},{4,7},{5,6},{6,5},{7,4},{8,11},{9,10},{10,... | collective-permute-start | bytes 393224 | tf_op jit(solution)/shard_map/ppermute | solution.py:151
  169.9 13.3 %collective-permute-start.24 = (bf16[64,1024]{1,0:T(8,128)(2,1)S(1)}, bf16[64,1024]{1,0:T(8,128)(2,1)S(1)}, u32[]{:S(2)}, u32[]{:S(2)}) collective-permute-start(bf16[64,1024]{1,0:T(8,128)(2,1)S(1)} %get-tuple-element.60), channel_id=1, source_target_pairs={{0,2},{1,3},{2,0},{3,1},{4,6},{5,7},{6,4},{7,5},{8,10},{9,11},{10,... | collective-permute-start | bytes 393224 | tf_op jit(solution)/shard_map/ppermute | solution.py:151
  183.3 14.7 %collective-permute-start.26 = (bf16[64,1024]{1,0:T(8,128)(2,1)S(1)}, bf16[64,1024]{1,0:T(8,128)(2,1)S(1)}, u32[]{:S(2)}, u32[]{:S(2)}) collective-permute-start(bf16[64,1024]{1,0:T(8,128)(2,1)S(1)} %add_convert_fusion.1), channel_id=1, source_target_pairs={{0,0},{1,4},{2,8},{3,12},{4,1},{5,5},{6,9},{7,13},{8,2},{9,6},{10,... | collective-permute-start | bytes 393224 | tf_op jit(solution)/shard_map/ppermute | solution.py:218
  195.0 10.1 %collective-permute-start.22 = (bf16[64,1024]{1,0:T(8,128)(2,1)S(1)}, bf16[64,1024]{1,0:T(8,128)(2,1)S(1)}, u32[]{:S(2)}, u32[]{:S(2)}) collective-permute-start(bf16[64,1024]{1,0:T(8,128)(2,1)S(1)} %add_convert_fusion.2), channel_id=1, source_target_pairs={{0,0},{1,4},{2,8},{3,12},{4,1},{5,5},{6,9},{7,13},{8,2},{9,6},{10,... | collective-permute-start | bytes 393224 | tf_op jit(solution)/shard_map/ppermute | solution.py:218

commit v4 on v1

v4 whole, which is shorter than its diff:
```python
import jax
import jax.numpy as jnp
from jax import lax
from jax.experimental import pallas as pl
from jax.experimental.pallas import tpu as pltpu
from jax.sharding import PartitionSpec as P

BF16, F32 = jnp.bfloat16, jnp.float32


def xor_perm(size, mask):
    return [(i, i ^ mask) for i in range(size)]


def active_units(block_ids, block_counts, unit_count):
    block_total = block_ids.shape[0]
    places = jnp.arange(block_total, dtype=jnp.int32)
    match = (block_ids[:, None] % block_total == places[None, :]) & (
        places < block_counts[0]
    )[:, None]
    active = jnp.any(match, axis=0).astype(F32)
    return jnp.repeat(active, unit_count // block_total)


def gate_up_kernel(td_ref, *refs):
    blocks, (gate_ref, up_ref, keep_ref, near_ref, far_ref, xs) = refs[:4], refs[4:]
    rows = xs.shape[0] // 4

    @pl.when(pl.program_id(0) == 0)
    def _():
        for j in range(4):
            place = pl.multiple_of((j ^ td_ref[0]) * rows, rows)
            xs[pl.ds(place, rows), :] = blocks[j][...]

    for i, w in enumerate((gate_ref, up_ref)):
        acc = jnp.dot(xs[...], w[...], preferred_element_type=F32)
        keep_ref[0, i] = acc[:rows]
        near_ref[i] = acc[rows : 2 * rows].astype(BF16)
        keep_ref[1, i] = acc[2 * rows : 3 * rows]
        far_ref[i] = acc[3 * rows :].astype(BF16)


def gate_up(td, blocks, gate_weight, up_weight, tile=1024):
    rows, depth = blocks[0].shape
    units = gate_weight.shape[1]
    whole = pl.BlockSpec((rows, depth), lambda i, td: (0, 0))
    weight = pl.BlockSpec((depth, tile), lambda i, td: (0, i))
    out = pl.BlockSpec((2, 2, rows, tile), lambda i, td: (0, 0, 0, i))
    side = pl.BlockSpec((2, rows, tile), lambda i, td: (0, 0, i))
    return pl.pallas_call(
        gate_up_kernel,
        grid_spec=pltpu.PrefetchScalarGridSpec(
            num_scalar_prefetch=1,
            grid=(units // tile,),
            in_specs=[whole] * 4 + [weight] * 2,
            out_specs=[out, side, side],
            scratch_shapes=[pltpu.VMEM((4 * rows, depth), BF16)],
        ),
        out_shape=[
            jax.ShapeDtypeStruct((2, 2, rows, units), F32),
            jax.ShapeDtypeStruct((2, rows, units), BF16),
            jax.ShapeDtypeStruct((2, rows, units), BF16),
        ],
        compiler_params=pltpu.CompilerParams(vmem_limit_bytes=40 << 20),
        cost_estimate=pl.CostEstimate(flops=20_000_000, bytes_accessed=20_000_000, transcendentals=0),
        name="gate_up",
    )(td, *blocks, gate_weight, up_weight)


def down_kernel(td_ref, h0, h1, h2, h3, down_ref, own_ref, *refs):
    outs, hs = refs[:-1], refs[-1]
    rows = h0.shape[0]

    @pl.when(pl.program_id(0) == 0)
    def _():
        for k, h in enumerate((h0, h1, h2, h3)):
            place = pl.multiple_of((k ^ td_ref[0]) * rows, rows)
            hs[pl.ds(place, rows), :] = h[...]

    acc = jnp.dot(hs[...], down_ref[...], preferred_element_type=F32)
    own_ref[...] = acc[:rows]
    if len(outs) == 1:
        for j in range(4):
            outs[0][j ^ td_ref[1]] = acc[j * rows : (j + 1) * rows].astype(BF16)
    else:
        for j in (1, 2, 3):
            outs[j - 1][...] = acc[j * rows : (j + 1) * rows].astype(BF16)


def down(td, hidden, down_weight, part, parts, stacked, tile=512):
    rows, depth = hidden[0].shape
    width = down_weight.shape[1] // parts
    first = part * (width // tile)
    whole = pl.BlockSpec((rows, depth), lambda i, td: (0, 0))
    weight = pl.BlockSpec((depth, tile), lambda i, td: (0, first + i))
    out = pl.BlockSpec((rows, tile), lambda i, td: (0, i))
    stack = pl.BlockSpec((4, rows, tile), lambda i, td: (0, 0, i))
    sent = [(4, rows, width)] if stacked else [(rows, width)] * 3
    return pl.pallas_call(
        down_kernel,
        grid_spec=pltpu.PrefetchScalarGridSpec(
            num_scalar_prefetch=1,
            grid=(width // tile,),
            in_specs=[whole] * 4 + [weight],
            out_specs=[out] + ([stack] if stacked else [out] * 3),
            scratch_shapes=[pltpu.VMEM((4 * rows, depth), BF16)],
        ),
        out_shape=[jax.ShapeDtypeStruct((rows, width), F32)]
        + [jax.ShapeDtypeStruct(shape, BF16) for shape in sent],
        compiler_params=pltpu.CompilerParams(vmem_limit_bytes=40 << 20),
        cost_estimate=pl.CostEstimate(flops=1_000_000, bytes_accessed=1_000_000, transcendentals=0),
        name="down",
    )(td, *hidden, down_weight)


def per_device(tokens, gate_weight, up_weight, down_weight, block_ids, block_counts):
    d, t = lax.axis_index("dp"), lax.axis_index("tensor")
    td = (d ^ t).reshape(1).astype(jnp.int32)
    dt = jnp.stack([d ^ t, t]).astype(jnp.int32)
    active = active_units(block_ids, block_counts, gate_weight.shape[1])
    turn = [(a * 4 + b, b * 4 + a) for a in range(4) for b in range(4)]
    rows = tokens.shape[0] // 2
    swap = lambda x, axis, mask: lax.ppermute(x, axis, xor_perm(4, mask))
    after = lambda x, *earlier: lax.optimization_barrier((x, *earlier))[0]
    mine, blocks, keep, send, near, across, hidden, partial, got, outs = ({} for _ in range(10))
    tick = [td]

    def turn_in(c):
        x = tokens[c * rows : (c + 1) * rows]
        mine[c] = lax.ppermute(x if c == 0 else after(x, mine[c - 1]), ("dp", "tensor"), turn)

    def spread(c):
        x = mine[c] if c == 0 else after(mine[c], *blocks[c - 1])
        one, two = swap(x, "tensor", 1), swap(x, "tensor", 2)
        blocks[c] = [mine[c], one, two, swap(two, "tensor", 1)]

    def first(c):
        keep[c], *send[c] = gate_up(after(td, *tick), blocks[c], gate_weight, up_weight)
        tick[:] = send[c]

    def to_core(c, *earlier):
        held = lax.optimization_barrier((*send[c], *earlier))[:2] if earlier else send[c]
        near[c] = [swap(x, "dp", 1) for x in held]

    def to_chip(c):
        keep[c] = lax.optimization_barrier((keep[c], *tick))[0]
        summed = (keep[c][1] + near[c][1].astype(F32)).astype(BF16)
        across[c] = swap(summed, "dp", 2)
        tick[:] = [summed]

    def gated(c):
        x = after(keep[c], *tick)
        total = x[0] + near[c][0].astype(F32) + across[c].astype(F32)
        own = (jnp.maximum(total[0], 0.0) * total[1] * active).astype(BF16)
        far = swap(own, "dp", 2)
        hidden[c] = [own, swap(own, "dp", 1), far, swap(far, "dp", 1)]
        tick[:] = [own]

    def second(c, h, parts):
        stacked = parts == 1
        partial[c, h], *sent = down(after(dt, *tick), hidden[c], down_weight, h, parts, stacked)
        if stacked:
            arrived = lax.all_to_all(sent[0], "tensor", 0, 0, tiled=True)
            got[c, h] = [(arrived[j], t == j) for j in range(4)]
        else:
            got[c, h] = [(swap(sent[j - 1], "tensor", j), None) for j in (1, 2, 3)]
        tick[:] = [sent[0]]

    def mix(c, h):
        mixed = after(partial[c, h], *tick)
        for x, is_own in got[c, h]:
            x = x.astype(F32)
            mixed = mixed + (x if is_own is None else jnp.where(is_own, 0.0, x))
        mixed = mixed.astype(BF16)
        outs[c, h] = lax.ppermute(mixed, ("dp", "tensor"), turn)
        tick[:] = [mixed]

    turn_in(0)
    spread(0)
    turn_in(1)
    tick.append(mine[1])
    first(0)
    spread(1)
    to_core(0, *blocks[1][:3])
    to_chip(0)
    first(1)
    to_core(1)
    gated(0)
    to_chip(1)
    second(0, 0, 1)
    gated(1)
    second(1, 0, 2)
    mix(0, 0)
    second(1, 1, 2)
    mix(1, 0)
    mix(1, 1)
    last = jnp.concatenate([outs[1, 0], outs[1, 1]], axis=1)
    return jnp.concatenate([outs[0, 0], last], axis=0)


def per_device_general(tokens, gate_weight, up_weight, down_weight, block_ids, block_counts):
    gathered = lax.all_gather(tokens, "tensor", axis=1, tiled=True)
    turned = lax.all_to_all(gathered, "dp", 1, 0, tiled=True)
    active = active_units(block_ids, block_counts, gate_weight.shape[1])
    sums = [
        lax.psum_scatter(
            jnp.dot(turned, w, preferred_element_type=F32), "dp", scatter_dimension=0, tiled=True
        )
        for w in (gate_weight, up_weight)
    ]
    hidden = (jnp.maximum(sums[0], 0.0) * sums[1] * active).astype(BF16)
    hidden = lax.all_gather(hidden, "dp", axis=0, tiled=True)
    partial = jnp.dot(hidden, down_weight, preferred_element_type=F32)
    partial = lax.all_to_all(partial, "dp", 0, 1, tiled=True)
    return lax.psum_scatter(partial, "tensor", scatter_dimension=1, tiled=True).astype(BF16)


def solution(mesh):
    placed = (
        P(("groups", "dp"), "tensor"),
        P("dp", "tensor"),
        P("dp", "tensor"),
        P("tensor", "dp"),
        P(("groups", "tensor")),
        P(("groups", "tensor")),
    )
    square = mesh.shape["dp"] == 4 and mesh.shape["tensor"] == 4
    return jax.shard_map(
        per_device if square else per_device_general,
        mesh=mesh,
        in_specs=placed,
        out_specs=P(("groups", "dp"), "tensor"),
        check_vma=False,
    )
```

time: 264 us -> 204 us (0.77)
  waiting for transfers between devices: 141 us -> 71.2 us
  starting transfers between devices: 63.6 us -> 72.5 us
  other arithmetic: 3.26 us -> 8.06 us
  Pallas kernels: 53.4 us -> 50.1 us
    ppermute x20 -> x24, waiting for transfers between devices: 115 us -> 46.8 us  [per_device(): swap = lambda x, axis, mask: lax.ppermute(x, axis, xor_perm(4, mask))]
    ppermute x4 -> x5, starting transfers between devices: 25.9 us -> 31.2 us  [the longest x3 24.9 us: mix(): outs[c, h] = lax.ppermute(mixed, ('dp', 'tensor'), turn)]
    all_to_all x0 -> x1, starting transfers between devices: none -> 4.59 us  [second(): arrived = lax.all_to_all(sent[0], 'tensor', 0, 0, tiled=True)]
    pallas_call x2, Pallas kernels: 32.1 us -> 29.1 us  [gate_up(): pl.pallas_call(gate_up_kernel, grid_spec=pltpu.PrefetchScalarGridSpec(num...]
    convert_element_type x6 -> x7, other arithmetic: 1.37 us -> 4.14 us  [the longest x3 2.45 us: mix(): mixed = mixed.astype(BF16)]
    ppermute x4 -> x5, waiting for transfers between devices: 26 us -> 24.4 us  [the longest x2 19.7 us: turn_in(): lax.ppermute(x if c == 0 else after(x, mine[c - 1]), ('dp', 'tensor'), turn)]
    ppermute x20 -> x24, starting transfers between devices: 37.7 us -> 36.7 us  [per_device(): swap = lambda x, axis, mask: lax.ppermute(x, axis, xor_perm(4, mask))]
    pallas_call x2 -> x3, Pallas kernels: 21.3 us -> 20.9 us  [down(): pl.pallas_call(down_kernel, grid_spec=pltpu.PrefetchScalarGridSpec(num_sc...]
  transfers between devices with their start and end apart: 24 -> 30, of which waited for: 15 -> 15; matrix products, arithmetic and copies ran while one was open for 1% -> 4% of each run, Pallas kernels for 20% -> 25%
where the time goes in v4:
time: 204 us
  starting transfers between devices  72.5 us (36%)
  waiting for transfers between devices  71.2 us (35%)
  Pallas kernels  50.1 us (25%)
  other arithmetic  8.06 us (4%)
    ppermute x24, waiting for transfers between devices, per_device(): swap = lambda x, axis, mask: lax.ppermute(x, axis, xor_perm(4, mask))  46.8 us
    ppermute x24, starting transfers between devices, per_device(): swap = lambda x, axis, mask: lax.ppermute(x, axis, xor_perm(4, mask))  36.7 us
    pallas_call x2, Pallas kernels, gate_up(): pl.pallas_call(gate_up_kernel, grid_spec=pltpu.PrefetchScalarGridSpec(num...  29.1 us
    ppermute x3, starting transfers between devices, mix(): outs[c, h] = lax.ppermute(mixed, ('dp', 'tensor'), turn)  24.9 us
    pallas_call x3, Pallas kernels, down(): pl.pallas_call(down_kernel, grid_spec=pltpu.PrefetchScalarGridSpec(num_sc...  20.9 us
    ppermute x2, waiting for transfers between devices, turn_in(): lax.ppermute(x if c == 0 else after(x, mine[c - 1]), ('dp', 'tensor'), turn)  19.7 us
    ppermute x2, starting transfers between devices, turn_in(): lax.ppermute(x if c == 0 else after(x, mine[c - 1]), ('dp', 'tensor'), turn)  6.38 us
    ppermute x3, waiting for transfers between devices, mix(): outs[c, h] = lax.ppermute(mixed, ('dp', 'tensor'), turn)  4.72 us
  transfers between devices with their start and end apart: 30, of which 15 were waited for; matrix products, arithmetic and copies ran while one was open for 4% of the time, Pallas kernels for 25%

profile of v4, /device:TPU:2, one launch (start us, length us, event | category | flops | bytes accessed | tf_op | source)
XLA Modules:
  0.0 203.8 jit_solution(2285124692257546509)
XLA Ops:
  1.1 4.5 %collective-permute-start = (bf16[64,2048]{1,0:T(8,128)(2,1)S(1)}, bf16[64,2048]{1,0:T(8,128)(2,1)S(1)}, u32[]{:S(2)}, u32[]{:S(2)}) collective-permute-start(bf16[64,2048]{1,0:T(8,128)(2,1)S(1)} %get-tuple-element.68), channel_id=1, source_target_pairs={{0,0},{1,4},{2,8},{3,12},{4,1},{5,5},{6,9},{7,13},{8,2},{9,6},{10,... | collective-permute-start | bytes 786440 | tf_op jit(solution)/shard_map/ppermute | solution.py:130
  5.5 13.6 %collective-permute-done.refs_0_ = bf16[64,2048]{1,0:T(8,128)(2,1)S(1)} collective-permute-done((bf16[64,2048]{1,0:T(8,128)(2,1)S(1)}, bf16[64,2048]{1,0:T(8,128)(2,1)S(1)}, u32[]{:S(2)}, u32[]{:S(2)}) %collective-permute-start) | collective-permute-done | bytes 262176 | tf_op jit(solution)/shard_map/ppermute | solution.py:130
  19.1 1.9 collective-permute-start.1
  21.0 4.3 %collective-permute-start.2 = (bf16[64,2048]{1,0:T(8,128)(2,1)S(1)}, bf16[64,2048]{1,0:T(8,128)(2,1)S(1)}, u32[]{:S(2)}, u32[]{:S(2)}) collective-permute-start(bf16[64,2048]{1,0:T(8,128)(2,1)S(1)} %collective-permute-done.refs_0_), channel_id=1, source_target_pairs={{0,1},{1,0},{2,3},{3,2},{4,5},{5,4},{6,7},{7,6},{8,9},{9,8},{10,11... | collective-permute-start | bytes 786440 | tf_op jit(solution)/shard_map/ppermute | solution.py:123
  25.4 6.7 %collective-permute-done.3.refs_2_ = bf16[64,2048]{1,0:T(8,128)(2,1)S(1)} collective-permute-done((bf16[64,2048]{1,0:T(8,128)(2,1)S(1)}, bf16[64,2048]{1,0:T(8,128)(2,1)S(1)}, u32[]{:S(2)}, u32[]{:S(2)}) %collective-permute-start.3) | collective-permute-done | bytes 262176 | tf_op jit(solution)/shard_map/ppermute | solution.py:123
  32.1 3.4 %collective-permute-start.4 = (bf16[64,2048]{1,0:T(8,128)(2,1)S(1)}, bf16[64,2048]{1,0:T(8,128)(2,1)S(1)}, u32[]{:S(2)}, u32[]{:S(2)}) collective-permute-start(bf16[64,2048]{1,0:T(8,128)(2,1)S(1)} %collective-permute-done.3.refs_2_), channel_id=1, source_target_pairs={{0,1},{1,0},{2,3},{3,2},{4,5},{5,4},{6,7},{7,6},{8,9},{9,8},{10,11... | collective-permute-start | bytes 786440 | tf_op jit(solution)/shard_map/ppermute | solution.py:123
  35.5 6.1 %collective-permute-done.1.refs_0_ = bf16[64,2048]{1,0:T(8,128)(2,1)S(1)} collective-permute-done((bf16[64,2048]{1,0:T(8,128)(2,1)S(1)}, bf16[64,2048]{1,0:T(8,128)(2,1)S(1)}, u32[]{:S(2)}, u32[]{:S(2)}) %collective-permute-start.1) | collective-permute-done | bytes 262176 | tf_op jit(solution)/shard_map/ppermute | solution.py:130
  41.6 4.8 %collective-permute-start.6 = (bf16[64,2048]{1,0:T(8,128)(2,1)S(1)}, bf16[64,2048]{1,0:T(8,128)(2,1)S(1)}, u32[]{:S(2)}, u32[]{:S(2)}) collective-permute-start(bf16[64,2048]{1,0:T(8,128)(2,1)S(1)} %collective-permute-done.1.refs_0_), channel_id=1, source_target_pairs={{0,2},{1,3},{2,0},{3,1},{4,6},{5,7},{6,4},{7,5},{8,10},{9,11},{10,... | collective-permute-start | bytes 786440 | tf_op jit(solution)/shard_map/ppermute | solution.py:123
  46.4 2.5 %collective-permute-start.5 = (bf16[64,2048]{1,0:T(8,128)(2,1)S(1)}, bf16[64,2048]{1,0:T(8,128)(2,1)S(1)}, u32[]{:S(2)}, u32[]{:S(2)}) collective-permute-start(bf16[64,2048]{1,0:T(8,128)(2,1)S(1)} %collective-permute-done.1.refs_0_), channel_id=1, source_target_pairs={{0,1},{1,0},{2,3},{3,2},{4,5},{5,4},{6,7},{7,6},{8,9},{9,8},{10,11... | collective-permute-start | bytes 786440 | tf_op jit(solution)/shard_map/ppermute | solution.py:123
  48.9 14.6 %gate_up.2 = (f32[2,2,64,4096]{3,2,1,0:T(8,128)S(1)}, bf16[2,64,4096]{2,1,0:T(8,128)(2,1)S(1)}, bf16[2,64,4096]{2,1,0:T(8,128)(2,1)S(1)}) custom-call(s32[1]{0:T(128)} %bitcast.td_ref, bf16[64,2048]{1,0:T(8,128)(2,1)S(1)} %collective-permute-done.refs_0_, bf16[64,2048]{1,0:T(8,128)(2,1)S(1)} %collective-permute-done.2.refs_1_, ...), custom_call_target="tpu_custom_call" | custom-call | flops 20000000 | bytes 20000000 | tf_op jit(solution)/shard_map/gate_up/pallas_call | solution.py:50
  65.3 2.2 %collective-permute-done.7 = bf16[2,64,4096]{2,1,0:T(8,128)(2,1)S(1)} collective-permute-done((bf16[2,64,4096]{2,1,0:T(8,128)(2,1)S(1)}, bf16[2,64,4096]{2,1,0:T(8,128)(2,1)S(1)}, u32[]{:S(2)}, u32[]{:S(2)}) %collective-permute-start.7) | collective-permute-done | bytes 1048608 | tf_op jit(solution)/shard_map/ppermute | solution.py:123
  68.9 2.1 %collective-permute-start.8 = (bf16[64,2048]{1,0:T(8,128)(2,1)S(1)}, bf16[64,2048]{1,0:T(8,128)(2,1)S(1)}, u32[]{:S(2)}, u32[]{:S(2)}) collective-permute-start(bf16[64,2048]{1,0:T(8,128)(2,1)S(1)} %collective-permute-done.6.refs_2_), channel_id=1, source_target_pairs={{0,1},{1,0},{2,3},{3,2},{4,5},{5,4},{6,7},{7,6},{8,9},{9,8},{10,11... | collective-permute-start | bytes 786440 | tf_op jit(solution)/shard_map/ppermute | solution.py:123
  71.2 6.2 %collective-permute-done.8.refs_3_ = bf16[64,2048]{1,0:T(8,128)(2,1)S(1)} collective-permute-done((bf16[64,2048]{1,0:T(8,128)(2,1)S(1)}, bf16[64,2048]{1,0:T(8,128)(2,1)S(1)}, u32[]{:S(2)}, u32[]{:S(2)}) %collective-permute-start.8) | collective-permute-done | bytes 262176 | tf_op jit(solution)/shard_map/ppermute | solution.py:123
  77.4 14.6 %gate_up.3 = (f32[2,2,64,4096]{3,2,1,0:T(8,128)S(1)}, bf16[2,64,4096]{2,1,0:T(8,128)(2,1)S(1)}, bf16[2,64,4096]{2,1,0:T(8,128)(2,1)S(1)}) custom-call(s32[1]{0:T(128)} %bitcast.td_ref, bf16[64,2048]{1,0:T(8,128)(2,1)S(1)} %collective-permute-done.1.refs_0_, bf16[64,2048]{1,0:T(8,128)(2,1)S(1)} %collective-permute-done.5.refs_1_, ...), custom_call_target="tpu_custom_call" | custom-call | flops 20000000 | bytes 20000000 | tf_op jit(solution)/shard_map/gate_up/pallas_call | solution.py:50
  98.1 10.5 %collective-permute-done.13.h2 = bf16[64,4096]{1,0:T(8,128)(2,1)S(1)} collective-permute-done((bf16[64,4096]{1,0:T(8,128)(2,1)S(1)}, bf16[64,4096]{1,0:T(8,128)(2,1)S(1)}, u32[]{:S(2)}, u32[]{:S(2)}) %collective-permute-start.13) | collective-permute-done | bytes 524320 | tf_op jit(solution)/shard_map/ppermute | solution.py:123
  108.7 1.8 collective-permute-done.14.h3
  110.5 10.1 %down.3 = (f32[64,2048]{1,0:T(8,128)S(1)}, bf16[4,64,2048]{2,1,0:T(8,128)(2,1)}) custom-call(s32[2]{0:T(128)S(1)} %pad_add_fusion.td_ref, bf16[64,4096]{1,0:T(8,128)(2,1)S(1)} %fusion.10.h0, bf16[64,4096]{1,0:T(8,128)(2,1)S(1)} %collective-permute-done.12.h1, bf16[64,4096]{1,0:T(8,128)(2,1)S(1)} %collective-permute-done.13.h2, ...), custom_call_target="tpu_custom_call" | custom-call | flops 1000000 | bytes 1000000 | tf_op jit(solution)/shard_map/down/pallas_call | solution.py:99
  120.6 4.6 %all-to-all-start = ((bf16[4,64,2048]{2,1,0:T(8,128)(2,1)}), bf16[4,64,2048]{2,1,0:T(8,128)(2,1)}, u32[]{:S(2)}, u32[]{:S(2)}) async-start(bf16[4,64,2048]{2,1,0:T(8,128)(2,1)} %get-tuple-element.53), calls=%async_computation | async-start | bytes 2097152 | tf_op jit(solution)/shard_map/all_to_all | solution.py:163
  125.2 4.5 %collective-permute-done.16 = bf16[2,64,4096]{2,1,0:T(8,128)(2,1)} collective-permute-done((bf16[2,64,4096]{2,1,0:T(8,128)(2,1)}, bf16[2,64,4096]{2,1,0:T(8,128)(2,1)}, u32[]{:S(2)}, u32[]{:S(2)}) %collective-permute-start.16) | collective-permute-done | bytes 1048608 | tf_op jit(solution)/shard_map/ppermute | solution.py:123
  129.7 2.6 %fusion.2 = f32[2,64,4096]{2,1,0:T(8,128)S(1)} fusion(bf16[2,64,4096]{2,1,0:T(8,128)(2,1)} %collective-permute-done.16, bf16[2,64,4096]{2,1,0:T(8,128)(2,1)} %collective-permute-done.15, f32[2,2,64,4096]{3,2,1,0:T(8,128)} %copy-done), kind=kLoop, calls=%fused_computation.4 | loop fusion | flops 2097152 | bytes 6291456 | tf_op jit(solution)/shard_map/add | solution.py:153
  133.8 11.3 %collective-permute-done.18.h2 = bf16[64,4096]{1,0:T(8,128)(2,1)S(1)} collective-permute-done((bf16[64,4096]{1,0:T(8,128)(2,1)S(1)}, bf16[64,4096]{1,0:T(8,128)(2,1)S(1)}, u32[]{:S(2)}, u32[]{:S(2)}) %collective-permute-start.18) | collective-permute-done | bytes 524320 | tf_op jit(solution)/shard_map/ppermute | solution.py:123
  145.2 1.9 collective-permute-done.19.h3
  147.1 5.4 %down.4 = (f32[64,1024]{1,0:T(8,128)S(1)}, bf16[64,1024]{1,0:T(8,128)(2,1)S(1)}, bf16[64,1024]{1,0:T(8,128)(2,1)S(1)}, bf16[64,1024]{1,0:T(8,128)(2,1)S(1)}) custom-call(s32[2]{0:T(128)S(1)} %pad_add_fusion.td_ref, bf16[64,4096]{1,0:T(8,128)(2,1)S(1)} %fusion.7.h0, bf16[64,4096]{1,0:T(8,128)(2,1)S(1)} %collective-permute-done.17.h1, ...), custom_call_target="tpu_custom_call" | custom-call | flops 1000000 | bytes 1000000 | tf_op jit(solution)/shard_map/down/pallas_call | solution.py:99
  152.5 2.0 collective-permute-start.21
  154.6 2.9 %collective-permute-start.22 = (bf16[64,1024]{1,0:T(8,128)(2,1)S(1)}, bf16[64,1024]{1,0:T(8,128)(2,1)S(1)}, u32[]{:S(2)}, u32[]{:S(2)}) collective-permute-start(bf16[64,1024]{1,0:T(8,128)(2,1)S(1)} %get-tuple-element.62), channel_id=1, source_target_pairs={{0,2},{1,3},{2,0},{3,1},{4,6},{5,7},{6,4},{7,5},{8,10},{9,11},{10,... | collective-permute-start | bytes 393224 | tf_op jit(solution)/shard_map/ppermute | solution.py:123
  158.9 3.4 %collective-permute-start.20 = (bf16[64,2048]{1,0:T(8,128)(2,1)S(1)}, bf16[64,2048]{1,0:T(8,128)(2,1)S(1)}, u32[]{:S(2)}, u32[]{:S(2)}) collective-permute-start(bf16[64,2048]{1,0:T(8,128)(2,1)S(1)} %fusion.11), channel_id=1, source_target_pairs={{0,0},{1,4},{2,8},{3,12},{4,1},{5,5},{6,9},{7,13},{8,2},{9,6},{10,... | collective-permute-start | bytes 786440 | tf_op jit(solution)/shard_map/ppermute | solution.py:175
  162.3 5.5 %down.5 = (f32[64,1024]{1,0:T(8,128)S(1)}, bf16[64,1024]{1,0:T(8,128)(2,1)S(1)}, bf16[64,1024]{1,0:T(8,128)(2,1)S(1)}, bf16[64,1024]{1,0:T(8,128)(2,1)S(1)}) custom-call(s32[2]{0:T(128)S(1)} %pad_add_fusion.td_ref, bf16[64,4096]{1,0:T(8,128)(2,1)S(1)} %fusion.7.h0, bf16[64,4096]{1,0:T(8,128)(2,1)S(1)} %collective-permute-done.17.h1, ...), custom_call_target="tpu_custom_call" | custom-call | flops 1000000 | bytes 1000000 | tf_op jit(solution)/shard_map/down/pallas_call | solution.py:99
  167.8 2.9 %collective-permute-start.26 = (bf16[64,1024]{1,0:T(8,128)(2,1)S(1)}, bf16[64,1024]{1,0:T(8,128)(2,1)S(1)}, u32[]{:S(2)}, u32[]{:S(2)}) collective-permute-start(bf16[64,1024]{1,0:T(8,128)(2,1)S(1)} %get-tuple-element.66), channel_id=1, source_target_pairs={{0,2},{1,3},{2,0},{3,1},{4,6},{5,7},{6,4},{7,5},{8,10},{9,11},{10,... | collective-permute-start | bytes 393224 | tf_op jit(solution)/shard_map/ppermute | solution.py:123
  170.7 5.0 %collective-permute-start.27 = (bf16[64,1024]{1,0:T(8,128)(2,1)S(1)}, bf16[64,1024]{1,0:T(8,128)(2,1)S(1)}, u32[]{:S(2)}, u32[]{:S(2)}) collective-permute-start(bf16[64,1024]{1,0:T(8,128)(2,1)S(1)} %get-tuple-element.67), channel_id=1, source_target_pairs={{0,3},{1,2},{2,1},{3,0},{4,7},{5,6},{6,5},{7,4},{8,11},{9,10},{10,... | collective-permute-start | bytes 393224 | tf_op jit(solution)/shard_map/ppermute | solution.py:123
  176.7 8.3 %collective-permute-start.24 = (bf16[64,1024]{1,0:T(8,128)(2,1)S(1)}, bf16[64,1024]{1,0:T(8,128)(2,1)S(1)}, u32[]{:S(2)}, u32[]{:S(2)}) collective-permute-start(bf16[64,1024]{1,0:T(8,128)(2,1)S(1)} %add_convert_fusion.1), channel_id=1, source_target_pairs={{0,0},{1,4},{2,8},{3,12},{4,1},{5,5},{6,9},{7,13},{8,2},{9,6},{10,... | collective-permute-start | bytes 393224 | tf_op jit(solution)/shard_map/ppermute | solution.py:175
  185.1 13.2 %collective-permute-start.28 = (bf16[64,1024]{1,0:T(8,128)(2,1)S(1)}, bf16[64,1024]{1,0:T(8,128)(2,1)S(1)}, u32[]{:S(2)}, u32[]{:S(2)}) collective-permute-start(bf16[64,1024]{1,0:T(8,128)(2,1)S(1)} %add_convert_fusion), channel_id=1, source_target_pairs={{0,0},{1,4},{2,8},{3,12},{4,1},{5,5},{6,9},{7,13},{8,2},{9,6},{10,... | collective-permute-start | bytes 393224 | tf_op jit(solution)/shard_map/ppermute | solution.py:175
  198.8 4.2 %collective-permute-done.28 = bf16[64,1024]{1,0:T(8,128)(2,1)S(1)} collective-permute-done((bf16[64,1024]{1,0:T(8,128)(2,1)S(1)}, bf16[64,1024]{1,0:T(8,128)(2,1)S(1)}, u32[]{:S(2)}, u32[]{:S(2)}) %collective-permute-start.28) | collective-permute-done | bytes 131104 | tf_op jit(solution)/shard_map/ppermute | solution.py:175
  (54 shorter events, 15.5 us)
Async XLA Ops:
  1.1 18.0 %collective-permute-start = (bf16[64,2048]{1,0:T(8,128)(2,1)S(1)}, bf16[64,2048]{1,0:T(8,128)(2,1)S(1)}, u32[]{:S(2)}, u32[]{:S(2)}) collective-permute-start(bf16[64,2048]{1,0:T(8,128)(2,1)S(1)} %get-tuple-element.68), channel_id=1, source_target_pairs={{0,0},{1,4},{2,8},{3,12},{4,1},{5,5},{6,9},{7,13},{8,2},{9,6},{10,... | collective-permute-start | bytes 786440 | tf_op jit(solution)/shard_map/ppermute | solution.py:130
  19.1 13.0 %collective-permute-start.3 = (bf16[64,2048]{1,0:T(8,128)(2,1)S(1)}, bf16[64,2048]{1,0:T(8,128)(2,1)S(1)}, u32[]{:S(2)}, u32[]{:S(2)}) collective-permute-start(bf16[64,2048]{1,0:T(8,128)(2,1)S(1)} %collective-permute-done.refs_0_), channel_id=1, source_target_pairs={{0,2},{1,3},{2,0},{3,1},{4,6},{5,7},{6,4},{7,5},{8,10},{9,11},{10,... | collective-permute-start | bytes 786440 | tf_op jit(solution)/shard_map/ppermute | solution.py:123
  19.1 22.5 %collective-permute-start.1 = (bf16[64,2048]{1,0:T(8,128)(2,1)S(1)}, bf16[64,2048]{1,0:T(8,128)(2,1)S(1)}, u32[]{:S(2)}, u32[]{:S(2)}) collective-permute-start(bf16[64,2048]{1,0:T(8,128)(2,1)S(1)} %get-tuple-element.37), channel_id=1, source_target_pairs={{0,0},{1,4},{2,8},{3,12},{4,1},{5,5},{6,9},{7,13},{8,2},{9,6},{10,... | collective-permute-start | bytes 786440 | tf_op jit(solution)/shard_map/ppermute | solution.py:130
  21.0 20.5 %collective-permute-start.2 = (bf16[64,2048]{1,0:T(8,128)(2,1)S(1)}, bf16[64,2048]{1,0:T(8,128)(2,1)S(1)}, u32[]{:S(2)}, u32[]{:S(2)}) collective-permute-start(bf16[64,2048]{1,0:T(8,128)(2,1)S(1)} %collective-permute-done.refs_0_), channel_id=1, source_target_pairs={{0,1},{1,0},{2,3},{3,2},{4,5},{5,4},{6,7},{7,6},{8,9},{9,8},{10,11... | collective-permute-start | bytes 786440 | tf_op jit(solution)/shard_map/ppermute | solution.py:123
  32.1 9.5 %collective-permute-start.4 = (bf16[64,2048]{1,0:T(8,128)(2,1)S(1)}, bf16[64,2048]{1,0:T(8,128)(2,1)S(1)}, u32[]{:S(2)}, u32[]{:S(2)}) collective-permute-start(bf16[64,2048]{1,0:T(8,128)(2,1)S(1)} %collective-permute-done.3.refs_2_), channel_id=1, source_target_pairs={{0,1},{1,0},{2,3},{3,2},{4,5},{5,4},{6,7},{7,6},{8,9},{9,8},{10,11... | collective-permute-start | bytes 786440 | tf_op jit(solution)/shard_map/ppermute | solution.py:123
  41.6 21.9 %collective-permute-start.6 = (bf16[64,2048]{1,0:T(8,128)(2,1)S(1)}, bf16[64,2048]{1,0:T(8,128)(2,1)S(1)}, u32[]{:S(2)}, u32[]{:S(2)}) collective-permute-start(bf16[64,2048]{1,0:T(8,128)(2,1)S(1)} %collective-permute-done.1.refs_0_), channel_id=1, source_target_pairs={{0,2},{1,3},{2,0},{3,1},{4,6},{5,7},{6,4},{7,5},{8,10},{9,11},{10,... | collective-permute-start | bytes 786440 | tf_op jit(solution)/shard_map/ppermute | solution.py:123
  46.4 17.1 %collective-permute-start.5 = (bf16[64,2048]{1,0:T(8,128)(2,1)S(1)}, bf16[64,2048]{1,0:T(8,128)(2,1)S(1)}, u32[]{:S(2)}, u32[]{:S(2)}) collective-permute-start(bf16[64,2048]{1,0:T(8,128)(2,1)S(1)} %collective-permute-done.1.refs_0_), channel_id=1, source_target_pairs={{0,1},{1,0},{2,3},{3,2},{4,5},{5,4},{6,7},{7,6},{8,9},{9,8},{10,11... | collective-permute-start | bytes 786440 | tf_op jit(solution)/shard_map/ppermute | solution.py:123
  63.5 4.0 %collective-permute-start.7 = (bf16[2,64,4096]{2,1,0:T(8,128)(2,1)S(1)}, bf16[2,64,4096]{2,1,0:T(8,128)(2,1)S(1)}, u32[]{:S(2)}, u32[]{:S(2)}) collective-permute-start(bf16[2,64,4096]{2,1,0:T(8,128)(2,1)S(1)} %get-tuple-element.43), channel_id=1, source_target_pairs={{0,4},{4,0},{8,12},{12,8},{1,5},{5,1},{9,13},{13,9},{2,6},{6,2},{1... | collective-permute-start | bytes 3145736 | tf_op jit(solution)/shard_map/ppermute | solution.py:123
  65.2 3.7 %copy-start.1 = (s32[32]{0:T(128)S(1)}, s32[32]{0:T(128)}, u32[]{:S(2)}) copy-start(s32[32]{0:T(128)} %param.10) | copy-start | bytes 388
  65.2 27.3 %collective-permute-start.9 = (bf16[2,64,4096]{2,1,0:T(8,128)(2,1)S(1)}, bf16[2,64,4096]{2,1,0:T(8,128)(2,1)S(1)}, u32[]{:S(2)}, u32[]{:S(2)}) collective-permute-start(bf16[2,64,4096]{2,1,0:T(8,128)(2,1)S(1)} %get-tuple-element.49), channel_id=1, source_target_pairs={{0,4},{4,0},{8,12},{12,8},{1,5},{5,1},{9,13},{13,9},{2,6},{6,2},{1... | collective-permute-start | bytes 3145736 | tf_op jit(solution)/shard_map/ppermute | solution.py:123
  67.7 25.5 %collective-permute-start.10 = (bf16[2,64,4096]{2,1,0:T(8,128)(2,1)S(1)}, bf16[2,64,4096]{2,1,0:T(8,128)(2,1)S(1)}, u32[]{:S(2)}, u32[]{:S(2)}) collective-permute-start(bf16[2,64,4096]{2,1,0:T(8,128)(2,1)S(1)} %fusion.1), channel_id=1, source_target_pairs={{0,8},{4,12},{8,0},{12,4},{1,9},{5,13},{9,1},{13,5},{2,10},{6,14},... | collective-permute-start | bytes 3145736 | tf_op jit(solution)/shard_map/ppermute | solution.py:123
  68.9 8.4 %collective-permute-start.8 = (bf16[64,2048]{1,0:T(8,128)(2,1)S(1)}, bf16[64,2048]{1,0:T(8,128)(2,1)S(1)}, u32[]{:S(2)}, u32[]{:S(2)}) collective-permute-start(bf16[64,2048]{1,0:T(8,128)(2,1)S(1)} %collective-permute-done.6.refs_2_), channel_id=1, source_target_pairs={{0,1},{1,0},{2,3},{3,2},{4,5},{5,4},{6,7},{7,6},{8,9},{9,8},{10,11... | collective-permute-start | bytes 786440 | tf_op jit(solution)/shard_map/ppermute | solution.py:123
  91.9 3.4 %copy-start = (f32[2,2,64,4096]{3,2,1,0:T(8,128)}, f32[2,2,64,4096]{3,2,1,0:T(8,128)S(1)}, u32[]{:S(2)}) copy-start(f32[2,2,64,4096]{3,2,1,0:T(8,128)S(1)} %get-tuple-element.54) | copy-start | bytes 12582916
  91.9 3.4 %collective-permute-start.11 = (bf16[2,64,4096]{2,1,0:T(8,128)(2,1)S(1)}, bf16[2,64,4096]{2,1,0:T(8,128)(2,1)S(1)}, u32[]{:S(2)}, u32[]{:S(2)}) collective-permute-start(bf16[2,64,4096]{2,1,0:T(8,128)(2,1)S(1)} %get-tuple-element.47), channel_id=1, source_target_pairs={{0,4},{4,0},{8,12},{12,8},{1,5},{5,1},{9,13},{13,9},{2,6},{6,2},{1... | collective-permute-start | bytes 3145736 | tf_op jit(solution)/shard_map/ppermute | solution.py:123
  92.0 33.2 %collective-permute-start.15 = (bf16[2,64,4096]{2,1,0:T(8,128)(2,1)S(1)}, bf16[2,64,4096]{2,1,0:T(8,128)(2,1)}, u32[]{:S(2)}, u32[]{:S(2)}) collective-permute-start(bf16[2,64,4096]{2,1,0:T(8,128)(2,1)S(1)} %get-tuple-element.46), channel_id=1, source_target_pairs={{0,4},{4,0},{8,12},{12,8},{1,5},{5,1},{9,13},{13,9},{2,6},{6,2},{1... | collective-permute-start | bytes 3145736 | tf_op jit(solution)/shard_map/ppermute | solution.py:123
  93.7 14.9 %collective-permute-start.13 = (bf16[64,4096]{1,0:T(8,128)(2,1)S(1)}, bf16[64,4096]{1,0:T(8,128)(2,1)S(1)}, u32[]{:S(2)}, u32[]{:S(2)}) collective-permute-start(bf16[64,4096]{1,0:T(8,128)(2,1)S(1)} %fusion.10.h0), channel_id=1, source_target_pairs={{0,8},{4,12},{8,0},{12,4},{1,9},{5,13},{9,1},{13,5},{2,10},{6,14},... | collective-permute-start | bytes 1572872 | tf_op jit(solution)/shard_map/ppermute | solution.py:123
  96.6 33.1 %collective-permute-start.16 = (bf16[2,64,4096]{2,1,0:T(8,128)(2,1)}, bf16[2,64,4096]{2,1,0:T(8,128)(2,1)}, u32[]{:S(2)}, u32[]{:S(2)}) collective-permute-start(bf16[2,64,4096]{2,1,0:T(8,128)(2,1)} %fusion.3), channel_id=1, source_target_pairs={{0,8},{4,12},{8,0},{12,4},{1,9},{5,13},{9,1},{13,5},{2,10},{6,14},... | collective-permute-start | bytes 3145736 | tf_op jit(solution)/shard_map/ppermute | solution.py:123
  98.1 10.6 %collective-permute-start.12 = (bf16[64,4096]{1,0:T(8,128)(2,1)S(1)}, bf16[64,4096]{1,0:T(8,128)(2,1)S(1)}, u32[]{:S(2)}, u32[]{:S(2)}) collective-permute-start(bf16[64,4096]{1,0:T(8,128)(2,1)S(1)} %fusion.10.h0), channel_id=1, source_target_pairs={{0,4},{4,0},{8,12},{12,8},{1,5},{5,1},{9,13},{13,9},{2,6},{6,2},{1... | collective-permute-start | bytes 1572872 | tf_op jit(solution)/shard_map/ppermute | solution.py:123
  108.6 1.9 collective-permute-start.14
  120.6 36.9 %all-to-all-start = ((bf16[4,64,2048]{2,1,0:T(8,128)(2,1)}), bf16[4,64,2048]{2,1,0:T(8,128)(2,1)}, u32[]{:S(2)}, u32[]{:S(2)}) async-start(bf16[4,64,2048]{2,1,0:T(8,128)(2,1)} %get-tuple-element.53), calls=%async_computation | async-start | bytes 2097152 | tf_op jit(solution)/shard_map/all_to_all | solution.py:163
  132.4 12.7 %collective-permute-start.18 = (bf16[64,4096]{1,0:T(8,128)(2,1)S(1)}, bf16[64,4096]{1,0:T(8,128)(2,1)S(1)}, u32[]{:S(2)}, u32[]{:S(2)}) collective-permute-start(bf16[64,4096]{1,0:T(8,128)(2,1)S(1)} %fusion.7.h0), channel_id=1, source_target_pairs={{0,8},{4,12},{8,0},{12,4},{1,9},{5,13},{9,1},{13,5},{2,10},{6,14},... | collective-permute-start | bytes 1572872 | tf_op jit(solution)/shard_map/ppermute | solution.py:123
  133.8 11.3 %collective-permute-start.17 = (bf16[64,4096]{1,0:T(8,128)(2,1)S(1)}, bf16[64,4096]{1,0:T(8,128)(2,1)S(1)}, u32[]{:S(2)}, u32[]{:S(2)}) collective-permute-start(bf16[64,4096]{1,0:T(8,128)(2,1)S(1)} %fusion.7.h0), channel_id=1, source_target_pairs={{0,4},{4,0},{8,12},{12,8},{1,5},{5,1},{9,13},{13,9},{2,6},{6,2},{1... | collective-permute-start | bytes 1572872 | tf_op jit(solution)/shard_map/ppermute | solution.py:123
  145.2 1.9 collective-permute-start.19
  152.5 15.3 %collective-permute-start.21 = (bf16[64,1024]{1,0:T(8,128)(2,1)S(1)}, bf16[64,1024]{1,0:T(8,128)(2,1)S(1)}, u32[]{:S(2)}, u32[]{:S(2)}) collective-permute-start(bf16[64,1024]{1,0:T(8,128)(2,1)S(1)} %get-tuple-element.56), channel_id=1, source_target_pairs={{0,1},{1,0},{2,3},{3,2},{4,5},{5,4},{6,7},{7,6},{8,9},{9,8},{10,11... | collective-permute-start | bytes 393224 | tf_op jit(solution)/shard_map/ppermute | solution.py:123
  154.6 16.2 %collective-permute-start.22 = (bf16[64,1024]{1,0:T(8,128)(2,1)S(1)}, bf16[64,1024]{1,0:T(8,128)(2,1)S(1)}, u32[]{:S(2)}, u32[]{:S(2)}) collective-permute-start(bf16[64,1024]{1,0:T(8,128)(2,1)S(1)} %get-tuple-element.62), channel_id=1, source_target_pairs={{0,2},{1,3},{2,0},{3,1},{4,6},{5,7},{6,4},{7,5},{8,10},{9,11},{10,... | collective-permute-start | bytes 393224 | tf_op jit(solution)/shard_map/ppermute | solution.py:123
  157.5 18.2 %collective-permute-start.23 = (bf16[64,1024]{1,0:T(8,128)(2,1)S(1)}, bf16[64,1024]{1,0:T(8,128)(2,1)}, u32[]{:S(2)}, u32[]{:S(2)}) collective-permute-start(bf16[64,1024]{1,0:T(8,128)(2,1)S(1)} %get-tuple-element.63), channel_id=1, source_target_pairs={{0,3},{1,2},{2,1},{3,0},{4,7},{5,6},{6,5},{7,4},{8,11},{9,10},{10,... | collective-permute-start | bytes 393224 | tf_op jit(solution)/shard_map/ppermute | solution.py:123
  158.9 44.1 %collective-permute-start.20 = (bf16[64,2048]{1,0:T(8,128)(2,1)S(1)}, bf16[64,2048]{1,0:T(8,128)(2,1)S(1)}, u32[]{:S(2)}, u32[]{:S(2)}) collective-permute-start(bf16[64,2048]{1,0:T(8,128)(2,1)S(1)} %fusion.11), channel_id=1, source_target_pairs={{0,0},{1,4},{2,8},{3,12},{4,1},{5,5},{6,9},{7,13},{8,2},{9,6},{10,... | collective-permute-start | bytes 786440 | tf_op jit(solution)/shard_map/ppermute | solution.py:175
  167.7 17.2 %collective-permute-start.25 = (bf16[64,1024]{1,0:T(8,128)(2,1)S(1)}, bf16[64,1024]{1,0:T(8,128)(2,1)S(1)}, u32[]{:S(2)}, u32[]{:S(2)}) collective-permute-start(bf16[64,1024]{1,0:T(8,128)(2,1)S(1)} %get-tuple-element.60), channel_id=1, source_target_pairs={{0,1},{1,0},{2,3},{3,2},{4,5},{5,4},{6,7},{7,6},{8,9},{9,8},{10,11... | collective-permute-start | bytes 393224 | tf_op jit(solution)/shard_map/ppermute | solution.py:123
  167.8 17.2 %collective-permute-start.26 = (bf16[64,1024]{1,0:T(8,128)(2,1)S(1)}, bf16[64,1024]{1,0:T(8,128)(2,1)S(1)}, u32[]{:S(2)}, u32[]{:S(2)}) collective-permute-start(bf16[64,1024]{1,0:T(8,128)(2,1)S(1)} %get-tuple-element.66), channel_id=1, source_target_pairs={{0,2},{1,3},{2,0},{3,1},{4,6},{5,7},{6,4},{7,5},{8,10},{9,11},{10,... | collective-permute-start | bytes 393224 | tf_op jit(solution)/shard_map/ppermute | solution.py:123
  170.7 14.3 %collective-permute-start.27 = (bf16[64,1024]{1,0:T(8,128)(2,1)S(1)}, bf16[64,1024]{1,0:T(8,128)(2,1)S(1)}, u32[]{:S(2)}, u32[]{:S(2)}) collective-permute-start(bf16[64,1024]{1,0:T(8,128)(2,1)S(1)} %get-tuple-element.67), channel_id=1, source_target_pairs={{0,3},{1,2},{2,1},{3,0},{4,7},{5,6},{6,5},{7,4},{8,11},{9,10},{10,... | collective-permute-start | bytes 393224 | tf_op jit(solution)/shard_map/ppermute | solution.py:123
  176.7 22.1 %collective-permute-start.24 = (bf16[64,1024]{1,0:T(8,128)(2,1)S(1)}, bf16[64,1024]{1,0:T(8,128)(2,1)S(1)}, u32[]{:S(2)}, u32[]{:S(2)}) collective-permute-start(bf16[64,1024]{1,0:T(8,128)(2,1)S(1)} %add_convert_fusion.1), channel_id=1, source_target_pairs={{0,0},{1,4},{2,8},{3,12},{4,1},{5,5},{6,9},{7,13},{8,2},{9,6},{10,... | collective-permute-start | bytes 393224 | tf_op jit(solution)/shard_map/ppermute | solution.py:175
  185.1 17.9 %collective-permute-start.28 = (bf16[64,1024]{1,0:T(8,128)(2,1)S(1)}, bf16[64,1024]{1,0:T(8,128)(2,1)S(1)}, u32[]{:S(2)}, u32[]{:S(2)}) collective-permute-start(bf16[64,1024]{1,0:T(8,128)(2,1)S(1)} %add_convert_fusion), channel_id=1, source_target_pairs={{0,0},{1,4},{2,8},{3,12},{4,1},{5,5},{6,9},{7,13},{8,2},{9,6},{10,... | collective-permute-start | bytes 393224 | tf_op jit(solution)/shard_map/ppermute | solution.py:175

commit v5 on v4

--- a/solution.py
+++ b/solution.py
@@ -84,7 +84,7 @@
             outs[0][j ^ td_ref[1]] = acc[j * rows : (j + 1) * rows].astype(BF16)
     else:
         for j in (1, 2, 3):
-            outs[j - 1][...] = acc[j * rows : (j + 1) * rows].astype(BF16)
+            outs[j - 1][...] = acc[j * rows : (j + 1) * rows].astype(outs[j - 1].dtype)
 
 
 def down(td, hidden, down_weight, part, parts, stacked, tile=512):
@@ -95,7 +95,7 @@
     weight = pl.BlockSpec((depth, tile), lambda i, td: (0, first + i))
     out = pl.BlockSpec((rows, tile), lambda i, td: (0, i))
     stack = pl.BlockSpec((4, rows, tile), lambda i, td: (0, 0, i))
-    sent = [(4, rows, width)] if stacked else [(rows, width)] * 3
+    sent = [((4, rows, width), BF16)] if stacked else [((rows, width), t) for t in (BF16, F32, BF16)]
     return pl.pallas_call(
         down_kernel,
         grid_spec=pltpu.PrefetchScalarGridSpec(
@@ -106,7 +106,7 @@
             scratch_shapes=[pltpu.VMEM((4 * rows, depth), BF16)],
         ),
         out_shape=[jax.ShapeDtypeStruct((rows, width), F32)]
-        + [jax.ShapeDtypeStruct(shape, BF16) for shape in sent],
+        + [jax.ShapeDtypeStruct(*each) for each in sent],
         compiler_params=pltpu.CompilerParams(vmem_limit_bytes=40 << 20),
         cost_estimate=pl.CostEstimate(flops=1_000_000, bytes_accessed=1_000_000, transcendentals=0),
         name="down",
@@ -123,6 +123,7 @@
     swap = lambda x, axis, mask: lax.ppermute(x, axis, xor_perm(4, mask))
     after = lambda x, *earlier: lax.optimization_barrier((x, *earlier))[0]
     mine, blocks, keep, send, near, across, hidden, partial, got, outs = ({} for _ in range(10))
+    kept, passed = {}, {}
     tick = [td]
 
     def turn_in(c):
@@ -163,8 +164,15 @@
             arrived = lax.all_to_all(sent[0], "tensor", 0, 0, tiled=True)
             got[c, h] = [(arrived[j], t == j) for j in range(4)]
         else:
-            got[c, h] = [(swap(sent[j - 1], "tensor", j), None) for j in (1, 2, 3)]
+            kept[h] = sent[1]
+            got[c, h] = [(swap(sent[0], "tensor", 1), None)]
+            passed[h] = swap(sent[2], "tensor", 1)
         tick[:] = [sent[0]]
+
+    def pass_on(c, h):
+        summed = (after(kept[h], *tick) + passed[h].astype(F32)).astype(BF16)
+        got[c, h].append((swap(summed, "tensor", 2), None))
+        tick[:] = [summed]
 
     def mix(c, h):
         mixed = after(partial[c, h], *tick)
@@ -192,6 +200,8 @@
     second(1, 0, 2)
     mix(0, 0)
     second(1, 1, 2)
+    pass_on(1, 0)
+    pass_on(1, 1)
     mix(1, 0)
     mix(1, 1)
     last = jnp.concatenate([outs[1, 0], outs[1, 1]], axis=1)

time: 204 us -> 200 us (0.980)
  starting transfers between devices: 72.5 us -> 51.7 us
  waiting for transfers between devices: 71.2 us -> 87 us
    ppermute x3, starting transfers between devices: 24.9 us -> 8.95 us  [mix(): outs[c, h] = lax.ppermute(mixed, ('dp', 'tensor'), turn)]
    ppermute x24, waiting for transfers between devices: 46.8 us -> 57.8 us  [per_device(): swap = lambda x, axis, mask: lax.ppermute(x, axis, xor_perm(4, mask))]
    ppermute x24, starting transfers between devices: 36.7 us -> 31.8 us  [per_device(): swap = lambda x, axis, mask: lax.ppermute(x, axis, xor_perm(4, mask))]
    ppermute x3, waiting for transfers between devices: 4.72 us -> 9.47 us  [mix(): outs[c, h] = lax.ppermute(mixed, ('dp', 'tensor'), turn)]
  transfers between devices with their start and end apart: 30 -> 30, of which waited for: 15 -> 17; matrix products, arithmetic and copies ran while one was open for 4% -> 4% of each run, Pallas kernels for 25% -> 25%
where the time goes in v5:
time: 200 us; the launch traced here: 199 us
  waiting for transfers between devices  87 us (44%)
  starting transfers between devices  51.7 us (26%)
  Pallas kernels  50.1 us (25%)
  other arithmetic  8.08 us (4%)
    ppermute x24, waiting for transfers between devices, per_device(): swap = lambda x, axis, mask: lax.ppermute(x, axis, xor_perm(4, mask))  57.8 us
    ppermute x24, starting transfers between devices, per_device(): swap = lambda x, axis, mask: lax.ppermute(x, axis, xor_perm(4, mask))  31.8 us
    pallas_call x2, Pallas kernels, gate_up(): pl.pallas_call(gate_up_kernel, grid_spec=pltpu.PrefetchScalarGridSpec(num...  29.1 us
    pallas_call x3, Pallas kernels, down(): pl.pallas_call(down_kernel, grid_spec=pltpu.PrefetchScalarGridSpec(num_sc...  21 us
    ppermute x2, waiting for transfers between devices, turn_in(): lax.ppermute(x if c == 0 else after(x, mine[c - 1]), ('dp', 'tensor'), turn)  19.7 us
    ppermute x3, waiting for transfers between devices, mix(): outs[c, h] = lax.ppermute(mixed, ('dp', 'tensor'), turn)  9.47 us
    ppermute x3, starting transfers between devices, mix(): outs[c, h] = lax.ppermute(mixed, ('dp', 'tensor'), turn)  8.95 us
    ppermute x2, starting transfers between devices, turn_in(): lax.ppermute(x if c == 0 else after(x, mine[c - 1]), ('dp', 'tensor'), turn)  6.38 us
  transfers between devices with their start and end apart: 30, of which 17 were waited for; matrix products, arithmetic and copies ran while one was open for 4% of the time, Pallas kernels for 25%

profile of v5, /device:TPU:2, one launch (start us, length us, event | category | flops | bytes accessed | tf_op | source)
XLA Modules:
  0.0 198.8 jit_solution(12137503083951236722)
XLA Ops:
  1.1 4.5 %collective-permute-start = (bf16[64,2048]{1,0:T(8,128)(2,1)S(1)}, bf16[64,2048]{1,0:T(8,128)(2,1)S(1)}, u32[]{:S(2)}, u32[]{:S(2)}) collective-permute-start(bf16[64,2048]{1,0:T(8,128)(2,1)S(1)} %get-tuple-element.72), channel_id=1, source_target_pairs={{0,0},{1,4},{2,8},{3,12},{4,1},{5,5},{6,9},{7,13},{8,2},{9,6},{10,... | collective-permute-start | bytes 786440 | tf_op jit(solution)/shard_map/ppermute | solution.py:131
  5.5 13.6 %collective-permute-done.refs_0_ = bf16[64,2048]{1,0:T(8,128)(2,1)S(1)} collective-permute-done((bf16[64,2048]{1,0:T(8,128)(2,1)S(1)}, bf16[64,2048]{1,0:T(8,128)(2,1)S(1)}, u32[]{:S(2)}, u32[]{:S(2)}) %collective-permute-start) | collective-permute-done | bytes 262176 | tf_op jit(solution)/shard_map/ppermute | solution.py:131
  19.1 1.9 collective-permute-start.1
  21.0 4.3 %collective-permute-start.2 = (bf16[64,2048]{1,0:T(8,128)(2,1)S(1)}, bf16[64,2048]{1,0:T(8,128)(2,1)S(1)}, u32[]{:S(2)}, u32[]{:S(2)}) collective-permute-start(bf16[64,2048]{1,0:T(8,128)(2,1)S(1)} %collective-permute-done.refs_0_), channel_id=1, source_target_pairs={{0,1},{1,0},{2,3},{3,2},{4,5},{5,4},{6,7},{7,6},{8,9},{9,8},{10,11... | collective-permute-start | bytes 786440 | tf_op jit(solution)/shard_map/ppermute | solution.py:123
  25.4 6.7 %collective-permute-done.3.refs_2_ = bf16[64,2048]{1,0:T(8,128)(2,1)S(1)} collective-permute-done((bf16[64,2048]{1,0:T(8,128)(2,1)S(1)}, bf16[64,2048]{1,0:T(8,128)(2,1)S(1)}, u32[]{:S(2)}, u32[]{:S(2)}) %collective-permute-start.3) | collective-permute-done | bytes 262176 | tf_op jit(solution)/shard_map/ppermute | solution.py:123
  32.1 3.4 %collective-permute-start.4 = (bf16[64,2048]{1,0:T(8,128)(2,1)S(1)}, bf16[64,2048]{1,0:T(8,128)(2,1)S(1)}, u32[]{:S(2)}, u32[]{:S(2)}) collective-permute-start(bf16[64,2048]{1,0:T(8,128)(2,1)S(1)} %collective-permute-done.3.refs_2_), channel_id=1, source_target_pairs={{0,1},{1,0},{2,3},{3,2},{4,5},{5,4},{6,7},{7,6},{8,9},{9,8},{10,11... | collective-permute-start | bytes 786440 | tf_op jit(solution)/shard_map/ppermute | solution.py:123
  35.5 6.1 %collective-permute-done.1.refs_0_ = bf16[64,2048]{1,0:T(8,128)(2,1)S(1)} collective-permute-done((bf16[64,2048]{1,0:T(8,128)(2,1)S(1)}, bf16[64,2048]{1,0:T(8,128)(2,1)S(1)}, u32[]{:S(2)}, u32[]{:S(2)}) %collective-permute-start.1) | collective-permute-done | bytes 262176 | tf_op jit(solution)/shard_map/ppermute | solution.py:131
  41.6 4.8 %collective-permute-start.6 = (bf16[64,2048]{1,0:T(8,128)(2,1)S(1)}, bf16[64,2048]{1,0:T(8,128)(2,1)S(1)}, u32[]{:S(2)}, u32[]{:S(2)}) collective-permute-start(bf16[64,2048]{1,0:T(8,128)(2,1)S(1)} %collective-permute-done.1.refs_0_), channel_id=1, source_target_pairs={{0,2},{1,3},{2,0},{3,1},{4,6},{5,7},{6,4},{7,5},{8,10},{9,11},{10,... | collective-permute-start | bytes 786440 | tf_op jit(solution)/shard_map/ppermute | solution.py:123
  46.4 2.5 %collective-permute-start.5 = (bf16[64,2048]{1,0:T(8,128)(2,1)S(1)}, bf16[64,2048]{1,0:T(8,128)(2,1)S(1)}, u32[]{:S(2)}, u32[]{:S(2)}) collective-permute-start(bf16[64,2048]{1,0:T(8,128)(2,1)S(1)} %collective-permute-done.1.refs_0_), channel_id=1, source_target_pairs={{0,1},{1,0},{2,3},{3,2},{4,5},{5,4},{6,7},{7,6},{8,9},{9,8},{10,11... | collective-permute-start | bytes 786440 | tf_op jit(solution)/shard_map/ppermute | solution.py:123
  48.9 14.6 %gate_up.2 = (f32[2,2,64,4096]{3,2,1,0:T(8,128)S(1)}, bf16[2,64,4096]{2,1,0:T(8,128)(2,1)S(1)}, bf16[2,64,4096]{2,1,0:T(8,128)(2,1)S(1)}) custom-call(s32[1]{0:T(128)} %bitcast.td_ref, bf16[64,2048]{1,0:T(8,128)(2,1)S(1)} %collective-permute-done.refs_0_, bf16[64,2048]{1,0:T(8,128)(2,1)S(1)} %collective-permute-done.2.refs_1_, ...), custom_call_target="tpu_custom_call" | custom-call | flops 20000000 | bytes 20000000 | tf_op jit(solution)/shard_map/gate_up/pallas_call | solution.py:50
  65.3 2.2 %collective-permute-done.7 = bf16[2,64,4096]{2,1,0:T(8,128)(2,1)S(1)} collective-permute-done((bf16[2,64,4096]{2,1,0:T(8,128)(2,1)S(1)}, bf16[2,64,4096]{2,1,0:T(8,128)(2,1)S(1)}, u32[]{:S(2)}, u32[]{:S(2)}) %collective-permute-start.7) | collective-permute-done | bytes 1048608 | tf_op jit(solution)/shard_map/ppermute | solution.py:123
  68.9 2.1 %collective-permute-start.8 = (bf16[64,2048]{1,0:T(8,128)(2,1)S(1)}, bf16[64,2048]{1,0:T(8,128)(2,1)S(1)}, u32[]{:S(2)}, u32[]{:S(2)}) collective-permute-start(bf16[64,2048]{1,0:T(8,128)(2,1)S(1)} %collective-permute-done.6.refs_2_), channel_id=1, source_target_pairs={{0,1},{1,0},{2,3},{3,2},{4,5},{5,4},{6,7},{7,6},{8,9},{9,8},{10,11... | collective-permute-start | bytes 786440 | tf_op jit(solution)/shard_map/ppermute | solution.py:123
  71.2 6.2 %collective-permute-done.8.refs_3_ = bf16[64,2048]{1,0:T(8,128)(2,1)S(1)} collective-permute-done((bf16[64,2048]{1,0:T(8,128)(2,1)S(1)}, bf16[64,2048]{1,0:T(8,128)(2,1)S(1)}, u32[]{:S(2)}, u32[]{:S(2)}) %collective-permute-start.8) | collective-permute-done | bytes 262176 | tf_op jit(solution)/shard_map/ppermute | solution.py:123
  77.4 14.6 %gate_up.3 = (f32[2,2,64,4096]{3,2,1,0:T(8,128)S(1)}, bf16[2,64,4096]{2,1,0:T(8,128)(2,1)S(1)}, bf16[2,64,4096]{2,1,0:T(8,128)(2,1)S(1)}) custom-call(s32[1]{0:T(128)} %bitcast.td_ref, bf16[64,2048]{1,0:T(8,128)(2,1)S(1)} %collective-permute-done.1.refs_0_, bf16[64,2048]{1,0:T(8,128)(2,1)S(1)} %collective-permute-done.5.refs_1_, ...), custom_call_target="tpu_custom_call" | custom-call | flops 20000000 | bytes 20000000 | tf_op jit(solution)/shard_map/gate_up/pallas_call | solution.py:50
  98.1 10.5 %collective-permute-done.13.h2 = bf16[64,4096]{1,0:T(8,128)(2,1)S(1)} collective-permute-done((bf16[64,4096]{1,0:T(8,128)(2,1)S(1)}, bf16[64,4096]{1,0:T(8,128)(2,1)S(1)}, u32[]{:S(2)}, u32[]{:S(2)}) %collective-permute-start.13) | collective-permute-done | bytes 524320 | tf_op jit(solution)/shard_map/ppermute | solution.py:123
  110.5 10.1 %down.3 = (f32[64,2048]{1,0:T(8,128)S(1)}, bf16[4,64,2048]{2,1,0:T(8,128)(2,1)}) custom-call(s32[2]{0:T(128)S(1)} %pad_add_fusion.td_ref, bf16[64,4096]{1,0:T(8,128)(2,1)S(1)} %fusion.10.h0, bf16[64,4096]{1,0:T(8,128)(2,1)S(1)} %collective-permute-done.12.h1, bf16[64,4096]{1,0:T(8,128)(2,1)S(1)} %collective-permute-done.13.h2, ...), custom_call_target="tpu_custom_call" | custom-call | flops 1000000 | bytes 1000000 | tf_op jit(solution)/shard_map/down/pallas_call | solution.py:99
  120.6 4.6 %all-to-all-start = ((bf16[4,64,2048]{2,1,0:T(8,128)(2,1)}), bf16[4,64,2048]{2,1,0:T(8,128)(2,1)}, u32[]{:S(2)}, u32[]{:S(2)}) async-start(bf16[4,64,2048]{2,1,0:T(8,128)(2,1)} %get-tuple-element.55), calls=%async_computation | async-start | bytes 2097152 | tf_op jit(solution)/shard_map/all_to_all | solution.py:164
  125.2 4.5 %collective-permute-done.16 = bf16[2,64,4096]{2,1,0:T(8,128)(2,1)} collective-permute-done((bf16[2,64,4096]{2,1,0:T(8,128)(2,1)}, bf16[2,64,4096]{2,1,0:T(8,128)(2,1)}, u32[]{:S(2)}, u32[]{:S(2)}) %collective-permute-start.16) | collective-permute-done | bytes 1048608 | tf_op jit(solution)/shard_map/ppermute | solution.py:123
  129.7 2.6 %fusion.2 = f32[2,64,4096]{2,1,0:T(8,128)S(1)} fusion(bf16[2,64,4096]{2,1,0:T(8,128)(2,1)} %collective-permute-done.16, bf16[2,64,4096]{2,1,0:T(8,128)(2,1)} %collective-permute-done.15, f32[2,2,64,4096]{3,2,1,0:T(8,128)} %copy-done), kind=kLoop, calls=%fused_computation.4 | loop fusion | flops 2097152 | bytes 6291456 | tf_op jit(solution)/shard_map/add | solution.py:154
  133.8 11.3 %collective-permute-done.18.h2 = bf16[64,4096]{1,0:T(8,128)(2,1)S(1)} collective-permute-done((bf16[64,4096]{1,0:T(8,128)(2,1)S(1)}, bf16[64,4096]{1,0:T(8,128)(2,1)S(1)}, u32[]{:S(2)}, u32[]{:S(2)}) %collective-permute-start.18) | collective-permute-done | bytes 524320 | tf_op jit(solution)/shard_map/ppermute | solution.py:123
  147.1 5.4 %down.4 = (f32[64,1024]{1,0:T(8,128)S(1)}, bf16[64,1024]{1,0:T(8,128)(2,1)S(1)}, f32[64,1024]{1,0:T(8,128)S(1)}, bf16[64,1024]{1,0:T(8,128)(2,1)S(1)}) custom-call(s32[2]{0:T(128)S(1)} %pad_add_fusion.td_ref, bf16[64,4096]{1,0:T(8,128)(2,1)S(1)} %fusion.7.h0, bf16[64,4096]{1,0:T(8,128)(2,1)S(1)} %collective-permute-done.17.h1, ...), custom_call_target="tpu_custom_call" | custom-call | flops 1000000 | bytes 1000000 | tf_op jit(solution)/shard_map/down/pallas_call | solution.py:99
  152.5 2.0 %collective-permute-start.23 = (bf16[64,1024]{1,0:T(8,128)(2,1)S(1)}, bf16[64,1024]{1,0:T(8,128)(2,1)S(1)}, u32[]{:S(2)}, u32[]{:S(2)}) collective-permute-start(bf16[64,1024]{1,0:T(8,128)(2,1)S(1)} %get-tuple-element.58), channel_id=1, source_target_pairs={{0,1},{1,0},{2,3},{3,2},{4,5},{5,4},{6,7},{7,6},{8,9},{9,8},{10,11... | collective-permute-start | bytes 393224 | tf_op jit(solution)/shard_map/ppermute | solution.py:123
  156.1 4.8 %collective-permute-start.20 = (bf16[64,2048]{1,0:T(8,128)(2,1)S(1)}, bf16[64,2048]{1,0:T(8,128)(2,1)S(1)}, u32[]{:S(2)}, u32[]{:S(2)}) collective-permute-start(bf16[64,2048]{1,0:T(8,128)(2,1)S(1)} %fusion.11), channel_id=1, source_target_pairs={{0,0},{1,4},{2,8},{3,12},{4,1},{5,5},{6,9},{7,13},{8,2},{9,6},{10,... | collective-permute-start | bytes 786440 | tf_op jit(solution)/shard_map/ppermute | solution.py:183
  160.8 5.5 %down.5 = (f32[64,1024]{1,0:T(8,128)S(1)}, bf16[64,1024]{1,0:T(8,128)(2,1)S(1)}, f32[64,1024]{1,0:T(8,128)S(1)}, bf16[64,1024]{1,0:T(8,128)(2,1)S(1)}) custom-call(s32[2]{0:T(128)S(1)} %pad_add_fusion.td_ref, bf16[64,4096]{1,0:T(8,128)(2,1)S(1)} %fusion.7.h0, bf16[64,4096]{1,0:T(8,128)(2,1)S(1)} %collective-permute-done.17.h1, ...), custom_call_target="tpu_custom_call" | custom-call | flops 1000000 | bytes 1000000 | tf_op jit(solution)/shard_map/down/pallas_call | solution.py:99
  166.4 2.0 %collective-permute-start.22 = (bf16[64,1024]{1,0:T(8,128)(2,1)S(1)}, bf16[64,1024]{1,0:T(8,128)(2,1)S(1)}, u32[]{:S(2)}, u32[]{:S(2)}) collective-permute-start(bf16[64,1024]{1,0:T(8,128)(2,1)S(1)} %get-tuple-element.68), channel_id=1, source_target_pairs={{0,1},{1,0},{2,3},{3,2},{4,5},{5,4},{6,7},{7,6},{8,9},{9,8},{10,11... | collective-permute-start | bytes 393224 | tf_op jit(solution)/shard_map/ppermute | solution.py:123
  169.5 7.2 %collective-permute-done.22 = bf16[64,1024]{1,0:T(8,128)(2,1)S(1)} collective-permute-done((bf16[64,1024]{1,0:T(8,128)(2,1)S(1)}, bf16[64,1024]{1,0:T(8,128)(2,1)S(1)}, u32[]{:S(2)}, u32[]{:S(2)}) %collective-permute-start.22) | collective-permute-done | bytes 131104 | tf_op jit(solution)/shard_map/ppermute | solution.py:123
  176.7 3.7 %collective-permute-start.27 = (bf16[64,1024]{1,0:T(8,128)(2,1)S(1)}, bf16[64,1024]{1,0:T(8,128)(2,1)S(1)}, u32[]{:S(2)}, u32[]{:S(2)}) collective-permute-start(bf16[64,1024]{1,0:T(8,128)(2,1)S(1)} %add_convert_fusion.2), channel_id=1, source_target_pairs={{0,2},{1,3},{2,0},{3,1},{4,6},{5,7},{6,4},{7,5},{8,10},{9,11},{10,... | collective-permute-start | bytes 393224 | tf_op jit(solution)/shard_map/ppermute | solution.py:123
  180.4 2.3 %collective-permute-start.25 = (bf16[64,1024]{1,0:T(8,128)(2,1)S(1)}, bf16[64,1024]{1,0:T(8,128)(2,1)S(1)}, u32[]{:S(2)}, u32[]{:S(2)}) collective-permute-start(bf16[64,1024]{1,0:T(8,128)(2,1)S(1)} %add_convert_fusion.1), channel_id=1, source_target_pairs={{0,0},{1,4},{2,8},{3,12},{4,1},{5,5},{6,9},{7,13},{8,2},{9,6},{10,... | collective-permute-start | bytes 393224 | tf_op jit(solution)/shard_map/ppermute | solution.py:183
  182.7 3.8 %collective-permute-done.27 = bf16[64,1024]{1,0:T(8,128)(2,1)S(1)} collective-permute-done((bf16[64,1024]{1,0:T(8,128)(2,1)S(1)}, bf16[64,1024]{1,0:T(8,128)(2,1)S(1)}, u32[]{:S(2)}, u32[]{:S(2)}) %collective-permute-start.27) | collective-permute-done | bytes 131104 | tf_op jit(solution)/shard_map/ppermute | solution.py:123
  186.6 1.9 collective-permute-start.28
  188.5 6.1 %collective-permute-done.25 = bf16[64,1024]{1,0:T(8,128)(2,1)S(1)} collective-permute-done((bf16[64,1024]{1,0:T(8,128)(2,1)S(1)}, bf16[64,1024]{1,0:T(8,128)(2,1)S(1)}, u32[]{:S(2)}, u32[]{:S(2)}) %collective-permute-start.25) | collective-permute-done | bytes 131104 | tf_op jit(solution)/shard_map/ppermute | solution.py:183
  194.6 3.4 %collective-permute-done.28 = bf16[64,1024]{1,0:T(8,128)(2,1)S(1)} collective-permute-done((bf16[64,1024]{1,0:T(8,128)(2,1)S(1)}, bf16[64,1024]{1,0:T(8,128)(2,1)S(1)}, u32[]{:S(2)}, u32[]{:S(2)}) %collective-permute-start.28) | collective-permute-done | bytes 131104 | tf_op jit(solution)/shard_map/ppermute | solution.py:183
  (56 shorter events, 19.0 us)
Async XLA Ops:
  1.1 18.0 %collective-permute-start = (bf16[64,2048]{1,0:T(8,128)(2,1)S(1)}, bf16[64,2048]{1,0:T(8,128)(2,1)S(1)}, u32[]{:S(2)}, u32[]{:S(2)}) collective-permute-start(bf16[64,2048]{1,0:T(8,128)(2,1)S(1)} %get-tuple-element.72), channel_id=1, source_target_pairs={{0,0},{1,4},{2,8},{3,12},{4,1},{5,5},{6,9},{7,13},{8,2},{9,6},{10,... | collective-permute-start | bytes 786440 | tf_op jit(solution)/shard_map/ppermute | solution.py:131
  19.1 13.0 %collective-permute-start.3 = (bf16[64,2048]{1,0:T(8,128)(2,1)S(1)}, bf16[64,2048]{1,0:T(8,128)(2,1)S(1)}, u32[]{:S(2)}, u32[]{:S(2)}) collective-permute-start(bf16[64,2048]{1,0:T(8,128)(2,1)S(1)} %collective-permute-done.refs_0_), channel_id=1, source_target_pairs={{0,2},{1,3},{2,0},{3,1},{4,6},{5,7},{6,4},{7,5},{8,10},{9,11},{10,... | collective-permute-start | bytes 786440 | tf_op jit(solution)/shard_map/ppermute | solution.py:123
  19.1 22.5 %collective-permute-start.1 = (bf16[64,2048]{1,0:T(8,128)(2,1)S(1)}, bf16[64,2048]{1,0:T(8,128)(2,1)S(1)}, u32[]{:S(2)}, u32[]{:S(2)}) collective-permute-start(bf16[64,2048]{1,0:T(8,128)(2,1)S(1)} %get-tuple-element.39), channel_id=1, source_target_pairs={{0,0},{1,4},{2,8},{3,12},{4,1},{5,5},{6,9},{7,13},{8,2},{9,6},{10,... | collective-permute-start | bytes 786440 | tf_op jit(solution)/shard_map/ppermute | solution.py:131
  21.0 20.5 %collective-permute-start.2 = (bf16[64,2048]{1,0:T(8,128)(2,1)S(1)}, bf16[64,2048]{1,0:T(8,128)(2,1)S(1)}, u32[]{:S(2)}, u32[]{:S(2)}) collective-permute-start(bf16[64,2048]{1,0:T(8,128)(2,1)S(1)} %collective-permute-done.refs_0_), channel_id=1, source_target_pairs={{0,1},{1,0},{2,3},{3,2},{4,5},{5,4},{6,7},{7,6},{8,9},{9,8},{10,11... | collective-permute-start | bytes 786440 | tf_op jit(solution)/shard_map/ppermute | solution.py:123
  32.1 9.5 %collective-permute-start.4 = (bf16[64,2048]{1,0:T(8,128)(2,1)S(1)}, bf16[64,2048]{1,0:T(8,128)(2,1)S(1)}, u32[]{:S(2)}, u32[]{:S(2)}) collective-permute-start(bf16[64,2048]{1,0:T(8,128)(2,1)S(1)} %collective-permute-done.3.refs_2_), channel_id=1, source_target_pairs={{0,1},{1,0},{2,3},{3,2},{4,5},{5,4},{6,7},{7,6},{8,9},{9,8},{10,11... | collective-permute-start | bytes 786440 | tf_op jit(solution)/shard_map/ppermute | solution.py:123
  41.6 21.9 %collective-permute-start.6 = (bf16[64,2048]{1,0:T(8,128)(2,1)S(1)}, bf16[64,2048]{1,0:T(8,128)(2,1)S(1)}, u32[]{:S(2)}, u32[]{:S(2)}) collective-permute-start(bf16[64,2048]{1,0:T(8,128)(2,1)S(1)} %collective-permute-done.1.refs_0_), channel_id=1, source_target_pairs={{0,2},{1,3},{2,0},{3,1},{4,6},{5,7},{6,4},{7,5},{8,10},{9,11},{10,... | collective-permute-start | bytes 786440 | tf_op jit(solution)/shard_map/ppermute | solution.py:123
  46.4 17.1 %collective-permute-start.5 = (bf16[64,2048]{1,0:T(8,128)(2,1)S(1)}, bf16[64,2048]{1,0:T(8,128)(2,1)S(1)}, u32[]{:S(2)}, u32[]{:S(2)}) collective-permute-start(bf16[64,2048]{1,0:T(8,128)(2,1)S(1)} %collective-permute-done.1.refs_0_), channel_id=1, source_target_pairs={{0,1},{1,0},{2,3},{3,2},{4,5},{5,4},{6,7},{7,6},{8,9},{9,8},{10,11... | collective-permute-start | bytes 786440 | tf_op jit(solution)/shard_map/ppermute | solution.py:123
  63.5 4.0 %collective-permute-start.7 = (bf16[2,64,4096]{2,1,0:T(8,128)(2,1)S(1)}, bf16[2,64,4096]{2,1,0:T(8,128)(2,1)S(1)}, u32[]{:S(2)}, u32[]{:S(2)}) collective-permute-start(bf16[2,64,4096]{2,1,0:T(8,128)(2,1)S(1)} %get-tuple-element.45), channel_id=1, source_target_pairs={{0,4},{4,0},{8,12},{12,8},{1,5},{5,1},{9,13},{13,9},{2,6},{6,2},{1... | collective-permute-start | bytes 3145736 | tf_op jit(solution)/shard_map/ppermute | solution.py:123
  65.2 3.7 %copy-start.1 = (s32[32]{0:T(128)S(1)}, s32[32]{0:T(128)}, u32[]{:S(2)}) copy-start(s32[32]{0:T(128)} %param.10) | copy-start | bytes 388
  65.2 27.3 %collective-permute-start.9 = (bf16[2,64,4096]{2,1,0:T(8,128)(2,1)S(1)}, bf16[2,64,4096]{2,1,0:T(8,128)(2,1)S(1)}, u32[]{:S(2)}, u32[]{:S(2)}) collective-permute-start(bf16[2,64,4096]{2,1,0:T(8,128)(2,1)S(1)} %get-tuple-element.51), channel_id=1, source_target_pairs={{0,4},{4,0},{8,12},{12,8},{1,5},{5,1},{9,13},{13,9},{2,6},{6,2},{1... | collective-permute-start | bytes 3145736 | tf_op jit(solution)/shard_map/ppermute | solution.py:123
  67.7 25.5 %collective-permute-start.10 = (bf16[2,64,4096]{2,1,0:T(8,128)(2,1)S(1)}, bf16[2,64,4096]{2,1,0:T(8,128)(2,1)S(1)}, u32[]{:S(2)}, u32[]{:S(2)}) collective-permute-start(bf16[2,64,4096]{2,1,0:T(8,128)(2,1)S(1)} %fusion.1), channel_id=1, source_target_pairs={{0,8},{4,12},{8,0},{12,4},{1,9},{5,13},{9,1},{13,5},{2,10},{6,14},... | collective-permute-start | bytes 3145736 | tf_op jit(solution)/shard_map/ppermute | solution.py:123
  68.9 8.4 %collective-permute-start.8 = (bf16[64,2048]{1,0:T(8,128)(2,1)S(1)}, bf16[64,2048]{1,0:T(8,128)(2,1)S(1)}, u32[]{:S(2)}, u32[]{:S(2)}) collective-permute-start(bf16[64,2048]{1,0:T(8,128)(2,1)S(1)} %collective-permute-done.6.refs_2_), channel_id=1, source_target_pairs={{0,1},{1,0},{2,3},{3,2},{4,5},{5,4},{6,7},{7,6},{8,9},{9,8},{10,11... | collective-permute-start | bytes 786440 | tf_op jit(solution)/shard_map/ppermute | solution.py:123
  91.9 3.4 %copy-start = (f32[2,2,64,4096]{3,2,1,0:T(8,128)}, f32[2,2,64,4096]{3,2,1,0:T(8,128)S(1)}, u32[]{:S(2)}) copy-start(f32[2,2,64,4096]{3,2,1,0:T(8,128)S(1)} %get-tuple-element.56) | copy-start | bytes 12582916
  91.9 3.4 %collective-permute-start.11 = (bf16[2,64,4096]{2,1,0:T(8,128)(2,1)S(1)}, bf16[2,64,4096]{2,1,0:T(8,128)(2,1)S(1)}, u32[]{:S(2)}, u32[]{:S(2)}) collective-permute-start(bf16[2,64,4096]{2,1,0:T(8,128)(2,1)S(1)} %get-tuple-element.49), channel_id=1, source_target_pairs={{0,4},{4,0},{8,12},{12,8},{1,5},{5,1},{9,13},{13,9},{2,6},{6,2},{1... | collective-permute-start | bytes 3145736 | tf_op jit(solution)/shard_map/ppermute | solution.py:123
  92.0 33.2 %collective-permute-start.15 = (bf16[2,64,4096]{2,1,0:T(8,128)(2,1)S(1)}, bf16[2,64,4096]{2,1,0:T(8,128)(2,1)}, u32[]{:S(2)}, u32[]{:S(2)}) collective-permute-start(bf16[2,64,4096]{2,1,0:T(8,128)(2,1)S(1)} %get-tuple-element.48), channel_id=1, source_target_pairs={{0,4},{4,0},{8,12},{12,8},{1,5},{5,1},{9,13},{13,9},{2,6},{6,2},{1... | collective-permute-start | bytes 3145736 | tf_op jit(solution)/shard_map/ppermute | solution.py:123
  93.7 14.9 %collective-permute-start.13 = (bf16[64,4096]{1,0:T(8,128)(2,1)S(1)}, bf16[64,4096]{1,0:T(8,128)(2,1)S(1)}, u32[]{:S(2)}, u32[]{:S(2)}) collective-permute-start(bf16[64,4096]{1,0:T(8,128)(2,1)S(1)} %fusion.10.h0), channel_id=1, source_target_pairs={{0,8},{4,12},{8,0},{12,4},{1,9},{5,13},{9,1},{13,5},{2,10},{6,14},... | collective-permute-start | bytes 1572872 | tf_op jit(solution)/shard_map/ppermute | solution.py:123
  96.6 33.1 %collective-permute-start.16 = (bf16[2,64,4096]{2,1,0:T(8,128)(2,1)}, bf16[2,64,4096]{2,1,0:T(8,128)(2,1)}, u32[]{:S(2)}, u32[]{:S(2)}) collective-permute-start(bf16[2,64,4096]{2,1,0:T(8,128)(2,1)} %fusion.3), channel_id=1, source_target_pairs={{0,8},{4,12},{8,0},{12,4},{1,9},{5,13},{9,1},{13,5},{2,10},{6,14},... | collective-permute-start | bytes 3145736 | tf_op jit(solution)/shard_map/ppermute | solution.py:123
  98.1 10.6 %collective-permute-start.12 = (bf16[64,4096]{1,0:T(8,128)(2,1)S(1)}, bf16[64,4096]{1,0:T(8,128)(2,1)S(1)}, u32[]{:S(2)}, u32[]{:S(2)}) collective-permute-start(bf16[64,4096]{1,0:T(8,128)(2,1)S(1)} %fusion.10.h0), channel_id=1, source_target_pairs={{0,4},{4,0},{8,12},{12,8},{1,5},{5,1},{9,13},{13,9},{2,6},{6,2},{1... | collective-permute-start | bytes 1572872 | tf_op jit(solution)/shard_map/ppermute | solution.py:123
  108.6 1.9 collective-permute-start.14
  120.6 34.1 %all-to-all-start = ((bf16[4,64,2048]{2,1,0:T(8,128)(2,1)}), bf16[4,64,2048]{2,1,0:T(8,128)(2,1)}, u32[]{:S(2)}, u32[]{:S(2)}) async-start(bf16[4,64,2048]{2,1,0:T(8,128)(2,1)} %get-tuple-element.55), calls=%async_computation | async-start | bytes 2097152 | tf_op jit(solution)/shard_map/all_to_all | solution.py:164
  132.4 12.7 %collective-permute-start.18 = (bf16[64,4096]{1,0:T(8,128)(2,1)S(1)}, bf16[64,4096]{1,0:T(8,128)(2,1)S(1)}, u32[]{:S(2)}, u32[]{:S(2)}) collective-permute-start(bf16[64,4096]{1,0:T(8,128)(2,1)S(1)} %fusion.7.h0), channel_id=1, source_target_pairs={{0,8},{4,12},{8,0},{12,4},{1,9},{5,13},{9,1},{13,5},{2,10},{6,14},... | collective-permute-start | bytes 1572872 | tf_op jit(solution)/shard_map/ppermute | solution.py:123
  133.8 11.3 %collective-permute-start.17 = (bf16[64,4096]{1,0:T(8,128)(2,1)S(1)}, bf16[64,4096]{1,0:T(8,128)(2,1)S(1)}, u32[]{:S(2)}, u32[]{:S(2)}) collective-permute-start(bf16[64,4096]{1,0:T(8,128)(2,1)S(1)} %fusion.7.h0), channel_id=1, source_target_pairs={{0,4},{4,0},{8,12},{12,8},{1,5},{5,1},{9,13},{13,9},{2,6},{6,2},{1... | collective-permute-start | bytes 1572872 | tf_op jit(solution)/shard_map/ppermute | solution.py:123
  145.2 1.9 collective-permute-start.19
  152.5 27.9 %collective-permute-start.23 = (bf16[64,1024]{1,0:T(8,128)(2,1)S(1)}, bf16[64,1024]{1,0:T(8,128)(2,1)S(1)}, u32[]{:S(2)}, u32[]{:S(2)}) collective-permute-start(bf16[64,1024]{1,0:T(8,128)(2,1)S(1)} %get-tuple-element.58), channel_id=1, source_target_pairs={{0,1},{1,0},{2,3},{3,2},{4,5},{5,4},{6,7},{7,6},{8,9},{9,8},{10,11... | collective-permute-start | bytes 393224 | tf_op jit(solution)/shard_map/ppermute | solution.py:123
  154.6 13.8 %collective-permute-start.21 = (bf16[64,1024]{1,0:T(8,128)(2,1)S(1)}, bf16[64,1024]{1,0:T(8,128)(2,1)}, u32[]{:S(2)}, u32[]{:S(2)}) collective-permute-start(bf16[64,1024]{1,0:T(8,128)(2,1)S(1)} %get-tuple-element.66), channel_id=1, source_target_pairs={{0,1},{1,0},{2,3},{3,2},{4,5},{5,4},{6,7},{7,6},{8,9},{9,8},{10,11... | collective-permute-start | bytes 393224 | tf_op jit(solution)/shard_map/ppermute | solution.py:123
  156.1 38.6 %collective-permute-start.20 = (bf16[64,2048]{1,0:T(8,128)(2,1)S(1)}, bf16[64,2048]{1,0:T(8,128)(2,1)S(1)}, u32[]{:S(2)}, u32[]{:S(2)}) collective-permute-start(bf16[64,2048]{1,0:T(8,128)(2,1)S(1)} %fusion.11), channel_id=1, source_target_pairs={{0,0},{1,4},{2,8},{3,12},{4,1},{5,5},{6,9},{7,13},{8,2},{9,6},{10,... | collective-permute-start | bytes 786440 | tf_op jit(solution)/shard_map/ppermute | solution.py:183
  166.3 16.4 %collective-permute-start.26 = (bf16[64,1024]{1,0:T(8,128)(2,1)S(1)}, bf16[64,1024]{1,0:T(8,128)(2,1)S(1)}, u32[]{:S(2)}, u32[]{:S(2)}) collective-permute-start(bf16[64,1024]{1,0:T(8,128)(2,1)S(1)} %get-tuple-element.64), channel_id=1, source_target_pairs={{0,1},{1,0},{2,3},{3,2},{4,5},{5,4},{6,7},{7,6},{8,9},{9,8},{10,11... | collective-permute-start | bytes 393224 | tf_op jit(solution)/shard_map/ppermute | solution.py:123
  166.4 10.3 %collective-permute-start.22 = (bf16[64,1024]{1,0:T(8,128)(2,1)S(1)}, bf16[64,1024]{1,0:T(8,128)(2,1)S(1)}, u32[]{:S(2)}, u32[]{:S(2)}) collective-permute-start(bf16[64,1024]{1,0:T(8,128)(2,1)S(1)} %get-tuple-element.68), channel_id=1, source_target_pairs={{0,1},{1,0},{2,3},{3,2},{4,5},{5,4},{6,7},{7,6},{8,9},{9,8},{10,11... | collective-permute-start | bytes 393224 | tf_op jit(solution)/shard_map/ppermute | solution.py:123
  169.3 11.1 %collective-permute-start.24 = (bf16[64,1024]{1,0:T(8,128)(2,1)S(1)}, bf16[64,1024]{1,0:T(8,128)(2,1)S(1)}, u32[]{:S(2)}, u32[]{:S(2)}) collective-permute-start(bf16[64,1024]{1,0:T(8,128)(2,1)S(1)} %add_convert_fusion.3), channel_id=1, source_target_pairs={{0,2},{1,3},{2,0},{3,1},{4,6},{5,7},{6,4},{7,5},{8,10},{9,11},{10,... | collective-permute-start | bytes 393224 | tf_op jit(solution)/shard_map/ppermute | solution.py:123
  176.7 9.8 %collective-permute-start.27 = (bf16[64,1024]{1,0:T(8,128)(2,1)S(1)}, bf16[64,1024]{1,0:T(8,128)(2,1)S(1)}, u32[]{:S(2)}, u32[]{:S(2)}) collective-permute-start(bf16[64,1024]{1,0:T(8,128)(2,1)S(1)} %add_convert_fusion.2), channel_id=1, source_target_pairs={{0,2},{1,3},{2,0},{3,1},{4,6},{5,7},{6,4},{7,5},{8,10},{9,11},{10,... | collective-permute-start | bytes 393224 | tf_op jit(solution)/shard_map/ppermute | solution.py:123
  180.4 14.2 %collective-permute-start.25 = (bf16[64,1024]{1,0:T(8,128)(2,1)S(1)}, bf16[64,1024]{1,0:T(8,128)(2,1)S(1)}, u32[]{:S(2)}, u32[]{:S(2)}) collective-permute-start(bf16[64,1024]{1,0:T(8,128)(2,1)S(1)} %add_convert_fusion.1), channel_id=1, source_target_pairs={{0,0},{1,4},{2,8},{3,12},{4,1},{5,5},{6,9},{7,13},{8,2},{9,6},{10,... | collective-permute-start | bytes 393224 | tf_op jit(solution)/shard_map/ppermute | solution.py:183
  186.6 11.4 %collective-permute-start.28 = (bf16[64,1024]{1,0:T(8,128)(2,1)S(1)}, bf16[64,1024]{1,0:T(8,128)(2,1)S(1)}, u32[]{:S(2)}, u32[]{:S(2)}) collective-permute-start(bf16[64,1024]{1,0:T(8,128)(2,1)S(1)} %add_convert_fusion), channel_id=1, source_target_pairs={{0,0},{1,4},{2,8},{3,12},{4,1},{5,5},{6,9},{7,13},{8,2},{9,6},{10,... | collective-permute-start | bytes 393224 | tf_op jit(solution)/shard_map/ppermute | solution.py:183

commit v6 on v5

--- a/solution.py
+++ b/solution.py
@@ -165,8 +165,9 @@
             got[c, h] = [(arrived[j], t == j) for j in range(4)]
         else:
             kept[h] = sent[1]
-            got[c, h] = [(swap(sent[0], "tensor", 1), None)]
             passed[h] = swap(sent[2], "tensor", 1)
+            direct = after(sent[0], passed[h]) if h else sent[0]
+            got[c, h] = [(swap(direct, "tensor", 1), None)]
         tick[:] = [sent[0]]
 
     def pass_on(c, h):

time: 200 us -> 198 us (0.990)
  waiting for transfers between devices: 87 us -> 78.5 us
  starting transfers between devices: 51.7 us -> 59.1 us
    ppermute x3, starting transfers between devices: 8.95 us -> 17.5 us  [mix(): outs[c, h] = lax.ppermute(mixed, ('dp', 'tensor'), turn)]
    ppermute x24, waiting for transfers between devices: 57.8 us -> 52 us  [per_device(): swap = lambda x, axis, mask: lax.ppermute(x, axis, xor_perm(4, mask))]
    ppermute x3, waiting for transfers between devices: 9.47 us -> 6.84 us  [mix(): outs[c, h] = lax.ppermute(mixed, ('dp', 'tensor'), turn)]
where the time goes in v6:
time: 198 us
  waiting for transfers between devices  78.5 us (40%)
  starting transfers between devices  59.1 us (30%)
  Pallas kernels  50.1 us (25%)
  other arithmetic  8.08 us (4%)
    ppermute x24, waiting for transfers between devices, per_device(): swap = lambda x, axis, mask: lax.ppermute(x, axis, xor_perm(4, mask))  52 us
    ppermute x24, starting transfers between devices, per_device(): swap = lambda x, axis, mask: lax.ppermute(x, axis, xor_perm(4, mask))  30.6 us
    pallas_call x2, Pallas kernels, gate_up(): pl.pallas_call(gate_up_kernel, grid_spec=pltpu.PrefetchScalarGridSpec(num...  29.1 us
    pallas_call x3, Pallas kernels, down(): pl.pallas_call(down_kernel, grid_spec=pltpu.PrefetchScalarGridSpec(num_sc...  21 us
    ppermute x2, waiting for transfers between devices, turn_in(): lax.ppermute(x if c == 0 else after(x, mine[c - 1]), ('dp', 'tensor'), turn)  19.7 us
    ppermute x3, starting transfers between devices, mix(): outs[c, h] = lax.ppermute(mixed, ('dp', 'tensor'), turn)  17.5 us
    ppermute x3, waiting for transfers between devices, mix(): outs[c, h] = lax.ppermute(mixed, ('dp', 'tensor'), turn)  6.84 us
    ppermute x2, starting transfers between devices, turn_in(): lax.ppermute(x if c == 0 else after(x, mine[c - 1]), ('dp', 'tensor'), turn)  6.38 us
  transfers between devices with their start and end apart: 30, of which 17 were waited for; matrix products, arithmetic and copies ran while one was open for 4% of the time, Pallas kernels for 25%

profile of v6, /device:TPU:2, one launch (start us, length us, event | category | flops | bytes accessed | tf_op | source)
XLA Modules:
  0.0 197.8 jit_solution(12486723071763588811)
XLA Ops:
  1.1 4.5 %collective-permute-start = (bf16[64,2048]{1,0:T(8,128)(2,1)S(1)}, bf16[64,2048]{1,0:T(8,128)(2,1)S(1)}, u32[]{:S(2)}, u32[]{:S(2)}) collective-permute-start(bf16[64,2048]{1,0:T(8,128)(2,1)S(1)} %get-tuple-element.74), channel_id=1, source_target_pairs={{0,0},{1,4},{2,8},{3,12},{4,1},{5,5},{6,9},{7,13},{8,2},{9,6},{10,... | collective-permute-start | bytes 786440 | tf_op jit(solution)/shard_map/ppermute | solution.py:131
  5.5 13.6 %collective-permute-done.refs_0_ = bf16[64,2048]{1,0:T(8,128)(2,1)S(1)} collective-permute-done((bf16[64,2048]{1,0:T(8,128)(2,1)S(1)}, bf16[64,2048]{1,0:T(8,128)(2,1)S(1)}, u32[]{:S(2)}, u32[]{:S(2)}) %collective-permute-start) | collective-permute-done | bytes 262176 | tf_op jit(solution)/shard_map/ppermute | solution.py:131
  19.1 1.9 collective-permute-start.1
  21.0 4.3 %collective-permute-start.2 = (bf16[64,2048]{1,0:T(8,128)(2,1)S(1)}, bf16[64,2048]{1,0:T(8,128)(2,1)S(1)}, u32[]{:S(2)}, u32[]{:S(2)}) collective-permute-start(bf16[64,2048]{1,0:T(8,128)(2,1)S(1)} %collective-permute-done.refs_0_), channel_id=1, source_target_pairs={{0,1},{1,0},{2,3},{3,2},{4,5},{5,4},{6,7},{7,6},{8,9},{9,8},{10,11... | collective-permute-start | bytes 786440 | tf_op jit(solution)/shard_map/ppermute | solution.py:123
  25.4 6.7 %collective-permute-done.3.refs_2_ = bf16[64,2048]{1,0:T(8,128)(2,1)S(1)} collective-permute-done((bf16[64,2048]{1,0:T(8,128)(2,1)S(1)}, bf16[64,2048]{1,0:T(8,128)(2,1)S(1)}, u32[]{:S(2)}, u32[]{:S(2)}) %collective-permute-start.3) | collective-permute-done | bytes 262176 | tf_op jit(solution)/shard_map/ppermute | solution.py:123
  32.1 3.4 %collective-permute-start.4 = (bf16[64,2048]{1,0:T(8,128)(2,1)S(1)}, bf16[64,2048]{1,0:T(8,128)(2,1)S(1)}, u32[]{:S(2)}, u32[]{:S(2)}) collective-permute-start(bf16[64,2048]{1,0:T(8,128)(2,1)S(1)} %collective-permute-done.3.refs_2_), channel_id=1, source_target_pairs={{0,1},{1,0},{2,3},{3,2},{4,5},{5,4},{6,7},{7,6},{8,9},{9,8},{10,11... | collective-permute-start | bytes 786440 | tf_op jit(solution)/shard_map/ppermute | solution.py:123
  35.5 6.1 %collective-permute-done.1.refs_0_ = bf16[64,2048]{1,0:T(8,128)(2,1)S(1)} collective-permute-done((bf16[64,2048]{1,0:T(8,128)(2,1)S(1)}, bf16[64,2048]{1,0:T(8,128)(2,1)S(1)}, u32[]{:S(2)}, u32[]{:S(2)}) %collective-permute-start.1) | collective-permute-done | bytes 262176 | tf_op jit(solution)/shard_map/ppermute | solution.py:131
  41.6 4.8 %collective-permute-start.6 = (bf16[64,2048]{1,0:T(8,128)(2,1)S(1)}, bf16[64,2048]{1,0:T(8,128)(2,1)S(1)}, u32[]{:S(2)}, u32[]{:S(2)}) collective-permute-start(bf16[64,2048]{1,0:T(8,128)(2,1)S(1)} %collective-permute-done.1.refs_0_), channel_id=1, source_target_pairs={{0,2},{1,3},{2,0},{3,1},{4,6},{5,7},{6,4},{7,5},{8,10},{9,11},{10,... | collective-permute-start | bytes 786440 | tf_op jit(solution)/shard_map/ppermute | solution.py:123
  46.4 2.5 %collective-permute-start.5 = (bf16[64,2048]{1,0:T(8,128)(2,1)S(1)}, bf16[64,2048]{1,0:T(8,128)(2,1)S(1)}, u32[]{:S(2)}, u32[]{:S(2)}) collective-permute-start(bf16[64,2048]{1,0:T(8,128)(2,1)S(1)} %collective-permute-done.1.refs_0_), channel_id=1, source_target_pairs={{0,1},{1,0},{2,3},{3,2},{4,5},{5,4},{6,7},{7,6},{8,9},{9,8},{10,11... | collective-permute-start | bytes 786440 | tf_op jit(solution)/shard_map/ppermute | solution.py:123
  48.9 14.6 %gate_up.2 = (f32[2,2,64,4096]{3,2,1,0:T(8,128)S(1)}, bf16[2,64,4096]{2,1,0:T(8,128)(2,1)S(1)}, bf16[2,64,4096]{2,1,0:T(8,128)(2,1)S(1)}) custom-call(s32[1]{0:T(128)} %bitcast.td_ref, bf16[64,2048]{1,0:T(8,128)(2,1)S(1)} %collective-permute-done.refs_0_, bf16[64,2048]{1,0:T(8,128)(2,1)S(1)} %collective-permute-done.2.refs_1_, ...), custom_call_target="tpu_custom_call" | custom-call | flops 20000000 | bytes 20000000 | tf_op jit(solution)/shard_map/gate_up/pallas_call | solution.py:50
  65.3 2.2 %collective-permute-done.7 = bf16[2,64,4096]{2,1,0:T(8,128)(2,1)S(1)} collective-permute-done((bf16[2,64,4096]{2,1,0:T(8,128)(2,1)S(1)}, bf16[2,64,4096]{2,1,0:T(8,128)(2,1)S(1)}, u32[]{:S(2)}, u32[]{:S(2)}) %collective-permute-start.7) | collective-permute-done | bytes 1048608 | tf_op jit(solution)/shard_map/ppermute | solution.py:123
  68.9 2.1 %collective-permute-start.8 = (bf16[64,2048]{1,0:T(8,128)(2,1)S(1)}, bf16[64,2048]{1,0:T(8,128)(2,1)S(1)}, u32[]{:S(2)}, u32[]{:S(2)}) collective-permute-start(bf16[64,2048]{1,0:T(8,128)(2,1)S(1)} %collective-permute-done.6.refs_2_), channel_id=1, source_target_pairs={{0,1},{1,0},{2,3},{3,2},{4,5},{5,4},{6,7},{7,6},{8,9},{9,8},{10,11... | collective-permute-start | bytes 786440 | tf_op jit(solution)/shard_map/ppermute | solution.py:123
  71.2 6.2 %collective-permute-done.8.refs_3_ = bf16[64,2048]{1,0:T(8,128)(2,1)S(1)} collective-permute-done((bf16[64,2048]{1,0:T(8,128)(2,1)S(1)}, bf16[64,2048]{1,0:T(8,128)(2,1)S(1)}, u32[]{:S(2)}, u32[]{:S(2)}) %collective-permute-start.8) | collective-permute-done | bytes 262176 | tf_op jit(solution)/shard_map/ppermute | solution.py:123
  77.4 14.6 %gate_up.3 = (f32[2,2,64,4096]{3,2,1,0:T(8,128)S(1)}, bf16[2,64,4096]{2,1,0:T(8,128)(2,1)S(1)}, bf16[2,64,4096]{2,1,0:T(8,128)(2,1)S(1)}) custom-call(s32[1]{0:T(128)} %bitcast.td_ref, bf16[64,2048]{1,0:T(8,128)(2,1)S(1)} %collective-permute-done.1.refs_0_, bf16[64,2048]{1,0:T(8,128)(2,1)S(1)} %collective-permute-done.5.refs_1_, ...), custom_call_target="tpu_custom_call" | custom-call | flops 20000000 | bytes 20000000 | tf_op jit(solution)/shard_map/gate_up/pallas_call | solution.py:50
  98.1 10.5 %collective-permute-done.13.h2 = bf16[64,4096]{1,0:T(8,128)(2,1)S(1)} collective-permute-done((bf16[64,4096]{1,0:T(8,128)(2,1)S(1)}, bf16[64,4096]{1,0:T(8,128)(2,1)S(1)}, u32[]{:S(2)}, u32[]{:S(2)}) %collective-permute-start.13) | collective-permute-done | bytes 524320 | tf_op jit(solution)/shard_map/ppermute | solution.py:123
  110.5 10.1 %down.3 = (f32[64,2048]{1,0:T(8,128)S(1)}, bf16[4,64,2048]{2,1,0:T(8,128)(2,1)}) custom-call(s32[2]{0:T(128)S(1)} %pad_add_fusion.td_ref, bf16[64,4096]{1,0:T(8,128)(2,1)S(1)} %fusion.10.h0, bf16[64,4096]{1,0:T(8,128)(2,1)S(1)} %collective-permute-done.12.h1, bf16[64,4096]{1,0:T(8,128)(2,1)S(1)} %collective-permute-done.13.h2, ...), custom_call_target="tpu_custom_call" | custom-call | flops 1000000 | bytes 1000000 | tf_op jit(solution)/shard_map/down/pallas_call | solution.py:99
  120.6 4.6 %all-to-all-start = ((bf16[4,64,2048]{2,1,0:T(8,128)(2,1)}), bf16[4,64,2048]{2,1,0:T(8,128)(2,1)}, u32[]{:S(2)}, u32[]{:S(2)}) async-start(bf16[4,64,2048]{2,1,0:T(8,128)(2,1)} %get-tuple-element.56), calls=%async_computation | async-start | bytes 2097152 | tf_op jit(solution)/shard_map/all_to_all | solution.py:164
  125.2 4.5 %collective-permute-done.16 = bf16[2,64,4096]{2,1,0:T(8,128)(2,1)} collective-permute-done((bf16[2,64,4096]{2,1,0:T(8,128)(2,1)}, bf16[2,64,4096]{2,1,0:T(8,128)(2,1)}, u32[]{:S(2)}, u32[]{:S(2)}) %collective-permute-start.16) | collective-permute-done | bytes 1048608 | tf_op jit(solution)/shard_map/ppermute | solution.py:123
  129.7 2.6 %fusion.2 = f32[2,64,4096]{2,1,0:T(8,128)S(1)} fusion(bf16[2,64,4096]{2,1,0:T(8,128)(2,1)} %collective-permute-done.16, bf16[2,64,4096]{2,1,0:T(8,128)(2,1)} %collective-permute-done.15, f32[2,2,64,4096]{3,2,1,0:T(8,128)} %copy-done), kind=kLoop, calls=%fused_computation.4 | loop fusion | flops 2097152 | bytes 6291456 | tf_op jit(solution)/shard_map/add | solution.py:154
  133.8 11.3 %collective-permute-done.18.h2 = bf16[64,4096]{1,0:T(8,128)(2,1)S(1)} collective-permute-done((bf16[64,4096]{1,0:T(8,128)(2,1)S(1)}, bf16[64,4096]{1,0:T(8,128)(2,1)S(1)}, u32[]{:S(2)}, u32[]{:S(2)}) %collective-permute-start.18) | collective-permute-done | bytes 524320 | tf_op jit(solution)/shard_map/ppermute | solution.py:123
  145.2 1.9 collective-permute-done.19.h3
  147.1 5.4 %down.4 = (f32[64,1024]{1,0:T(8,128)S(1)}, bf16[64,1024]{1,0:T(8,128)(2,1)S(1)}, f32[64,1024]{1,0:T(8,128)S(1)}, bf16[64,1024]{1,0:T(8,128)(2,1)S(1)}) custom-call(s32[2]{0:T(128)S(1)} %pad_add_fusion.td_ref, bf16[64,4096]{1,0:T(8,128)(2,1)S(1)} %fusion.7.h0, bf16[64,4096]{1,0:T(8,128)(2,1)S(1)} %collective-permute-done.17.h1, ...), custom_call_target="tpu_custom_call" | custom-call | flops 1000000 | bytes 1000000 | tf_op jit(solution)/shard_map/down/pallas_call | solution.py:99
  152.5 2.0 %collective-permute-start.23 = (bf16[64,1024]{1,0:T(8,128)(2,1)S(1)}, bf16[64,1024]{1,0:T(8,128)(2,1)S(1)}, u32[]{:S(2)}, u32[]{:S(2)}) collective-permute-start(bf16[64,1024]{1,0:T(8,128)(2,1)S(1)} %get-tuple-element.59), channel_id=1, source_target_pairs={{0,1},{1,0},{2,3},{3,2},{4,5},{5,4},{6,7},{7,6},{8,9},{9,8},{10,11... | collective-permute-start | bytes 393224 | tf_op jit(solution)/shard_map/ppermute | solution.py:123
  156.1 4.8 %collective-permute-start.20 = (bf16[64,2048]{1,0:T(8,128)(2,1)S(1)}, bf16[64,2048]{1,0:T(8,128)(2,1)S(1)}, u32[]{:S(2)}, u32[]{:S(2)}) collective-permute-start(bf16[64,2048]{1,0:T(8,128)(2,1)S(1)} %fusion.11), channel_id=1, source_target_pairs={{0,0},{1,4},{2,8},{3,12},{4,1},{5,5},{6,9},{7,13},{8,2},{9,6},{10,... | collective-permute-start | bytes 786440 | tf_op jit(solution)/shard_map/ppermute | solution.py:184
  160.8 5.5 %down.5 = (f32[64,1024]{1,0:T(8,128)S(1)}, bf16[64,1024]{1,0:T(8,128)(2,1)S(1)}, f32[64,1024]{1,0:T(8,128)S(1)}, bf16[64,1024]{1,0:T(8,128)(2,1)S(1)}) custom-call(s32[2]{0:T(128)S(1)} %pad_add_fusion.td_ref, bf16[64,4096]{1,0:T(8,128)(2,1)S(1)} %fusion.7.h0, bf16[64,4096]{1,0:T(8,128)(2,1)S(1)} %collective-permute-done.17.h1, ...), custom_call_target="tpu_custom_call" | custom-call | flops 1000000 | bytes 1000000 | tf_op jit(solution)/shard_map/down/pallas_call | solution.py:99
  167.3 2.1 %collective-permute-start.24 = (bf16[64,1024]{1,0:T(8,128)(2,1)S(1)}, bf16[64,1024]{1,0:T(8,128)(2,1)S(1)}, u32[]{:S(2)}, u32[]{:S(2)}) collective-permute-start(bf16[64,1024]{1,0:T(8,128)(2,1)S(1)} %add_convert_fusion.3), channel_id=1, source_target_pairs={{0,2},{1,3},{2,0},{3,1},{4,6},{5,7},{6,4},{7,5},{8,10},{9,11},{10,... | collective-permute-start | bytes 393224 | tf_op jit(solution)/shard_map/ppermute | solution.py:123
  169.4 4.5 %collective-permute-done.22 = bf16[64,1024]{1,0:T(8,128)(2,1)S(1)} collective-permute-done((bf16[64,1024]{1,0:T(8,128)(2,1)S(1)}, bf16[64,1024]{1,0:T(8,128)(2,1)S(1)}, u32[]{:S(2)}, u32[]{:S(2)}) %collective-permute-start.22) | collective-permute-done | bytes 131104 | tf_op jit(solution)/shard_map/ppermute | solution.py:123
  173.9 2.6 %collective-permute-start.27 = (bf16[64,1024]{1,0:T(8,128)(2,1)S(1)}, bf16[64,1024]{1,0:T(8,128)(2,1)S(1)}, u32[]{:S(2)}, u32[]{:S(2)}) collective-permute-start(bf16[64,1024]{1,0:T(8,128)(2,1)S(1)} %add_convert_fusion.2), channel_id=1, source_target_pairs={{0,2},{1,3},{2,0},{3,1},{4,6},{5,7},{6,4},{7,5},{8,10},{9,11},{10,... | collective-permute-start | bytes 393224 | tf_op jit(solution)/shard_map/ppermute | solution.py:123
  177.3 7.2 %collective-permute-start.25 = (bf16[64,1024]{1,0:T(8,128)(2,1)S(1)}, bf16[64,1024]{1,0:T(8,128)(2,1)S(1)}, u32[]{:S(2)}, u32[]{:S(2)}) collective-permute-start(bf16[64,1024]{1,0:T(8,128)(2,1)S(1)} %add_convert_fusion.1), channel_id=1, source_target_pairs={{0,0},{1,4},{2,8},{3,12},{4,1},{5,5},{6,9},{7,13},{8,2},{9,6},{10,... | collective-permute-start | bytes 393224 | tf_op jit(solution)/shard_map/ppermute | solution.py:184
  184.6 5.5 %collective-permute-start.28 = (bf16[64,1024]{1,0:T(8,128)(2,1)S(1)}, bf16[64,1024]{1,0:T(8,128)(2,1)S(1)}, u32[]{:S(2)}, u32[]{:S(2)}) collective-permute-start(bf16[64,1024]{1,0:T(8,128)(2,1)S(1)} %add_convert_fusion), channel_id=1, source_target_pairs={{0,0},{1,4},{2,8},{3,12},{4,1},{5,5},{6,9},{7,13},{8,2},{9,6},{10,... | collective-permute-start | bytes 393224 | tf_op jit(solution)/shard_map/ppermute | solution.py:184
  190.1 4.1 %collective-permute-done.25 = bf16[64,1024]{1,0:T(8,128)(2,1)S(1)} collective-permute-done((bf16[64,1024]{1,0:T(8,128)(2,1)S(1)}, bf16[64,1024]{1,0:T(8,128)(2,1)S(1)}, u32[]{:S(2)}, u32[]{:S(2)}) %collective-permute-start.25) | collective-permute-done | bytes 131104 | tf_op jit(solution)/shard_map/ppermute | solution.py:184
  194.2 2.7 %collective-permute-done.28 = bf16[64,1024]{1,0:T(8,128)(2,1)S(1)} collective-permute-done((bf16[64,1024]{1,0:T(8,128)(2,1)S(1)}, bf16[64,1024]{1,0:T(8,128)(2,1)S(1)}, u32[]{:S(2)}, u32[]{:S(2)}) %collective-permute-start.28) | collective-permute-done | bytes 131104 | tf_op jit(solution)/shard_map/ppermute | solution.py:184
  (56 shorter events, 17.6 us)
Async XLA Ops:
  1.1 18.0 %collective-permute-start = (bf16[64,2048]{1,0:T(8,128)(2,1)S(1)}, bf16[64,2048]{1,0:T(8,128)(2,1)S(1)}, u32[]{:S(2)}, u32[]{:S(2)}) collective-permute-start(bf16[64,2048]{1,0:T(8,128)(2,1)S(1)} %get-tuple-element.74), channel_id=1, source_target_pairs={{0,0},{1,4},{2,8},{3,12},{4,1},{5,5},{6,9},{7,13},{8,2},{9,6},{10,... | collective-permute-start | bytes 786440 | tf_op jit(solution)/shard_map/ppermute | solution.py:131
  19.1 13.0 %collective-permute-start.3 = (bf16[64,2048]{1,0:T(8,128)(2,1)S(1)}, bf16[64,2048]{1,0:T(8,128)(2,1)S(1)}, u32[]{:S(2)}, u32[]{:S(2)}) collective-permute-start(bf16[64,2048]{1,0:T(8,128)(2,1)S(1)} %collective-permute-done.refs_0_), channel_id=1, source_target_pairs={{0,2},{1,3},{2,0},{3,1},{4,6},{5,7},{6,4},{7,5},{8,10},{9,11},{10,... | collective-permute-start | bytes 786440 | tf_op jit(solution)/shard_map/ppermute | solution.py:123
  19.1 22.5 %collective-permute-start.1 = (bf16[64,2048]{1,0:T(8,128)(2,1)S(1)}, bf16[64,2048]{1,0:T(8,128)(2,1)S(1)}, u32[]{:S(2)}, u32[]{:S(2)}) collective-permute-start(bf16[64,2048]{1,0:T(8,128)(2,1)S(1)} %get-tuple-element.40), channel_id=1, source_target_pairs={{0,0},{1,4},{2,8},{3,12},{4,1},{5,5},{6,9},{7,13},{8,2},{9,6},{10,... | collective-permute-start | bytes 786440 | tf_op jit(solution)/shard_map/ppermute | solution.py:131
  21.0 20.5 %collective-permute-start.2 = (bf16[64,2048]{1,0:T(8,128)(2,1)S(1)}, bf16[64,2048]{1,0:T(8,128)(2,1)S(1)}, u32[]{:S(2)}, u32[]{:S(2)}) collective-permute-start(bf16[64,2048]{1,0:T(8,128)(2,1)S(1)} %collective-permute-done.refs_0_), channel_id=1, source_target_pairs={{0,1},{1,0},{2,3},{3,2},{4,5},{5,4},{6,7},{7,6},{8,9},{9,8},{10,11... | collective-permute-start | bytes 786440 | tf_op jit(solution)/shard_map/ppermute | solution.py:123
  32.1 9.5 %collective-permute-start.4 = (bf16[64,2048]{1,0:T(8,128)(2,1)S(1)}, bf16[64,2048]{1,0:T(8,128)(2,1)S(1)}, u32[]{:S(2)}, u32[]{:S(2)}) collective-permute-start(bf16[64,2048]{1,0:T(8,128)(2,1)S(1)} %collective-permute-done.3.refs_2_), channel_id=1, source_target_pairs={{0,1},{1,0},{2,3},{3,2},{4,5},{5,4},{6,7},{7,6},{8,9},{9,8},{10,11... | collective-permute-start | bytes 786440 | tf_op jit(solution)/shard_map/ppermute | solution.py:123
  41.6 21.9 %collective-permute-start.6 = (bf16[64,2048]{1,0:T(8,128)(2,1)S(1)}, bf16[64,2048]{1,0:T(8,128)(2,1)S(1)}, u32[]{:S(2)}, u32[]{:S(2)}) collective-permute-start(bf16[64,2048]{1,0:T(8,128)(2,1)S(1)} %collective-permute-done.1.refs_0_), channel_id=1, source_target_pairs={{0,2},{1,3},{2,0},{3,1},{4,6},{5,7},{6,4},{7,5},{8,10},{9,11},{10,... | collective-permute-start | bytes 786440 | tf_op jit(solution)/shard_map/ppermute | solution.py:123
  46.4 17.1 %collective-permute-start.5 = (bf16[64,2048]{1,0:T(8,128)(2,1)S(1)}, bf16[64,2048]{1,0:T(8,128)(2,1)S(1)}, u32[]{:S(2)}, u32[]{:S(2)}) collective-permute-start(bf16[64,2048]{1,0:T(8,128)(2,1)S(1)} %collective-permute-done.1.refs_0_), channel_id=1, source_target_pairs={{0,1},{1,0},{2,3},{3,2},{4,5},{5,4},{6,7},{7,6},{8,9},{9,8},{10,11... | collective-permute-start | bytes 786440 | tf_op jit(solution)/shard_map/ppermute | solution.py:123
  63.5 4.0 %collective-permute-start.7 = (bf16[2,64,4096]{2,1,0:T(8,128)(2,1)S(1)}, bf16[2,64,4096]{2,1,0:T(8,128)(2,1)S(1)}, u32[]{:S(2)}, u32[]{:S(2)}) collective-permute-start(bf16[2,64,4096]{2,1,0:T(8,128)(2,1)S(1)} %get-tuple-element.46), channel_id=1, source_target_pairs={{0,4},{4,0},{8,12},{12,8},{1,5},{5,1},{9,13},{13,9},{2,6},{6,2},{1... | collective-permute-start | bytes 3145736 | tf_op jit(solution)/shard_map/ppermute | solution.py:123
  65.2 3.7 %copy-start.1 = (s32[32]{0:T(128)S(1)}, s32[32]{0:T(128)}, u32[]{:S(2)}) copy-start(s32[32]{0:T(128)} %param.10) | copy-start | bytes 388
  65.2 27.3 %collective-permute-start.9 = (bf16[2,64,4096]{2,1,0:T(8,128)(2,1)S(1)}, bf16[2,64,4096]{2,1,0:T(8,128)(2,1)S(1)}, u32[]{:S(2)}, u32[]{:S(2)}) collective-permute-start(bf16[2,64,4096]{2,1,0:T(8,128)(2,1)S(1)} %get-tuple-element.52), channel_id=1, source_target_pairs={{0,4},{4,0},{8,12},{12,8},{1,5},{5,1},{9,13},{13,9},{2,6},{6,2},{1... | collective-permute-start | bytes 3145736 | tf_op jit(solution)/shard_map/ppermute | solution.py:123
  67.7 25.5 %collective-permute-start.10 = (bf16[2,64,4096]{2,1,0:T(8,128)(2,1)S(1)}, bf16[2,64,4096]{2,1,0:T(8,128)(2,1)S(1)}, u32[]{:S(2)}, u32[]{:S(2)}) collective-permute-start(bf16[2,64,4096]{2,1,0:T(8,128)(2,1)S(1)} %fusion.1), channel_id=1, source_target_pairs={{0,8},{4,12},{8,0},{12,4},{1,9},{5,13},{9,1},{13,5},{2,10},{6,14},... | collective-permute-start | bytes 3145736 | tf_op jit(solution)/shard_map/ppermute | solution.py:123
  68.9 8.4 %collective-permute-start.8 = (bf16[64,2048]{1,0:T(8,128)(2,1)S(1)}, bf16[64,2048]{1,0:T(8,128)(2,1)S(1)}, u32[]{:S(2)}, u32[]{:S(2)}) collective-permute-start(bf16[64,2048]{1,0:T(8,128)(2,1)S(1)} %collective-permute-done.6.refs_2_), channel_id=1, source_target_pairs={{0,1},{1,0},{2,3},{3,2},{4,5},{5,4},{6,7},{7,6},{8,9},{9,8},{10,11... | collective-permute-start | bytes 786440 | tf_op jit(solution)/shard_map/ppermute | solution.py:123
  91.9 3.4 %copy-start = (f32[2,2,64,4096]{3,2,1,0:T(8,128)}, f32[2,2,64,4096]{3,2,1,0:T(8,128)S(1)}, u32[]{:S(2)}) copy-start(f32[2,2,64,4096]{3,2,1,0:T(8,128)S(1)} %get-tuple-element.57) | copy-start | bytes 12582916
  91.9 3.4 %collective-permute-start.11 = (bf16[2,64,4096]{2,1,0:T(8,128)(2,1)S(1)}, bf16[2,64,4096]{2,1,0:T(8,128)(2,1)S(1)}, u32[]{:S(2)}, u32[]{:S(2)}) collective-permute-start(bf16[2,64,4096]{2,1,0:T(8,128)(2,1)S(1)} %get-tuple-element.50), channel_id=1, source_target_pairs={{0,4},{4,0},{8,12},{12,8},{1,5},{5,1},{9,13},{13,9},{2,6},{6,2},{1... | collective-permute-start | bytes 3145736 | tf_op jit(solution)/shard_map/ppermute | solution.py:123
  92.0 33.2 %collective-permute-start.15 = (bf16[2,64,4096]{2,1,0:T(8,128)(2,1)S(1)}, bf16[2,64,4096]{2,1,0:T(8,128)(2,1)}, u32[]{:S(2)}, u32[]{:S(2)}) collective-permute-start(bf16[2,64,4096]{2,1,0:T(8,128)(2,1)S(1)} %get-tuple-element.49), channel_id=1, source_target_pairs={{0,4},{4,0},{8,12},{12,8},{1,5},{5,1},{9,13},{13,9},{2,6},{6,2},{1... | collective-permute-start | bytes 3145736 | tf_op jit(solution)/shard_map/ppermute | solution.py:123
  93.7 14.9 %collective-permute-start.13 = (bf16[64,4096]{1,0:T(8,128)(2,1)S(1)}, bf16[64,4096]{1,0:T(8,128)(2,1)S(1)}, u32[]{:S(2)}, u32[]{:S(2)}) collective-permute-start(bf16[64,4096]{1,0:T(8,128)(2,1)S(1)} %fusion.10.h0), channel_id=1, source_target_pairs={{0,8},{4,12},{8,0},{12,4},{1,9},{5,13},{9,1},{13,5},{2,10},{6,14},... | collective-permute-start | bytes 1572872 | tf_op jit(solution)/shard_map/ppermute | solution.py:123
  96.6 33.1 %collective-permute-start.16 = (bf16[2,64,4096]{2,1,0:T(8,128)(2,1)}, bf16[2,64,4096]{2,1,0:T(8,128)(2,1)}, u32[]{:S(2)}, u32[]{:S(2)}) collective-permute-start(bf16[2,64,4096]{2,1,0:T(8,128)(2,1)} %fusion.3), channel_id=1, source_target_pairs={{0,8},{4,12},{8,0},{12,4},{1,9},{5,13},{9,1},{13,5},{2,10},{6,14},... | collective-permute-start | bytes 3145736 | tf_op jit(solution)/shard_map/ppermute | solution.py:123
  98.1 10.6 %collective-permute-start.12 = (bf16[64,4096]{1,0:T(8,128)(2,1)S(1)}, bf16[64,4096]{1,0:T(8,128)(2,1)S(1)}, u32[]{:S(2)}, u32[]{:S(2)}) collective-permute-start(bf16[64,4096]{1,0:T(8,128)(2,1)S(1)} %fusion.10.h0), channel_id=1, source_target_pairs={{0,4},{4,0},{8,12},{12,8},{1,5},{5,1},{9,13},{13,9},{2,6},{6,2},{1... | collective-permute-start | bytes 1572872 | tf_op jit(solution)/shard_map/ppermute | solution.py:123
  108.6 1.9 collective-permute-start.14
  120.6 34.1 %all-to-all-start = ((bf16[4,64,2048]{2,1,0:T(8,128)(2,1)}), bf16[4,64,2048]{2,1,0:T(8,128)(2,1)}, u32[]{:S(2)}, u32[]{:S(2)}) async-start(bf16[4,64,2048]{2,1,0:T(8,128)(2,1)} %get-tuple-element.56), calls=%async_computation | async-start | bytes 2097152 | tf_op jit(solution)/shard_map/all_to_all | solution.py:164
  132.4 12.7 %collective-permute-start.18 = (bf16[64,4096]{1,0:T(8,128)(2,1)S(1)}, bf16[64,4096]{1,0:T(8,128)(2,1)S(1)}, u32[]{:S(2)}, u32[]{:S(2)}) collective-permute-start(bf16[64,4096]{1,0:T(8,128)(2,1)S(1)} %fusion.7.h0), channel_id=1, source_target_pairs={{0,8},{4,12},{8,0},{12,4},{1,9},{5,13},{9,1},{13,5},{2,10},{6,14},... | collective-permute-start | bytes 1572872 | tf_op jit(solution)/shard_map/ppermute | solution.py:123
  133.8 11.3 %collective-permute-start.17 = (bf16[64,4096]{1,0:T(8,128)(2,1)S(1)}, bf16[64,4096]{1,0:T(8,128)(2,1)S(1)}, u32[]{:S(2)}, u32[]{:S(2)}) collective-permute-start(bf16[64,4096]{1,0:T(8,128)(2,1)S(1)} %fusion.7.h0), channel_id=1, source_target_pairs={{0,4},{4,0},{8,12},{12,8},{1,5},{5,1},{9,13},{13,9},{2,6},{6,2},{1... | collective-permute-start | bytes 1572872 | tf_op jit(solution)/shard_map/ppermute | solution.py:123
  145.2 1.9 collective-permute-start.19
  152.5 24.0 %collective-permute-start.23 = (bf16[64,1024]{1,0:T(8,128)(2,1)S(1)}, bf16[64,1024]{1,0:T(8,128)(2,1)S(1)}, u32[]{:S(2)}, u32[]{:S(2)}) collective-permute-start(bf16[64,1024]{1,0:T(8,128)(2,1)S(1)} %get-tuple-element.59), channel_id=1, source_target_pairs={{0,1},{1,0},{2,3},{3,2},{4,5},{5,4},{6,7},{7,6},{8,9},{9,8},{10,11... | collective-permute-start | bytes 393224 | tf_op jit(solution)/shard_map/ppermute | solution.py:123
  154.6 11.8 %collective-permute-start.21 = (bf16[64,1024]{1,0:T(8,128)(2,1)S(1)}, bf16[64,1024]{1,0:T(8,128)(2,1)}, u32[]{:S(2)}, u32[]{:S(2)}) collective-permute-start(bf16[64,1024]{1,0:T(8,128)(2,1)S(1)} %get-tuple-element.67), channel_id=1, source_target_pairs={{0,1},{1,0},{2,3},{3,2},{4,5},{5,4},{6,7},{7,6},{8,9},{9,8},{10,11... | collective-permute-start | bytes 393224 | tf_op jit(solution)/shard_map/ppermute | solution.py:123
  156.1 38.1 %collective-permute-start.20 = (bf16[64,2048]{1,0:T(8,128)(2,1)S(1)}, bf16[64,2048]{1,0:T(8,128)(2,1)S(1)}, u32[]{:S(2)}, u32[]{:S(2)}) collective-permute-start(bf16[64,2048]{1,0:T(8,128)(2,1)S(1)} %fusion.11), channel_id=1, source_target_pairs={{0,0},{1,4},{2,8},{3,12},{4,1},{5,5},{6,9},{7,13},{8,2},{9,6},{10,... | collective-permute-start | bytes 786440 | tf_op jit(solution)/shard_map/ppermute | solution.py:184
  166.3 7.6 %collective-permute-start.22 = (bf16[64,1024]{1,0:T(8,128)(2,1)S(1)}, bf16[64,1024]{1,0:T(8,128)(2,1)S(1)}, u32[]{:S(2)}, u32[]{:S(2)}) collective-permute-start(bf16[64,1024]{1,0:T(8,128)(2,1)S(1)} %get-tuple-element.69), channel_id=1, source_target_pairs={{0,1},{1,0},{2,3},{3,2},{4,5},{5,4},{6,7},{7,6},{8,9},{9,8},{10,11... | collective-permute-start | bytes 393224 | tf_op jit(solution)/shard_map/ppermute | solution.py:123
  167.3 9.9 %collective-permute-start.24 = (bf16[64,1024]{1,0:T(8,128)(2,1)S(1)}, bf16[64,1024]{1,0:T(8,128)(2,1)S(1)}, u32[]{:S(2)}, u32[]{:S(2)}) collective-permute-start(bf16[64,1024]{1,0:T(8,128)(2,1)S(1)} %add_convert_fusion.3), channel_id=1, source_target_pairs={{0,2},{1,3},{2,0},{3,1},{4,6},{5,7},{6,4},{7,5},{8,10},{9,11},{10,... | collective-permute-start | bytes 393224 | tf_op jit(solution)/shard_map/ppermute | solution.py:123
  173.9 10.6 %collective-permute-start.26 = (bf16[64,1024]{1,0:T(8,128)(2,1)S(1)}, bf16[64,1024]{1,0:T(8,128)(2,1)S(1)}, u32[]{:S(2)}, u32[]{:S(2)}) collective-permute-start(bf16[64,1024]{1,0:T(8,128)(2,1)S(1)} %get-tuple-element.73), channel_id=1, source_target_pairs={{0,1},{1,0},{2,3},{3,2},{4,5},{5,4},{6,7},{7,6},{8,9},{9,8},{10,11... | collective-permute-start | bytes 393224 | tf_op jit(solution)/shard_map/ppermute | solution.py:123
  173.9 10.5 %collective-permute-start.27 = (bf16[64,1024]{1,0:T(8,128)(2,1)S(1)}, bf16[64,1024]{1,0:T(8,128)(2,1)S(1)}, u32[]{:S(2)}, u32[]{:S(2)}) collective-permute-start(bf16[64,1024]{1,0:T(8,128)(2,1)S(1)} %add_convert_fusion.2), channel_id=1, source_target_pairs={{0,2},{1,3},{2,0},{3,1},{4,6},{5,7},{6,4},{7,5},{8,10},{9,11},{10,... | collective-permute-start | bytes 393224 | tf_op jit(solution)/shard_map/ppermute | solution.py:123
  177.3 16.9 %collective-permute-start.25 = (bf16[64,1024]{1,0:T(8,128)(2,1)S(1)}, bf16[64,1024]{1,0:T(8,128)(2,1)S(1)}, u32[]{:S(2)}, u32[]{:S(2)}) collective-permute-start(bf16[64,1024]{1,0:T(8,128)(2,1)S(1)} %add_convert_fusion.1), channel_id=1, source_target_pairs={{0,0},{1,4},{2,8},{3,12},{4,1},{5,5},{6,9},{7,13},{8,2},{9,6},{10,... | collective-permute-start | bytes 393224 | tf_op jit(solution)/shard_map/ppermute | solution.py:184
  184.6 12.4 %collective-permute-start.28 = (bf16[64,1024]{1,0:T(8,128)(2,1)S(1)}, bf16[64,1024]{1,0:T(8,128)(2,1)S(1)}, u32[]{:S(2)}, u32[]{:S(2)}) collective-permute-start(bf16[64,1024]{1,0:T(8,128)(2,1)S(1)} %add_convert_fusion), channel_id=1, source_target_pairs={{0,0},{1,4},{2,8},{3,12},{4,1},{5,5},{6,9},{7,13},{8,2},{9,6},{10,... | collective-permute-start | bytes 393224 | tf_op jit(solution)/shard_map/ppermute | solution.py:184

commit v7 on v6

--- a/solution.py
+++ b/solution.py
@@ -132,7 +132,8 @@
 
     def spread(c):
         x = mine[c] if c == 0 else after(mine[c], *blocks[c - 1])
-        one, two = swap(x, "tensor", 1), swap(x, "tensor", 2)
+        two = swap(x, "tensor", 2)
+        one = swap(after(x, two) if c == 0 else x, "tensor", 1)
         blocks[c] = [mine[c], one, two, swap(two, "tensor", 1)]
 
     def first(c):

time: 198 us -> 200 us (1.010)
  waiting for transfers between devices: 78.5 us -> 90.5 us
  starting transfers between devices: 59.1 us -> 48.8 us
    ppermute x24, waiting for transfers between devices: 52 us -> 64.2 us  [per_device(): swap = lambda x, axis, mask: lax.ppermute(x, axis, xor_perm(4, mask))]
    ppermute x24, starting transfers between devices: 30.6 us -> 22.2 us  [per_device(): swap = lambda x, axis, mask: lax.ppermute(x, axis, xor_perm(4, mask))]
  transfers between devices with their start and end apart: 30 -> 30, of which waited for: 17 -> 18; matrix products, arithmetic and copies ran while one was open for 4% -> 4% of each run, Pallas kernels for 25% -> 25%
where the time goes in v7:
time: 200 us
  waiting for transfers between devices  90.5 us (45%)
  Pallas kernels  50.1 us (25%)
  starting transfers between devices  48.8 us (24%)
  other arithmetic  8.08 us (4%)
    ppermute x24, waiting for transfers between devices, per_device(): swap = lambda x, axis, mask: lax.ppermute(x, axis, xor_perm(4, mask))  64.2 us
    pallas_call x2, Pallas kernels, gate_up(): pl.pallas_call(gate_up_kernel, grid_spec=pltpu.PrefetchScalarGridSpec(num...  29.1 us
    ppermute x24, starting transfers between devices, per_device(): swap = lambda x, axis, mask: lax.ppermute(x, axis, xor_perm(4, mask))  22.2 us
    pallas_call x3, Pallas kernels, down(): pl.pallas_call(down_kernel, grid_spec=pltpu.PrefetchScalarGridSpec(num_sc...  21 us
    ppermute x2, waiting for transfers between devices, turn_in(): lax.ppermute(x if c == 0 else after(x, mine[c - 1]), ('dp', 'tensor'), turn)  19.7 us
    ppermute x3, starting transfers between devices, mix(): outs[c, h] = lax.ppermute(mixed, ('dp', 'tensor'), turn)  15.9 us
    ppermute x3, waiting for transfers between devices, mix(): outs[c, h] = lax.ppermute(mixed, ('dp', 'tensor'), turn)  6.67 us
    ppermute x2, starting transfers between devices, turn_in(): lax.ppermute(x if c == 0 else after(x, mine[c - 1]), ('dp', 'tensor'), turn)  6.38 us
  transfers between devices with their start and end apart: 30, of which 18 were waited for; matrix products, arithmetic and copies ran while one was open for 4% of the time, Pallas kernels for 25%

profile of v7, /device:TPU:2, one launch (start us, length us, event | category | flops | bytes accessed | tf_op | source)
XLA Modules:
  0.0 199.5 jit_solution(10905185614126091854)
XLA Ops:
  1.1 4.5 %collective-permute-start = (bf16[64,2048]{1,0:T(8,128)(2,1)S(1)}, bf16[64,2048]{1,0:T(8,128)(2,1)S(1)}, u32[]{:S(2)}, u32[]{:S(2)}) collective-permute-start(bf16[64,2048]{1,0:T(8,128)(2,1)S(1)} %get-tuple-element.76), channel_id=1, source_target_pairs={{0,0},{1,4},{2,8},{3,12},{4,1},{5,5},{6,9},{7,13},{8,2},{9,6},{10,... | collective-permute-start | bytes 786440 | tf_op jit(solution)/shard_map/ppermute | solution.py:131
  5.5 13.6 %collective-permute-done.refs_0_ = bf16[64,2048]{1,0:T(8,128)(2,1)S(1)} collective-permute-done((bf16[64,2048]{1,0:T(8,128)(2,1)S(1)}, bf16[64,2048]{1,0:T(8,128)(2,1)S(1)}, u32[]{:S(2)}, u32[]{:S(2)}) %collective-permute-start) | collective-permute-done | bytes 262176 | tf_op jit(solution)/shard_map/ppermute | solution.py:131
  19.1 1.9 collective-permute-start.1
  21.0 11.0 %collective-permute-done.2.refs_2_ = bf16[64,2048]{1,0:T(8,128)(2,1)S(1)} collective-permute-done((bf16[64,2048]{1,0:T(8,128)(2,1)S(1)}, bf16[64,2048]{1,0:T(8,128)(2,1)S(1)}, u32[]{:S(2)}, u32[]{:S(2)}) %collective-permute-start.2) | collective-permute-done | bytes 262176 | tf_op jit(solution)/shard_map/ppermute | solution.py:123
  32.0 3.4 %collective-permute-start.3 = (bf16[64,2048]{1,0:T(8,128)(2,1)S(1)}, bf16[64,2048]{1,0:T(8,128)(2,1)S(1)}, u32[]{:S(2)}, u32[]{:S(2)}) collective-permute-start(bf16[64,2048]{1,0:T(8,128)(2,1)S(1)} %collective-permute-done.refs_0_), channel_id=1, source_target_pairs={{0,1},{1,0},{2,3},{3,2},{4,5},{5,4},{6,7},{7,6},{8,9},{9,8},{10,11... | collective-permute-start | bytes 786440 | tf_op jit(solution)/shard_map/ppermute | solution.py:123
  35.4 6.1 %collective-permute-done.1.refs_0_ = bf16[64,2048]{1,0:T(8,128)(2,1)S(1)} collective-permute-done((bf16[64,2048]{1,0:T(8,128)(2,1)S(1)}, bf16[64,2048]{1,0:T(8,128)(2,1)S(1)}, u32[]{:S(2)}, u32[]{:S(2)}) %collective-permute-start.1) | collective-permute-done | bytes 262176 | tf_op jit(solution)/shard_map/ppermute | solution.py:131
  42.6 4.6 %collective-permute-done.4.refs_3_ = bf16[64,2048]{1,0:T(8,128)(2,1)S(1)} collective-permute-done((bf16[64,2048]{1,0:T(8,128)(2,1)S(1)}, bf16[64,2048]{1,0:T(8,128)(2,1)S(1)}, u32[]{:S(2)}, u32[]{:S(2)}) %collective-permute-start.4) | collective-permute-done | bytes 262176 | tf_op jit(solution)/shard_map/ppermute | solution.py:123
  47.2 4.1 %collective-permute-start.6 = (bf16[64,2048]{1,0:T(8,128)(2,1)S(1)}, bf16[64,2048]{1,0:T(8,128)(2,1)S(1)}, u32[]{:S(2)}, u32[]{:S(2)}) collective-permute-start(bf16[64,2048]{1,0:T(8,128)(2,1)S(1)} %collective-permute-done.1.refs_0_), channel_id=1, source_target_pairs={{0,2},{1,3},{2,0},{3,1},{4,6},{5,7},{6,4},{7,5},{8,10},{9,11},{10,... | collective-permute-start | bytes 786440 | tf_op jit(solution)/shard_map/ppermute | solution.py:123
  51.3 2.5 %collective-permute-start.5 = (bf16[64,2048]{1,0:T(8,128)(2,1)S(1)}, bf16[64,2048]{1,0:T(8,128)(2,1)S(1)}, u32[]{:S(2)}, u32[]{:S(2)}) collective-permute-start(bf16[64,2048]{1,0:T(8,128)(2,1)S(1)} %collective-permute-done.1.refs_0_), channel_id=1, source_target_pairs={{0,1},{1,0},{2,3},{3,2},{4,5},{5,4},{6,7},{7,6},{8,9},{9,8},{10,11... | collective-permute-start | bytes 786440 | tf_op jit(solution)/shard_map/ppermute | solution.py:123
  53.8 14.6 %gate_up.2 = (f32[2,2,64,4096]{3,2,1,0:T(8,128)S(1)}, bf16[2,64,4096]{2,1,0:T(8,128)(2,1)S(1)}, bf16[2,64,4096]{2,1,0:T(8,128)(2,1)S(1)}) custom-call(s32[1]{0:T(128)} %bitcast.td_ref, bf16[64,2048]{1,0:T(8,128)(2,1)S(1)} %collective-permute-done.refs_0_, bf16[64,2048]{1,0:T(8,128)(2,1)S(1)} %collective-permute-done.3.refs_1_, ...), custom_call_target="tpu_custom_call" | custom-call | flops 20000000 | bytes 20000000 | tf_op jit(solution)/shard_map/gate_up/pallas_call | solution.py:50
  69.0 2.1 %collective-permute-done.7 = bf16[2,64,4096]{2,1,0:T(8,128)(2,1)S(1)} collective-permute-done((bf16[2,64,4096]{2,1,0:T(8,128)(2,1)S(1)}, bf16[2,64,4096]{2,1,0:T(8,128)(2,1)S(1)}, u32[]{:S(2)}, u32[]{:S(2)}) %collective-permute-start.7) | collective-permute-done | bytes 1048608 | tf_op jit(solution)/shard_map/ppermute | solution.py:123
  72.5 8.0 %collective-permute-done.8.refs_3_ = bf16[64,2048]{1,0:T(8,128)(2,1)S(1)} collective-permute-done((bf16[64,2048]{1,0:T(8,128)(2,1)S(1)}, bf16[64,2048]{1,0:T(8,128)(2,1)S(1)}, u32[]{:S(2)}, u32[]{:S(2)}) %collective-permute-start.8) | collective-permute-done | bytes 262176 | tf_op jit(solution)/shard_map/ppermute | solution.py:123
  80.5 14.6 %gate_up.3 = (f32[2,2,64,4096]{3,2,1,0:T(8,128)S(1)}, bf16[2,64,4096]{2,1,0:T(8,128)(2,1)S(1)}, bf16[2,64,4096]{2,1,0:T(8,128)(2,1)S(1)}) custom-call(s32[1]{0:T(128)} %bitcast.td_ref, bf16[64,2048]{1,0:T(8,128)(2,1)S(1)} %collective-permute-done.1.refs_0_, bf16[64,2048]{1,0:T(8,128)(2,1)S(1)} %collective-permute-done.5.refs_1_, ...), custom_call_target="tpu_custom_call" | custom-call | flops 20000000 | bytes 20000000 | tf_op jit(solution)/shard_map/gate_up/pallas_call | solution.py:50
  101.5 10.5 %collective-permute-done.13.h2 = bf16[64,4096]{1,0:T(8,128)(2,1)S(1)} collective-permute-done((bf16[64,4096]{1,0:T(8,128)(2,1)S(1)}, bf16[64,4096]{1,0:T(8,128)(2,1)S(1)}, u32[]{:S(2)}, u32[]{:S(2)}) %collective-permute-start.13) | collective-permute-done | bytes 524320 | tf_op jit(solution)/shard_map/ppermute | solution.py:123
  112.1 1.8 collective-permute-done.14.h3
  113.9 10.1 %down.3 = (f32[64,2048]{1,0:T(8,128)S(1)}, bf16[4,64,2048]{2,1,0:T(8,128)(2,1)}) custom-call(s32[2]{0:T(128)S(1)} %pad_add_fusion.td_ref, bf16[64,4096]{1,0:T(8,128)(2,1)S(1)} %fusion.10.h0, bf16[64,4096]{1,0:T(8,128)(2,1)S(1)} %collective-permute-done.12.h1, bf16[64,4096]{1,0:T(8,128)(2,1)S(1)} %collective-permute-done.13.h2, ...), custom_call_target="tpu_custom_call" | custom-call | flops 1000000 | bytes 1000000 | tf_op jit(solution)/shard_map/down/pallas_call | solution.py:99
  123.9 4.2 %all-to-all-start = ((bf16[4,64,2048]{2,1,0:T(8,128)(2,1)}), bf16[4,64,2048]{2,1,0:T(8,128)(2,1)}, u32[]{:S(2)}, u32[]{:S(2)}) async-start(bf16[4,64,2048]{2,1,0:T(8,128)(2,1)} %get-tuple-element.58), calls=%async_computation | async-start | bytes 2097152 | tf_op jit(solution)/shard_map/all_to_all | solution.py:165
  128.2 4.6 %collective-permute-done.16 = bf16[2,64,4096]{2,1,0:T(8,128)(2,1)} collective-permute-done((bf16[2,64,4096]{2,1,0:T(8,128)(2,1)}, bf16[2,64,4096]{2,1,0:T(8,128)(2,1)}, u32[]{:S(2)}, u32[]{:S(2)}) %collective-permute-start.16) | collective-permute-done | bytes 1048608 | tf_op jit(solution)/shard_map/ppermute | solution.py:123
  132.8 2.6 %fusion.2 = f32[2,64,4096]{2,1,0:T(8,128)S(1)} fusion(bf16[2,64,4096]{2,1,0:T(8,128)(2,1)} %collective-permute-done.16, bf16[2,64,4096]{2,1,0:T(8,128)(2,1)} %collective-permute-done.15, f32[2,2,64,4096]{3,2,1,0:T(8,128)} %copy-done), kind=kLoop, calls=%fused_computation.4 | loop fusion | flops 2097152 | bytes 6291456 | tf_op jit(solution)/shard_map/add | solution.py:155
  137.2 11.3 %collective-permute-done.18.h2 = bf16[64,4096]{1,0:T(8,128)(2,1)S(1)} collective-permute-done((bf16[64,4096]{1,0:T(8,128)(2,1)S(1)}, bf16[64,4096]{1,0:T(8,128)(2,1)S(1)}, u32[]{:S(2)}, u32[]{:S(2)}) %collective-permute-start.18) | collective-permute-done | bytes 524320 | tf_op jit(solution)/shard_map/ppermute | solution.py:123
  148.5 1.9 collective-permute-done.19.h3
  150.4 5.4 %down.4 = (f32[64,1024]{1,0:T(8,128)S(1)}, bf16[64,1024]{1,0:T(8,128)(2,1)S(1)}, f32[64,1024]{1,0:T(8,128)S(1)}, bf16[64,1024]{1,0:T(8,128)(2,1)S(1)}) custom-call(s32[2]{0:T(128)S(1)} %pad_add_fusion.td_ref, bf16[64,4096]{1,0:T(8,128)(2,1)S(1)} %fusion.7.h0, bf16[64,4096]{1,0:T(8,128)(2,1)S(1)} %collective-permute-done.17.h1, ...), custom_call_target="tpu_custom_call" | custom-call | flops 1000000 | bytes 1000000 | tf_op jit(solution)/shard_map/down/pallas_call | solution.py:99
  156.2 1.7 collective-permute-start.21
  159.4 2.8 %collective-permute-start.20 = (bf16[64,2048]{1,0:T(8,128)(2,1)S(1)}, bf16[64,2048]{1,0:T(8,128)(2,1)S(1)}, u32[]{:S(2)}, u32[]{:S(2)}) collective-permute-start(bf16[64,2048]{1,0:T(8,128)(2,1)S(1)} %fusion.11), channel_id=1, source_target_pairs={{0,0},{1,4},{2,8},{3,12},{4,1},{5,5},{6,9},{7,13},{8,2},{9,6},{10,... | collective-permute-start | bytes 786440 | tf_op jit(solution)/shard_map/ppermute | solution.py:185
  162.2 5.5 %down.5 = (f32[64,1024]{1,0:T(8,128)S(1)}, bf16[64,1024]{1,0:T(8,128)(2,1)S(1)}, f32[64,1024]{1,0:T(8,128)S(1)}, bf16[64,1024]{1,0:T(8,128)(2,1)S(1)}) custom-call(s32[2]{0:T(128)S(1)} %pad_add_fusion.td_ref, bf16[64,4096]{1,0:T(8,128)(2,1)S(1)} %fusion.7.h0, bf16[64,4096]{1,0:T(8,128)(2,1)S(1)} %collective-permute-done.17.h1, ...), custom_call_target="tpu_custom_call" | custom-call | flops 1000000 | bytes 1000000 | tf_op jit(solution)/shard_map/down/pallas_call | solution.py:99
  168.7 1.9 collective-permute-start.24
  170.7 4.7 %collective-permute-done.22 = bf16[64,1024]{1,0:T(8,128)(2,1)S(1)} collective-permute-done((bf16[64,1024]{1,0:T(8,128)(2,1)S(1)}, bf16[64,1024]{1,0:T(8,128)(2,1)S(1)}, u32[]{:S(2)}, u32[]{:S(2)}) %collective-permute-start.22) | collective-permute-done | bytes 131104 | tf_op jit(solution)/shard_map/ppermute | solution.py:123
  175.4 2.4 %collective-permute-start.27 = (bf16[64,1024]{1,0:T(8,128)(2,1)S(1)}, bf16[64,1024]{1,0:T(8,128)(2,1)S(1)}, u32[]{:S(2)}, u32[]{:S(2)}) collective-permute-start(bf16[64,1024]{1,0:T(8,128)(2,1)S(1)} %add_convert_fusion.2), channel_id=1, source_target_pairs={{0,2},{1,3},{2,0},{3,1},{4,6},{5,7},{6,4},{7,5},{8,10},{9,11},{10,... | collective-permute-start | bytes 393224 | tf_op jit(solution)/shard_map/ppermute | solution.py:123
  178.8 7.6 %collective-permute-start.25 = (bf16[64,1024]{1,0:T(8,128)(2,1)S(1)}, bf16[64,1024]{1,0:T(8,128)(2,1)S(1)}, u32[]{:S(2)}, u32[]{:S(2)}) collective-permute-start(bf16[64,1024]{1,0:T(8,128)(2,1)S(1)} %add_convert_fusion.1), channel_id=1, source_target_pairs={{0,0},{1,4},{2,8},{3,12},{4,1},{5,5},{6,9},{7,13},{8,2},{9,6},{10,... | collective-permute-start | bytes 393224 | tf_op jit(solution)/shard_map/ppermute | solution.py:185
  186.5 5.5 %collective-permute-start.28 = (bf16[64,1024]{1,0:T(8,128)(2,1)S(1)}, bf16[64,1024]{1,0:T(8,128)(2,1)S(1)}, u32[]{:S(2)}, u32[]{:S(2)}) collective-permute-start(bf16[64,1024]{1,0:T(8,128)(2,1)S(1)} %add_convert_fusion), channel_id=1, source_target_pairs={{0,0},{1,4},{2,8},{3,12},{4,1},{5,5},{6,9},{7,13},{8,2},{9,6},{10,... | collective-permute-start | bytes 393224 | tf_op jit(solution)/shard_map/ppermute | solution.py:185
  192.0 4.1 %collective-permute-done.25 = bf16[64,1024]{1,0:T(8,128)(2,1)S(1)} collective-permute-done((bf16[64,1024]{1,0:T(8,128)(2,1)S(1)}, bf16[64,1024]{1,0:T(8,128)(2,1)S(1)}, u32[]{:S(2)}, u32[]{:S(2)}) %collective-permute-start.25) | collective-permute-done | bytes 131104 | tf_op jit(solution)/shard_map/ppermute | solution.py:185
  196.1 2.6 %collective-permute-done.28 = bf16[64,1024]{1,0:T(8,128)(2,1)S(1)} collective-permute-done((bf16[64,1024]{1,0:T(8,128)(2,1)S(1)}, bf16[64,1024]{1,0:T(8,128)(2,1)S(1)}, u32[]{:S(2)}, u32[]{:S(2)}) %collective-permute-start.28) | collective-permute-done | bytes 131104 | tf_op jit(solution)/shard_map/ppermute | solution.py:185
  (56 shorter events, 16.3 us)
Async XLA Ops:
  1.1 18.0 %collective-permute-start = (bf16[64,2048]{1,0:T(8,128)(2,1)S(1)}, bf16[64,2048]{1,0:T(8,128)(2,1)S(1)}, u32[]{:S(2)}, u32[]{:S(2)}) collective-permute-start(bf16[64,2048]{1,0:T(8,128)(2,1)S(1)} %get-tuple-element.76), channel_id=1, source_target_pairs={{0,0},{1,4},{2,8},{3,12},{4,1},{5,5},{6,9},{7,13},{8,2},{9,6},{10,... | collective-permute-start | bytes 786440 | tf_op jit(solution)/shard_map/ppermute | solution.py:131
  19.1 12.9 %collective-permute-start.2 = (bf16[64,2048]{1,0:T(8,128)(2,1)S(1)}, bf16[64,2048]{1,0:T(8,128)(2,1)S(1)}, u32[]{:S(2)}, u32[]{:S(2)}) collective-permute-start(bf16[64,2048]{1,0:T(8,128)(2,1)S(1)} %collective-permute-done.refs_0_), channel_id=1, source_target_pairs={{0,2},{1,3},{2,0},{3,1},{4,6},{5,7},{6,4},{7,5},{8,10},{9,11},{10,... | collective-permute-start | bytes 786440 | tf_op jit(solution)/shard_map/ppermute | solution.py:123
  19.1 22.5 %collective-permute-start.1 = (bf16[64,2048]{1,0:T(8,128)(2,1)S(1)}, bf16[64,2048]{1,0:T(8,128)(2,1)S(1)}, u32[]{:S(2)}, u32[]{:S(2)}) collective-permute-start(bf16[64,2048]{1,0:T(8,128)(2,1)S(1)} %get-tuple-element.41), channel_id=1, source_target_pairs={{0,0},{1,4},{2,8},{3,12},{4,1},{5,5},{6,9},{7,13},{8,2},{9,6},{10,... | collective-permute-start | bytes 786440 | tf_op jit(solution)/shard_map/ppermute | solution.py:131
  32.0 10.6 %collective-permute-start.3 = (bf16[64,2048]{1,0:T(8,128)(2,1)S(1)}, bf16[64,2048]{1,0:T(8,128)(2,1)S(1)}, u32[]{:S(2)}, u32[]{:S(2)}) collective-permute-start(bf16[64,2048]{1,0:T(8,128)(2,1)S(1)} %collective-permute-done.refs_0_), channel_id=1, source_target_pairs={{0,1},{1,0},{2,3},{3,2},{4,5},{5,4},{6,7},{7,6},{8,9},{9,8},{10,11... | collective-permute-start | bytes 786440 | tf_op jit(solution)/shard_map/ppermute | solution.py:123
  35.4 11.8 %collective-permute-start.4 = (bf16[64,2048]{1,0:T(8,128)(2,1)S(1)}, bf16[64,2048]{1,0:T(8,128)(2,1)S(1)}, u32[]{:S(2)}, u32[]{:S(2)}) collective-permute-start(bf16[64,2048]{1,0:T(8,128)(2,1)S(1)} %collective-permute-done.2.refs_2_), channel_id=1, source_target_pairs={{0,1},{1,0},{2,3},{3,2},{4,5},{5,4},{6,7},{7,6},{8,9},{9,8},{10,11... | collective-permute-start | bytes 786440 | tf_op jit(solution)/shard_map/ppermute | solution.py:123
  47.2 21.2 %collective-permute-start.6 = (bf16[64,2048]{1,0:T(8,128)(2,1)S(1)}, bf16[64,2048]{1,0:T(8,128)(2,1)S(1)}, u32[]{:S(2)}, u32[]{:S(2)}) collective-permute-start(bf16[64,2048]{1,0:T(8,128)(2,1)S(1)} %collective-permute-done.1.refs_0_), channel_id=1, source_target_pairs={{0,2},{1,3},{2,0},{3,1},{4,6},{5,7},{6,4},{7,5},{8,10},{9,11},{10,... | collective-permute-start | bytes 786440 | tf_op jit(solution)/shard_map/ppermute | solution.py:123
  51.3 17.1 %collective-permute-start.5 = (bf16[64,2048]{1,0:T(8,128)(2,1)S(1)}, bf16[64,2048]{1,0:T(8,128)(2,1)S(1)}, u32[]{:S(2)}, u32[]{:S(2)}) collective-permute-start(bf16[64,2048]{1,0:T(8,128)(2,1)S(1)} %collective-permute-done.1.refs_0_), channel_id=1, source_target_pairs={{0,1},{1,0},{2,3},{3,2},{4,5},{5,4},{6,7},{7,6},{8,9},{9,8},{10,11... | collective-permute-start | bytes 786440 | tf_op jit(solution)/shard_map/ppermute | solution.py:123
  68.4 2.7 %collective-permute-start.7 = (bf16[2,64,4096]{2,1,0:T(8,128)(2,1)S(1)}, bf16[2,64,4096]{2,1,0:T(8,128)(2,1)S(1)}, u32[]{:S(2)}, u32[]{:S(2)}) collective-permute-start(bf16[2,64,4096]{2,1,0:T(8,128)(2,1)S(1)} %get-tuple-element.48), channel_id=1, source_target_pairs={{0,4},{4,0},{8,12},{12,8},{1,5},{5,1},{9,13},{13,9},{2,6},{6,2},{1... | collective-permute-start | bytes 3145736 | tf_op jit(solution)/shard_map/ppermute | solution.py:123
  68.5 3.6 %copy-start.1 = (s32[32]{0:T(128)S(1)}, s32[32]{0:T(128)}, u32[]{:S(2)}) copy-start(s32[32]{0:T(128)} %param.10) | copy-start | bytes 388
  68.5 27.2 %collective-permute-start.9 = (bf16[2,64,4096]{2,1,0:T(8,128)(2,1)S(1)}, bf16[2,64,4096]{2,1,0:T(8,128)(2,1)S(1)}, u32[]{:S(2)}, u32[]{:S(2)}) collective-permute-start(bf16[2,64,4096]{2,1,0:T(8,128)(2,1)S(1)} %get-tuple-element.54), channel_id=1, source_target_pairs={{0,4},{4,0},{8,12},{12,8},{1,5},{5,1},{9,13},{13,9},{2,6},{6,2},{1... | collective-permute-start | bytes 3145736 | tf_op jit(solution)/shard_map/ppermute | solution.py:123
  71.3 25.3 %collective-permute-start.10 = (bf16[2,64,4096]{2,1,0:T(8,128)(2,1)S(1)}, bf16[2,64,4096]{2,1,0:T(8,128)(2,1)S(1)}, u32[]{:S(2)}, u32[]{:S(2)}) collective-permute-start(bf16[2,64,4096]{2,1,0:T(8,128)(2,1)S(1)} %fusion.1), channel_id=1, source_target_pairs={{0,8},{4,12},{8,0},{12,4},{1,9},{5,13},{9,1},{13,5},{2,10},{6,14},... | collective-permute-start | bytes 3145736 | tf_op jit(solution)/shard_map/ppermute | solution.py:123
  72.1 8.4 %collective-permute-start.8 = (bf16[64,2048]{1,0:T(8,128)(2,1)S(1)}, bf16[64,2048]{1,0:T(8,128)(2,1)S(1)}, u32[]{:S(2)}, u32[]{:S(2)}) collective-permute-start(bf16[64,2048]{1,0:T(8,128)(2,1)S(1)} %collective-permute-done.6.refs_2_), channel_id=1, source_target_pairs={{0,1},{1,0},{2,3},{3,2},{4,5},{5,4},{6,7},{7,6},{8,9},{9,8},{10,11... | collective-permute-start | bytes 786440 | tf_op jit(solution)/shard_map/ppermute | solution.py:123
  95.1 3.4 %copy-start = (f32[2,2,64,4096]{3,2,1,0:T(8,128)}, f32[2,2,64,4096]{3,2,1,0:T(8,128)S(1)}, u32[]{:S(2)}) copy-start(f32[2,2,64,4096]{3,2,1,0:T(8,128)S(1)} %get-tuple-element.59) | copy-start | bytes 12582916
  95.1 3.4 %collective-permute-start.11 = (bf16[2,64,4096]{2,1,0:T(8,128)(2,1)S(1)}, bf16[2,64,4096]{2,1,0:T(8,128)(2,1)S(1)}, u32[]{:S(2)}, u32[]{:S(2)}) collective-permute-start(bf16[2,64,4096]{2,1,0:T(8,128)(2,1)S(1)} %get-tuple-element.52), channel_id=1, source_target_pairs={{0,4},{4,0},{8,12},{12,8},{1,5},{5,1},{9,13},{13,9},{2,6},{6,2},{1... | collective-permute-start | bytes 3145736 | tf_op jit(solution)/shard_map/ppermute | solution.py:123
  95.2 33.1 %collective-permute-start.15 = (bf16[2,64,4096]{2,1,0:T(8,128)(2,1)S(1)}, bf16[2,64,4096]{2,1,0:T(8,128)(2,1)}, u32[]{:S(2)}, u32[]{:S(2)}) collective-permute-start(bf16[2,64,4096]{2,1,0:T(8,128)(2,1)S(1)} %get-tuple-element.51), channel_id=1, source_target_pairs={{0,4},{4,0},{8,12},{12,8},{1,5},{5,1},{9,13},{13,9},{2,6},{6,2},{1... | collective-permute-start | bytes 3145736 | tf_op jit(solution)/shard_map/ppermute | solution.py:123
  97.1 14.9 %collective-permute-start.13 = (bf16[64,4096]{1,0:T(8,128)(2,1)S(1)}, bf16[64,4096]{1,0:T(8,128)(2,1)S(1)}, u32[]{:S(2)}, u32[]{:S(2)}) collective-permute-start(bf16[64,4096]{1,0:T(8,128)(2,1)S(1)} %fusion.10.h0), channel_id=1, source_target_pairs={{0,8},{4,12},{8,0},{12,4},{1,9},{5,13},{9,1},{13,5},{2,10},{6,14},... | collective-permute-start | bytes 1572872 | tf_op jit(solution)/shard_map/ppermute | solution.py:123
  99.7 33.1 %collective-permute-start.16 = (bf16[2,64,4096]{2,1,0:T(8,128)(2,1)}, bf16[2,64,4096]{2,1,0:T(8,128)(2,1)}, u32[]{:S(2)}, u32[]{:S(2)}) collective-permute-start(bf16[2,64,4096]{2,1,0:T(8,128)(2,1)} %fusion.3), channel_id=1, source_target_pairs={{0,8},{4,12},{8,0},{12,4},{1,9},{5,13},{9,1},{13,5},{2,10},{6,14},... | collective-permute-start | bytes 3145736 | tf_op jit(solution)/shard_map/ppermute | solution.py:123
  101.5 10.6 %collective-permute-start.12 = (bf16[64,4096]{1,0:T(8,128)(2,1)S(1)}, bf16[64,4096]{1,0:T(8,128)(2,1)S(1)}, u32[]{:S(2)}, u32[]{:S(2)}) collective-permute-start(bf16[64,4096]{1,0:T(8,128)(2,1)S(1)} %fusion.10.h0), channel_id=1, source_target_pairs={{0,4},{4,0},{8,12},{12,8},{1,5},{5,1},{9,13},{13,9},{2,6},{6,2},{1... | collective-permute-start | bytes 1572872 | tf_op jit(solution)/shard_map/ppermute | solution.py:123
  112.0 1.9 collective-permute-start.14
  123.9 34.0 %all-to-all-start = ((bf16[4,64,2048]{2,1,0:T(8,128)(2,1)}), bf16[4,64,2048]{2,1,0:T(8,128)(2,1)}, u32[]{:S(2)}, u32[]{:S(2)}) async-start(bf16[4,64,2048]{2,1,0:T(8,128)(2,1)} %get-tuple-element.58), calls=%async_computation | async-start | bytes 2097152 | tf_op jit(solution)/shard_map/all_to_all | solution.py:165
  135.5 13.0 %collective-permute-start.18 = (bf16[64,4096]{1,0:T(8,128)(2,1)S(1)}, bf16[64,4096]{1,0:T(8,128)(2,1)S(1)}, u32[]{:S(2)}, u32[]{:S(2)}) collective-permute-start(bf16[64,4096]{1,0:T(8,128)(2,1)S(1)} %fusion.7.h0), channel_id=1, source_target_pairs={{0,8},{4,12},{8,0},{12,4},{1,9},{5,13},{9,1},{13,5},{2,10},{6,14},... | collective-permute-start | bytes 1572872 | tf_op jit(solution)/shard_map/ppermute | solution.py:123
  137.2 11.3 %collective-permute-start.17 = (bf16[64,4096]{1,0:T(8,128)(2,1)S(1)}, bf16[64,4096]{1,0:T(8,128)(2,1)S(1)}, u32[]{:S(2)}, u32[]{:S(2)}) collective-permute-start(bf16[64,4096]{1,0:T(8,128)(2,1)S(1)} %fusion.7.h0), channel_id=1, source_target_pairs={{0,4},{4,0},{8,12},{12,8},{1,5},{5,1},{9,13},{13,9},{2,6},{6,2},{1... | collective-permute-start | bytes 1572872 | tf_op jit(solution)/shard_map/ppermute | solution.py:123
  148.5 1.9 collective-permute-start.19
  155.9 21.9 %collective-permute-start.23 = (bf16[64,1024]{1,0:T(8,128)(2,1)S(1)}, bf16[64,1024]{1,0:T(8,128)(2,1)S(1)}, u32[]{:S(2)}, u32[]{:S(2)}) collective-permute-start(bf16[64,1024]{1,0:T(8,128)(2,1)S(1)} %get-tuple-element.61), channel_id=1, source_target_pairs={{0,1},{1,0},{2,3},{3,2},{4,5},{5,4},{6,7},{7,6},{8,9},{9,8},{10,11... | collective-permute-start | bytes 393224 | tf_op jit(solution)/shard_map/ppermute | solution.py:123
  156.2 11.5 %collective-permute-start.21 = (bf16[64,1024]{1,0:T(8,128)(2,1)S(1)}, bf16[64,1024]{1,0:T(8,128)(2,1)}, u32[]{:S(2)}, u32[]{:S(2)}) collective-permute-start(bf16[64,1024]{1,0:T(8,128)(2,1)S(1)} %get-tuple-element.69), channel_id=1, source_target_pairs={{0,1},{1,0},{2,3},{3,2},{4,5},{5,4},{6,7},{7,6},{8,9},{9,8},{10,11... | collective-permute-start | bytes 393224 | tf_op jit(solution)/shard_map/ppermute | solution.py:123
  159.4 36.7 %collective-permute-start.20 = (bf16[64,2048]{1,0:T(8,128)(2,1)S(1)}, bf16[64,2048]{1,0:T(8,128)(2,1)S(1)}, u32[]{:S(2)}, u32[]{:S(2)}) collective-permute-start(bf16[64,2048]{1,0:T(8,128)(2,1)S(1)} %fusion.11), channel_id=1, source_target_pairs={{0,0},{1,4},{2,8},{3,12},{4,1},{5,5},{6,9},{7,13},{8,2},{9,6},{10,... | collective-permute-start | bytes 786440 | tf_op jit(solution)/shard_map/ppermute | solution.py:185
  167.7 7.7 %collective-permute-start.22 = (bf16[64,1024]{1,0:T(8,128)(2,1)S(1)}, bf16[64,1024]{1,0:T(8,128)(2,1)S(1)}, u32[]{:S(2)}, u32[]{:S(2)}) collective-permute-start(bf16[64,1024]{1,0:T(8,128)(2,1)S(1)} %get-tuple-element.71), channel_id=1, source_target_pairs={{0,1},{1,0},{2,3},{3,2},{4,5},{5,4},{6,7},{7,6},{8,9},{9,8},{10,11... | collective-permute-start | bytes 393224 | tf_op jit(solution)/shard_map/ppermute | solution.py:123
  168.7 10.0 %collective-permute-start.24 = (bf16[64,1024]{1,0:T(8,128)(2,1)S(1)}, bf16[64,1024]{1,0:T(8,128)(2,1)S(1)}, u32[]{:S(2)}, u32[]{:S(2)}) collective-permute-start(bf16[64,1024]{1,0:T(8,128)(2,1)S(1)} %add_convert_fusion.3), channel_id=1, source_target_pairs={{0,2},{1,3},{2,0},{3,1},{4,6},{5,7},{6,4},{7,5},{8,10},{9,11},{10,... | collective-permute-start | bytes 393224 | tf_op jit(solution)/shard_map/ppermute | solution.py:123
  175.3 11.1 %collective-permute-start.26 = (bf16[64,1024]{1,0:T(8,128)(2,1)S(1)}, bf16[64,1024]{1,0:T(8,128)(2,1)S(1)}, u32[]{:S(2)}, u32[]{:S(2)}) collective-permute-start(bf16[64,1024]{1,0:T(8,128)(2,1)S(1)} %get-tuple-element.75), channel_id=1, source_target_pairs={{0,1},{1,0},{2,3},{3,2},{4,5},{5,4},{6,7},{7,6},{8,9},{9,8},{10,11... | collective-permute-start | bytes 393224 | tf_op jit(solution)/shard_map/ppermute | solution.py:123
  175.4 11.1 %collective-permute-start.27 = (bf16[64,1024]{1,0:T(8,128)(2,1)S(1)}, bf16[64,1024]{1,0:T(8,128)(2,1)S(1)}, u32[]{:S(2)}, u32[]{:S(2)}) collective-permute-start(bf16[64,1024]{1,0:T(8,128)(2,1)S(1)} %add_convert_fusion.2), channel_id=1, source_target_pairs={{0,2},{1,3},{2,0},{3,1},{4,6},{5,7},{6,4},{7,5},{8,10},{9,11},{10,... | collective-permute-start | bytes 393224 | tf_op jit(solution)/shard_map/ppermute | solution.py:123
  178.8 17.3 %collective-permute-start.25 = (bf16[64,1024]{1,0:T(8,128)(2,1)S(1)}, bf16[64,1024]{1,0:T(8,128)(2,1)S(1)}, u32[]{:S(2)}, u32[]{:S(2)}) collective-permute-start(bf16[64,1024]{1,0:T(8,128)(2,1)S(1)} %add_convert_fusion.1), channel_id=1, source_target_pairs={{0,0},{1,4},{2,8},{3,12},{4,1},{5,5},{6,9},{7,13},{8,2},{9,6},{10,... | collective-permute-start | bytes 393224 | tf_op jit(solution)/shard_map/ppermute | solution.py:185
  186.5 12.2 %collective-permute-start.28 = (bf16[64,1024]{1,0:T(8,128)(2,1)S(1)}, bf16[64,1024]{1,0:T(8,128)(2,1)S(1)}, u32[]{:S(2)}, u32[]{:S(2)}) collective-permute-start(bf16[64,1024]{1,0:T(8,128)(2,1)S(1)} %add_convert_fusion), channel_id=1, source_target_pairs={{0,0},{1,4},{2,8},{3,12},{4,1},{5,5},{6,9},{7,13},{8,2},{9,6},{10,... | collective-permute-start | bytes 393224 | tf_op jit(solution)/shard_map/ppermute | solution.py:185
